TPU v7x, 32 devices: a whole 2x2x4 slice. The times are simulated.
32 devices in a mesh: row: 8 (over z, x), col: 4 (over y, core).
Axes of the slice: x: 2, y: 2, z: 4, core: 2. Of those that a mesh axis runs over, the one named last changes fastest.
Arguments:
- p2_panel: bfloat16 [4096, 3584], P('row'), may hold values from -6 to 6
- density: bfloat16 [4096, 3584], P('row', 'col'), may hold values from -0.09375 to 0.09375
- pattern: int32 [64, 56], P('row'), may hold values 0 or 1
- x_basis: bfloat16 [4096, 32], P('row'), may hold values from -0.59765625 to 0.59765625
- x_offset: int32 [64], P('row'), may hold values from 0 to 160
- x_extent: int32 [64], P('row'), may hold values from 1 to 32
- y_basis: bfloat16 [8, 3584, 32], P('row', 'col'), may hold values from -0.59765625 to 0.59765625
- y_offset: int32 [8, 56], P('row', 'col'), may hold values from 0 to 160
- y_extent: int32 [8, 56], P('row', 'col'), may hold values from 1 to 32
Outputs:
- new_density: bfloat16 [4096, 3584], P('row', 'col')
- grid_density: float32 [1024, 512], P('row', 'col')
Inputs may be any that keep to these rules, and one draw needn't show every extreme that they name: `pattern`: 1 where a block of the window is stored.
All inputs are finite; a program needn't handle non-finite values.
Results may differ from a plain program's by a relative error of at most 0.0049.
Values may be sent and summed in bfloat16 or wider, within the bound.
No kernel may reach another device: no remote copies, remote signals or barrier semaphores. Data moves between devices by JAX's collectives and lax.ppermute only.
A program may use at most 64 MiB of HBM per device.

v0:
```python
import jax
import jax.numpy as jnp
from jax import lax
from jax.sharding import PartitionSpec as P

HD = 3
SX = 128
SY = 128
M = 32


def passed_along(value, axis, steps):
    count = lax.axis_size(axis)
    pairs = [(source, (source + steps) % count) for source in range(count)]
    return lax.ppermute(value, axis, pairs)


def mask_blocks(values, pattern):
    number, win_slots = pattern.shape
    block_size = values.shape[0] // number
    shaped = values.reshape(number, block_size, win_slots, block_size)
    return (shaped * pattern.astype(values.dtype)[:, None, :, None]).reshape(values.shape)


def place(tile_vals, offset, extent, length):
    number = offset.shape[0]
    breadth = tile_vals.shape[1]
    blocks = tile_vals.reshape(number, -1, breadth)
    cell_ids = jnp.arange(length, dtype=jnp.int32)
    step_ids = jnp.arange(breadth, dtype=jnp.int32)
    onehot = (cell_ids[None, None, :] == offset[:, None, None] + step_ids[None, :, None]) & (
        step_ids[None, :, None] < extent[:, None, None]
    )
    spread = jnp.einsum(
        "iat,ite->iae", blocks, onehot.astype(blocks.dtype), preferred_element_type=jnp.float32
    )
    return spread.reshape(-1, length).astype(jnp.bfloat16)


def shards(p2_panel, density, pattern, x_basis, x_offset, x_extent, y_basis, y_offset, y_extent):
    col_count = lax.axis_size("col")
    column = lax.axis_index("col")
    row_blocks, win_slots = pattern.shape
    block_size = x_basis.shape[0] // row_blocks
    per_class = win_slots // col_count
    stride = row_blocks // col_count
    panel_rows = row_blocks * block_size
    square = mask_blocks(p2_panel, pattern)
    own_pattern = lax.dynamic_index_in_dim(
        pattern.reshape(row_blocks, per_class, col_count), column, 2, keepdims=False
    )
    own_tile = mask_blocks(density, own_pattern)

    def contribute(summed, distance, incoming):
        first = row_blocks * (distance + HD) * block_size
        panel_cols = square[:, first : first + panel_rows]
        product = jnp.dot(panel_cols, incoming, preferred_element_type=jnp.float32)
        padding = per_class * block_size - incoming.shape[1]
        if distance > 0:
            product = jnp.pad(product, ((0, 0), (padding, 0)))
        elif distance < 0:
            product = jnp.pad(product, ((0, 0), (0, padding)))
        return summed + product

    summed = contribute(jnp.zeros((panel_rows, per_class * block_size), jnp.float32), 0, own_tile)
    lower_tile = own_tile
    upper_tile = own_tile
    for distance in range(1, HD + 1):
        kept_cols = (per_class - stride * distance) * block_size
        lower_tile = passed_along(lower_tile[:, :kept_cols], "row", -1)
        upper_tile = passed_along(upper_tile[:, stride * block_size :], "row", 1)
        summed = contribute(summed, distance, lower_tile)
        summed = contribute(summed, -distance, upper_tile)
    own_square = lax.dynamic_index_in_dim(
        square.reshape(panel_rows, per_class, col_count, block_size), column, 2, keepdims=False
    )
    own_square = own_square.reshape(panel_rows, per_class * block_size)
    renewed = mask_blocks(3.0 * own_square.astype(jnp.float32) - 2.0 * summed, own_pattern).astype(
        jnp.bfloat16
    )
    y_spread = place(y_basis[0], y_offset[0], y_extent[0], SY + 2 * M)
    half_done = jnp.dot(renewed, y_spread, preferred_element_type=jnp.float32).astype(jnp.bfloat16)
    x_spread = place(x_basis, x_offset, x_extent, SX + 2 * M)
    extended = lax.dot_general(
        x_spread, half_done, (((0,), (0,)), ((), ())), preferred_element_type=jnp.float32
    )
    interior = extended[M : M + SX]
    for shift_by, rim_cells, position in ((-1, extended[:M], SX - M), (1, extended[SX + M :], 0)):
        received = passed_along(rim_cells, "row", shift_by)
        interior = interior + jnp.pad(received, ((position, SX - M - position), (0, 0)))
    grid_out = interior[:, M : M + SY]
    for shift_by, rim_cells, position in (
        (-1, interior[:, :M], SY - M),
        (1, interior[:, SY + M :], 0),
    ):
        received = passed_along(rim_cells, "col", shift_by)
        grid_out = grid_out + jnp.pad(received, ((0, 0), (position, SY - M - position)))
    return (renewed, grid_out)


def solution(mesh):
    placed = (
        P("row", None),
        P("row", "col"),
        P("row", None),
        P("row", None),
        P("row"),
        P("row"),
        P("row", "col", None),
        P("row", "col"),
        P("row", "col"),
    )
    return jax.shard_map(
        shards,
        mesh=mesh,
        in_specs=placed,
        out_specs=(P("row", "col"), P("row", "col")),
        check_vma=False,
    )
```

profile of v0, /device:TPU:0, one launch (start us, length us, event | category | flops | bytes accessed | tf_op | source)
XLA Modules:
  0.0 125.4 jit_solution(8786586552109112601)
XLA Ops:
  1.5 1.5 %copy.31 = bf16[512,896]{0,1:T(8,128)(2,1)S(1)} copy(bf16[512,896]{1,0:T(8,128)(2,1)} %param.10) | data formatting | bytes 1835008 | tf_op args[1]
  3.4 1.9 %mul.68 = bf16[512,896]{0,1:T(8,128)(2,1)} reshape(bf16[8,64,14,64]{1,0,3,2:T(8,128)(2,1)S(1)} %mul.67) | data formatting | bytes 1835008 | tf_op jit(solution)/shard_map/mul | solution.py:22
  5.3 1.4 %mul.69 = bf16[512,896]{0,1:T(8,128)(2,1)S(1)} multiply(bf16[512,896]{0,1:T(8,128)(2,1)S(1)} %copy.31, bf16[512,896]{0,1:T(8,128)(2,1)} %mul.68) | non-fusion elementwise | flops 458752 | bytes 2752512 | tf_op jit(solution)/shard_map/mul | solution.py:22
  6.8 1.3 %fusion.29 = (bf16[512,768]{0,1:T(8,128)(2,1)}, bf16[512,768]{0,1:T(8,128)(2,1)}) fusion(bf16[512,896]{0,1:T(8,128)(2,1)S(1)} %mul.69), kind=kLoop, calls=%fused_computation.43 | loop fusion | bytes 3145728 | tf_op jit(solution)/shard_map/slice | solution.py:70
  8.0 2.9 %collective-permute-start.1 = (bf16[512,768]{0,1:T(8,128)(2,1)}, bf16[512,768]{0,1:T(8,128)(2,1)S(1)}, u32[]{:S(2)}, u32[]{:S(2)}) collective-permute-start(bf16[512,768]{0,1:T(8,128)(2,1)} %get-tuple-element.3), channel_id=1, source_target_pairs={{0,4},{4,8},{8,12},{12,16},{16,20},{20,24},{24,28},{28,0},{1,5},{5... | collective-permute-start | bytes 2359304 | tf_op jit(solution)/shard_map/ppermute | solution.py:15
  11.0 3.0 %collective-permute-start = (bf16[512,768]{0,1:T(8,128)(2,1)}, bf16[512,768]{0,1:T(8,128)(2,1)}, u32[]{:S(2)}, u32[]{:S(2)}) collective-permute-start(bf16[512,768]{0,1:T(8,128)(2,1)} %get-tuple-element.2), channel_id=1, source_target_pairs={{0,28},{4,0},{8,4},{12,8},{16,12},{20,16},{24,20},{28,24},{1,29},{... | collective-permute-start | bytes 2359304 | tf_op jit(solution)/shard_map/ppermute | solution.py:15
  16.4 6.0 %copy.26 = bf16[512,3584]{0,1:T(8,128)(2,1)} copy(bf16[512,3584]{1,0:T(8,128)(2,1)} %param.9) | data formatting | bytes 7340032 | tf_op args[0]
  23.3 1.2 convolution_convert_fusion
  24.6 1.5 %convert_multiply_fusion = f32[512,14,1,64]{0,3,2,1:T(8,128)S(1)} fusion(bf16[512,14,4,64]{0,3,2,1:T(8,128)(2,1)} %bitcast.42, s32[]{:T(128)S(6)} %select_n.6, bf16[512,14,1]{0,2,1:T(2,128)(2,1)} %constant_dynamic-slice_fusion.1), kind=kLoop, calls=%fused_computation.1 | loop fusion | flops 1376256 | bytes 2766852 | tf_op jit(solution)/shard_map/mul | solution.py:78
  26.1 18.9 %collective-permute-done.1 = bf16[512,768]{0,1:T(8,128)(2,1)S(1)} collective-permute-done((bf16[512,768]{0,1:T(8,128)(2,1)}, bf16[512,768]{0,1:T(8,128)(2,1)S(1)}, u32[]{:S(2)}, u32[]{:S(2)}) %collective-permute-start.1) | collective-permute-done | bytes 786464 | tf_op jit(solution)/shard_map/ppermute | solution.py:15
  45.8 2.4 %collective-permute-start.3 = (bf16[512,640]{0,1:T(8,128)(2,1)}, bf16[512,640]{0,1:T(8,128)(2,1)}, u32[]{:S(2)}, u32[]{:S(2)}) collective-permute-start(bf16[512,640]{0,1:T(8,128)(2,1)} %slice.84), channel_id=1, source_target_pairs={{0,4},{4,8},{8,12},{12,16},{16,20},{20,24},{24,28},{28,0},{1,5},{5... | collective-permute-start | bytes 1966088 | tf_op jit(solution)/shard_map/ppermute | solution.py:15
  48.2 2.0 %slice.82 = bf16[512,640]{0,1:T(8,128)(2,1)} slice(bf16[512,768]{0,1:T(8,128)(2,1)} %collective-permute-done), slice={[0:512], [0:640]} | slice | bytes 1310720 | tf_op jit(solution)/shard_map/slice | solution.py:70
  50.2 3.0 %collective-permute-start.2 = (bf16[512,640]{0,1:T(8,128)(2,1)}, bf16[512,640]{0,1:T(8,128)(2,1)}, u32[]{:S(2)}, u32[]{:S(2)}) collective-permute-start(bf16[512,640]{0,1:T(8,128)(2,1)} %slice.82), channel_id=1, source_target_pairs={{0,28},{4,0},{8,4},{12,8},{16,12},{20,16},{24,20},{28,24},{1,29},{... | collective-permute-start | bytes 1966088 | tf_op jit(solution)/shard_map/ppermute | solution.py:15
  54.4 2.1 %mul.72 = f32[8,64,14,64]{1,0,3,2:T(8,128)} broadcast(f32[8,14]{0,1:T(8,128)S(1)} %copy.33), dimensions={0,2} | broadcast | bytes 1835456 | tf_op jit(solution)/shard_map/mul | solution.py:22
  56.5 4.4 %mul.73 = f32[512,896]{0,1:T(8,128)} reshape(f32[8,64,14,64]{1,0,3,2:T(8,128)} %mul.72) | data formatting | bytes 3670016 | tf_op jit(solution)/shard_map/mul | solution.py:22
  60.9 2.8 %copy.34 = f32[512,896]{1,0:T(8,128)} copy(f32[512,896]{0,1:T(8,128)} %mul.73) | data formatting | bytes 3670016 | tf_op jit(solution)/shard_map/mul | solution.py:22
  63.6 1.7 %copy.32 = f32[512,896]{1,0:T(8,128)} copy(f32[512,896]{0,1:T(8,128)S(1)} %bitcast.41) | data formatting | bytes 3670016 | tf_op jit(solution)/shard_map/mul | solution.py:78
  65.3 3.9 %mul.64 = bf16[8,64,56,64]{3,2,1,0:T(8,128)(2,1)} broadcast(bf16[8,56]{1,0:T(8,128)(2,1)S(1)} %convert_element_type.73), dimensions={0,2} | broadcast | bytes 3670912 | tf_op jit(solution)/shard_map/mul | solution.py:22
  69.3 10.0 %mul.65 = bf16[512,3584]{1,0:T(8,128)(2,1)} reshape(bf16[8,64,56,64]{3,2,1,0:T(8,128)(2,1)} %mul.64) | data formatting | bytes 7340032 | tf_op jit(solution)/shard_map/mul | solution.py:22
  79.2 4.0 %mul.66 = bf16[512,3584]{1,0:T(8,128)(2,1)S(1)} multiply(bf16[512,3584]{1,0:T(8,128)(2,1)} %param.9, bf16[512,3584]{1,0:T(8,128)(2,1)} %mul.65) | non-fusion elementwise | flops 1835008 | bytes 11010048 | tf_op jit(solution)/shard_map/mul | solution.py:22
  83.9 1.7 %fusion.11 = f32[512,768]{1,0:T(8,128)S(1)} fusion(bf16[512,768]{0,1:T(8,128)(2,1)} %collective-permute-done, bf16[512,3584]{1,0:T(8,128)(2,1)S(1)} %mul.66), kind=kOutput, calls=%fused_computation.17 | convolution fusion | flops 402653184 | bytes 2883584 | tf_op jit(solution)/shard_map/dot_general | solution.py:57
  85.6 1.1 slice.88
  87.9 4.8 %collective-permute-start.4 = (bf16[512,512]{0,1:T(8,128)(2,1)S(1)}, bf16[512,512]{0,1:T(8,128)(2,1)S(1)}, u32[]{:S(2)}, u32[]{:S(2)}) collective-permute-start(bf16[512,512]{0,1:T(8,128)(2,1)S(1)} %slice.86), channel_id=1, source_target_pairs={{0,28},{4,0},{8,4},{12,8},{16,12},{20,16},{24,20},{28,24},{1,29},{... | collective-permute-start | bytes 1572872 | tf_op jit(solution)/shard_map/ppermute | solution.py:15
  92.6 1.7 %fusion.5 = f32[512,640]{1,0:T(8,128)S(1)} fusion(bf16[512,640]{0,1:T(8,128)(2,1)} %collective-permute-done.3, bf16[512,3584]{1,0:T(8,128)(2,1)S(1)} %mul.66), kind=kOutput, calls=%fused_computation.11 | convolution fusion | flops 335544320 | bytes 2490368 | tf_op jit(solution)/shard_map/dot_general | solution.py:57
  94.3 1.7 %fusion.7 = f32[512,640]{1,0:T(8,128)S(1)} fusion(bf16[512,640]{0,1:T(8,128)(2,1)} %collective-permute-done.2, bf16[512,3584]{1,0:T(8,128)(2,1)S(1)} %mul.66), kind=kOutput, calls=%fused_computation.13 | convolution fusion | flops 335544320 | bytes 2490368 | tf_op jit(solution)/shard_map/dot_general | solution.py:57
  96.0 12.3 %collective-permute-done.5 = bf16[512,512]{0,1:T(8,128)(2,1)S(1)} collective-permute-done((bf16[512,512]{0,1:T(8,128)(2,1)S(1)}, bf16[512,512]{0,1:T(8,128)(2,1)S(1)}, u32[]{:S(2)}, u32[]{:S(2)}) %collective-permute-start.5) | collective-permute-done | bytes 524320 | tf_op jit(solution)/shard_map/ppermute | solution.py:15
  108.8 2.9 %collective-permute-done.4 = bf16[512,512]{0,1:T(8,128)(2,1)S(1)} collective-permute-done((bf16[512,512]{0,1:T(8,128)(2,1)S(1)}, bf16[512,512]{0,1:T(8,128)(2,1)S(1)}, u32[]{:S(2)}, u32[]{:S(2)}) %collective-permute-start.4) | collective-permute-done | bytes 524320 | tf_op jit(solution)/shard_map/ppermute | solution.py:15
  112.2 1.2 multiply_convert_fusion
  114.2 4.7 %collective-permute-start.6 = (f32[32,192]{1,0:T(8,128)S(1)}, f32[32,192]{1,0:T(8,128)S(1)}, u32[]{:S(2)}, u32[]{:S(2)}) collective-permute-start(f32[32,192]{1,0:T(8,128)S(1)} %get-tuple-element.4), channel_id=1, source_target_pairs={{0,28},{4,0},{8,4},{12,8},{16,12},{20,16},{24,20},{28,24},{1,29},{... | collective-permute-start | bytes 73736 | tf_op jit(solution)/shard_map/ppermute | solution.py:15
  118.9 1.9 %collective-permute-done.7 = f32[32,192]{1,0:T(8,128)S(1)} collective-permute-done((f32[32,192]{1,0:T(8,128)S(1)}, f32[32,192]{1,0:T(8,128)S(1)}, u32[]{:S(2)}, u32[]{:S(2)}) %collective-permute-start.7) | collective-permute-done | bytes 24608 | tf_op jit(solution)/shard_map/ppermute | solution.py:15
  120.9 1.7 %collective-permute-start.8 = (f32[128,32]{1,0:T(8,128)S(1)}, f32[128,32]{1,0:T(8,128)S(1)}, u32[]{:S(2)}, u32[]{:S(2)}) collective-permute-start(f32[128,32]{1,0:T(8,128)S(1)} %get-tuple-element.6), channel_id=1, source_target_pairs={{0,3},{1,0},{2,1},{3,2},{4,7},{5,4},{6,5},{7,6},{8,11},{9,8},{10,9... | collective-permute-start | bytes 49160 | tf_op jit(solution)/shard_map/ppermute | solution.py:15
  122.7 1.9 %collective-permute-done.9 = f32[128,32]{1,0:T(8,128)S(1)} collective-permute-done((f32[128,32]{1,0:T(8,128)S(1)}, f32[128,32]{1,0:T(8,128)S(1)}, u32[]{:S(2)}, u32[]{:S(2)}) %collective-permute-start.9) | collective-permute-done | bytes 16416 | tf_op jit(solution)/shard_map/ppermute | solution.py:15
  (67 shorter events, 11.0 us)
Async XLA Ops:
  6.7 7.3 %copy-start.8 = (s32[8,56]{1,0:T(8,128)S(1)}, s32[8,56]{1,0:T(8,128)}, u32[]{:S(2)}) copy-start(s32[8,56]{1,0:T(8,128)} %param.11) | copy-start | bytes 5380
  6.7 7.6 %copy-start.10 = (s32[8]{0:T(128)S(1)}, s32[8]{0:T(128)}, u32[]{:S(2)}) copy-start(s32[8]{0:T(128)} %param.13) | copy-start | bytes 100
  6.7 8.3 %copy-start.13 = (s32[8]{0:T(128)S(1)}, s32[8]{0:T(128)}, u32[]{:S(2)}) copy-start(s32[8]{0:T(128)} %param.14) | copy-start | bytes 100
  6.7 8.9 %copy-start.11 = (s32[1,14]{1,0:T(1,128)S(1)}, s32[1,14]{1,0:T(1,128)}, u32[]{:S(2)}) copy-start(s32[1,14]{1,0:T(1,128)} %param.17) | copy-start | bytes 172
  8.0 36.9 %collective-permute-start.1 = (bf16[512,768]{0,1:T(8,128)(2,1)}, bf16[512,768]{0,1:T(8,128)(2,1)S(1)}, u32[]{:S(2)}, u32[]{:S(2)}) collective-permute-start(bf16[512,768]{0,1:T(8,128)(2,1)} %get-tuple-element.3), channel_id=1, source_target_pairs={{0,4},{4,8},{8,12},{12,16},{16,20},{20,24},{24,28},{28,0},{1,5},{5... | collective-permute-start | bytes 2359304 | tf_op jit(solution)/shard_map/ppermute | solution.py:15
  11.0 37.2 %collective-permute-start = (bf16[512,768]{0,1:T(8,128)(2,1)}, bf16[512,768]{0,1:T(8,128)(2,1)}, u32[]{:S(2)}, u32[]{:S(2)}) collective-permute-start(bf16[512,768]{0,1:T(8,128)(2,1)} %get-tuple-element.2), channel_id=1, source_target_pairs={{0,28},{4,0},{8,4},{12,8},{16,12},{20,16},{24,20},{28,24},{1,29},{... | collective-permute-start | bytes 2359304 | tf_op jit(solution)/shard_map/ppermute | solution.py:15
  16.4 6.0 %copy-start.7 = (bf16[512,32]{0,1:T(8,128)(2,1)S(1)}, bf16[512,32]{0,1:T(8,128)(2,1)}, u32[]{:S(2)}) copy-start(bf16[512,32]{0,1:T(8,128)(2,1)} %param.12) | copy-start | bytes 98308
  16.4 6.7 %copy-start.6 = (bf16[1,896,32]{1,2,0:T(8,128)(2,1)S(1)}, bf16[1,896,32]{1,2,0:T(8,128)(2,1)}, u32[]{:S(2)}) copy-start(bf16[1,896,32]{1,2,0:T(8,128)(2,1)} %param.15) | copy-start | bytes 172036
  16.4 6.9 %copy-start.12 = (s32[1,14]{1,0:T(1,128)S(1)}, s32[1,14]{1,0:T(1,128)}, u32[]{:S(2)}) copy-start(s32[1,14]{1,0:T(1,128)} %param.16) | copy-start | bytes 172
  26.0 27.2 %copy-start.5 = (bf16[8,64,32]{1,0,2:T(8,128)(2,1)S(1)}, bf16[8,64,32]{1,0,2:T(8,128)(2,1)}, u32[]{:S(2)}) copy-start(bf16[8,64,32]{1,0,2:T(8,128)(2,1)} %reshape.153) | copy-start | bytes 98308
  26.0 27.2 %copy-start.9 = (s32[8,32]{1,0:T(8,128)S(1)}, s32[8,32]{1,0:T(8,128)}, u32[]{:S(2)}) copy-start(s32[8,32]{1,0:T(8,128)} %iota_add_fusion.1) | copy-start | bytes 3076
  26.1 27.2 %copy-start.14 = (pred[8,32]{1,0:T(8,128)(4,1)S(1)}, pred[8,32]{1,0:T(8,128)(4,1)}, u32[]{:S(2)}) copy-start(pred[8,32]{1,0:T(8,128)(4,1)} %iota_compare_fusion.3) | copy-start | bytes 772
  45.8 39.8 %collective-permute-start.3 = (bf16[512,640]{0,1:T(8,128)(2,1)}, bf16[512,640]{0,1:T(8,128)(2,1)}, u32[]{:S(2)}, u32[]{:S(2)}) collective-permute-start(bf16[512,640]{0,1:T(8,128)(2,1)} %slice.84), channel_id=1, source_target_pairs={{0,4},{4,8},{8,12},{12,16},{16,20},{20,24},{24,28},{28,0},{1,5},{5... | collective-permute-start | bytes 1966088 | tf_op jit(solution)/shard_map/ppermute | solution.py:15
  50.2 36.6 %collective-permute-start.2 = (bf16[512,640]{0,1:T(8,128)(2,1)}, bf16[512,640]{0,1:T(8,128)(2,1)}, u32[]{:S(2)}, u32[]{:S(2)}) collective-permute-start(bf16[512,640]{0,1:T(8,128)(2,1)} %slice.82), channel_id=1, source_target_pairs={{0,28},{4,0},{8,4},{12,8},{16,12},{20,16},{24,20},{28,24},{1,29},{... | collective-permute-start | bytes 1966088 | tf_op jit(solution)/shard_map/ppermute | solution.py:15
  86.7 21.6 %collective-permute-start.5 = (bf16[512,512]{0,1:T(8,128)(2,1)S(1)}, bf16[512,512]{0,1:T(8,128)(2,1)S(1)}, u32[]{:S(2)}, u32[]{:S(2)}) collective-permute-start(bf16[512,512]{0,1:T(8,128)(2,1)S(1)} %slice.88), channel_id=1, source_target_pairs={{0,4},{4,8},{8,12},{12,16},{16,20},{20,24},{24,28},{28,0},{1,5},{5... | collective-permute-start | bytes 1572872 | tf_op jit(solution)/shard_map/ppermute | solution.py:15
  87.9 23.8 %collective-permute-start.4 = (bf16[512,512]{0,1:T(8,128)(2,1)S(1)}, bf16[512,512]{0,1:T(8,128)(2,1)S(1)}, u32[]{:S(2)}, u32[]{:S(2)}) collective-permute-start(bf16[512,512]{0,1:T(8,128)(2,1)S(1)} %slice.86), channel_id=1, source_target_pairs={{0,28},{4,0},{8,4},{12,8},{16,12},{20,16},{24,20},{28,24},{1,29},{... | collective-permute-start | bytes 1572872 | tf_op jit(solution)/shard_map/ppermute | solution.py:15
  96.0 16.1 %copy-start = (f32[512,896]{1,0:T(8,128)S(1)}, f32[512,896]{1,0:T(8,128)}, u32[]{:S(2)}) copy-start(f32[512,896]{1,0:T(8,128)} %copy.34) | copy-start | bytes 5505028
  96.0 16.1 %copy-start.1 = (f32[512,896]{1,0:T(8,128)S(1)}, f32[512,896]{1,0:T(8,128)}, u32[]{:S(2)}) copy-start(f32[512,896]{1,0:T(8,128)} %copy.32) | copy-start | bytes 5505028
  112.2 1.3 %copy-start.3 = (bf16[14,192,64]{1,2,0:T(8,128)(2,1)S(1)}, bf16[14,192,64]{1,2,0:T(8,128)(2,1)}, u32[]{:S(2)}) copy-start(bf16[14,192,64]{1,2,0:T(8,128)(2,1)} %convolution_convert_fusion) | copy-start | bytes 1032196
  112.2 1.3 %copy-start.4 = (bf16[8,192,64]{1,2,0:T(8,128)(2,1)S(1)}, bf16[8,192,64]{1,2,0:T(8,128)(2,1)}, u32[]{:S(2)}) copy-start(bf16[8,192,64]{1,2,0:T(8,128)(2,1)} %convolution_convert_fusion.1) | copy-start | bytes 589828
  113.4 12.0 %copy-start.2 = (bf16[512,896]{1,0:T(8,128)(2,1)}, bf16[512,896]{1,0:T(8,128)(2,1)S(1)}, u32[]{:S(2)}) copy-start(bf16[512,896]{1,0:T(8,128)(2,1)S(1)} %multiply_convert_fusion) | copy-start | bytes 2752516
  114.1 6.7 %collective-permute-start.7 = (f32[32,192]{1,0:T(8,128)S(1)}, f32[32,192]{1,0:T(8,128)S(1)}, u32[]{:S(2)}, u32[]{:S(2)}) collective-permute-start(f32[32,192]{1,0:T(8,128)S(1)} %get-tuple-element.5), channel_id=1, source_target_pairs={{0,4},{4,8},{8,12},{12,16},{16,20},{20,24},{24,28},{28,0},{1,5},{5... | collective-permute-start | bytes 73736 | tf_op jit(solution)/shard_map/ppermute | solution.py:15
  114.2 6.6 %collective-permute-start.6 = (f32[32,192]{1,0:T(8,128)S(1)}, f32[32,192]{1,0:T(8,128)S(1)}, u32[]{:S(2)}, u32[]{:S(2)}) collective-permute-start(f32[32,192]{1,0:T(8,128)S(1)} %get-tuple-element.4), channel_id=1, source_target_pairs={{0,28},{4,0},{8,4},{12,8},{16,12},{20,16},{24,20},{28,24},{1,29},{... | collective-permute-start | bytes 73736 | tf_op jit(solution)/shard_map/ppermute | solution.py:15
  120.9 3.7 %collective-permute-start.9 = (f32[128,32]{1,0:T(8,128)S(1)}, f32[128,32]{1,0:T(8,128)S(1)}, u32[]{:S(2)}, u32[]{:S(2)}) collective-permute-start(f32[128,32]{1,0:T(8,128)S(1)} %get-tuple-element.7), channel_id=1, source_target_pairs={{0,1},{1,2},{2,3},{3,0},{4,5},{5,6},{6,7},{7,4},{8,9},{9,10},{10,1... | collective-permute-start | bytes 49160 | tf_op jit(solution)/shard_map/ppermute | solution.py:15
  120.9 3.7 %collective-permute-start.8 = (f32[128,32]{1,0:T(8,128)S(1)}, f32[128,32]{1,0:T(8,128)S(1)}, u32[]{:S(2)}, u32[]{:S(2)}) collective-permute-start(f32[128,32]{1,0:T(8,128)S(1)} %get-tuple-element.6), channel_id=1, source_target_pairs={{0,3},{1,0},{2,1},{3,2},{4,7},{5,4},{6,5},{7,6},{8,11},{9,8},{10,9... | collective-permute-start | bytes 49160 | tf_op jit(solution)/shard_map/ppermute | solution.py:15
where the time goes:
time: 127 us; the launch traced here: 125 us
  local copies, waits for them, and re-layouts  43.8 us (34%)
  waiting for transfers between devices  37.9 us (30%)
  starting transfers between devices  22.7 us (18%)
  matrix products  10.9 us (9%)
  other arithmetic  9.11 us (7%)
    ppermute x10, waiting for transfers between devices, passed_along(): return lax.ppermute(value, axis, pairs)  37.9 us
    mul x9, local copies, waits for them, and re-layouts, mask_blocks(): shaped * pattern.astype(values.dtype)[:, None, :, None]  25.6 us
    ppermute x10, starting transfers between devices, passed_along(): return lax.ppermute(value, axis, pairs)  22.7 us
    unnamed x34, local copies, waits for them, and re-layouts  8.34 us
    dot_general x7, matrix products, contribute(): product = jnp.dot(panel_cols, incoming, preferred_element_type=jnp.float32)  7.85 us
    mul x2, other arithmetic, mask_blocks(): shaped * pattern.astype(values.dtype)[:, None, :, None]  5.46 us
    slice x3, local copies, waits for them, and re-layouts, shards(): lower_tile = passed_along(lower_tile[:, :kept_cols], 'row', -1)  4.31 us
  transfers between devices with their start and end apart: 10, of which 5 were waited for; matrix products, arithmetic and copies ran while one was open for 42% of the time, Pallas kernels for 0%

commit v1 on v0

v1 whole, which is shorter than its diff:
```python
import functools

import jax
import jax.numpy as jnp
from jax import lax
from jax.experimental import pallas as pl
from jax.experimental.pallas import tpu as pltpu
from jax.sharding import PartitionSpec as P

HD = 3
SX = 128
SY = 128
M = 32
EX = SX + 2 * M
EY = SY + 2 * M
CHUNKS = 2 * HD + 1
VMEM = pl.BlockSpec(memory_space=pltpu.VMEM)
SMEM = pl.BlockSpec(memory_space=pltpu.SMEM)
LIMIT = pltpu.CompilerParams(vmem_limit_bytes=40 * 1024 * 1024)
F32 = jnp.float32
BF16 = jnp.bfloat16


class Dims:
    def __init__(self, pattern, x_basis, n_col):
        self.br, self.win = pattern.shape
        self.bs = x_basis.shape[0] // self.br
        self.n_col = n_col
        self.wc = self.win // n_col
        self.stride = self.br // n_col
        self.uw = self.stride * self.bs
        self.rows = self.br * self.bs


def block_mask(pattern_ref, block_row, slots, bs, dtype):
    lane = lax.broadcasted_iota(jnp.int32, (1, bs * len(slots)), 1)
    row = jnp.zeros((1, bs * len(slots)), jnp.int32)
    for place, slot in enumerate(slots):
        inside = (lane >= place * bs) & (lane < (place + 1) * bs)
        row = jnp.where(inside, pattern_ref[block_row, slot], row)
    return row.astype(F32).astype(dtype)


def own_slots(dims, chunk, column):
    return [dims.n_col * (chunk * dims.stride + s) + column for s in range(dims.stride)]


def mask_kernel(dims, pattern_ref, density_ref, x1a_ref, x1b_ref, z1_ref):
    odd = lax.axis_index("row") % 2
    column = lax.axis_index("col")
    bs, uw = dims.bs, dims.uw
    near = x1a_ref.shape[0]
    for chunk in range(CHUNKS):
        for i in range(dims.br):
            rows = slice(i * bs, (i + 1) * bs)
            mask = block_mask(pattern_ref, i, own_slots(dims, chunk, column), bs, BF16)
            kept = density_ref[rows, chunk * uw : (chunk + 1) * uw] * mask
            for lane_odd in (0, 1):
                own = chunk if lane_odd else CHUNKS - 1 - chunk
                sent = CHUNKS - 1 - own

                @pl.when(odd == lane_odd)
                def _():
                    if sent < near:
                        x1a_ref[sent, rows, :] = kept
                    else:
                        x1b_ref[sent - near, rows, :] = kept
                    if own < near:
                        z1_ref[own, rows, :] = kept


def own_block_cols(dims, p2_ref, slot, column):
    pair = pl.multiple_of((dims.n_col * slot // 2 + column // 2) * 2 * dims.bs, 2 * dims.bs)
    wide = p2_ref[:, pl.ds(pair, 2 * dims.bs)].astype(F32)
    return jnp.where(column % 2 == 1, wide[:, dims.bs :], wide[:, : dims.bs])


def spread_kernel(
    dims,
    pattern_ref,
    x_offset_ref,
    x_extent_ref,
    y_offset_ref,
    y_extent_ref,
    p2_ref,
    x_basis_ref,
    y_basis_ref,
    squares_ref,
    summed_ref,
    xt_ref,
    y_ref,
):
    odd = lax.axis_index("row") % 2
    column = lax.axis_index("col")
    bs, uw, br = dims.bs, dims.uw, dims.br
    width = br * bs
    for block in range(CHUNKS):
        for i in range(br):
            rows = slice(i * bs, (i + 1) * bs)
            slots = [block * br + t for t in range(br)]
            mask = block_mask(pattern_ref, i, slots, bs, BF16)
            place = jnp.where(odd == 1, block, CHUNKS - 1 - block)
            squares_ref[place, rows, :] = p2_ref[rows, block * width : (block + 1) * width] * mask
    for chunk in range(CHUNKS):
        place = jnp.where(odd == 1, chunk, CHUNKS - 1 - chunk)
        parts = [
            own_block_cols(dims, p2_ref, chunk * dims.stride + s, column)
            for s in range(dims.stride)
        ]
        own = parts[0] if len(parts) == 1 else jnp.concatenate(parts, axis=1)
        summed_ref[place] = 1.5 * own
        for s in range(dims.stride):
            m = chunk * dims.stride + s
            tx = y_basis_ref.shape[1]
            step = lax.broadcasted_iota(jnp.int32, (tx, EY), 0)
            cell = lax.broadcasted_iota(jnp.int32, (tx, EY), 1)
            hit = (cell == y_offset_ref[0, m] + step) & (step < y_extent_ref[0, m])
            spread = jnp.dot(
                y_basis_ref[m * bs : (m + 1) * bs, :],
                hit.astype(F32).astype(BF16),
                preferred_element_type=F32,
            )
            y_ref[place, s * bs : (s + 1) * bs, :] = spread.astype(BF16)
    tx = x_basis_ref.shape[1]
    for i in range(br):
        step = lax.broadcasted_iota(jnp.int32, (EX, tx), 1)
        cell = lax.broadcasted_iota(jnp.int32, (EX, tx), 0)
        hit = (cell == x_offset_ref[i] + step) & (step < x_extent_ref[i])
        spread = lax.dot_general(
            hit.astype(F32).astype(BF16),
            x_basis_ref[i * bs : (i + 1) * bs, :],
            (((1,), (1,)), ((), ())),
            preferred_element_type=F32,
        )
        xt_ref[:, i * bs : (i + 1) * bs] = spread.astype(BF16)


def paired(terms):
    return [terms[at : at + 2] for at in range(0, len(terms), 2)]


def add_products(square, terms, summed_ref):
    for group in paired(terms):
        tiles = [tile[...] for _, tile in group]
        wide = tiles[0] if len(tiles) == 1 else jnp.concatenate(tiles, axis=1)
        product = jnp.dot(square, wide, preferred_element_type=F32)
        uw = tiles[0].shape[1]
        for at, (place, _) in enumerate(group):
            summed_ref[place] -= product[:, at * uw : (at + 1) * uw]


def first_kernel(squares_ref, before_ref, x1a_ref, x1b_ref, summed_ref):
    summed_ref[...] = before_ref[...]
    near = x1a_ref.shape[0]
    own = lambda j: x1a_ref.at[j] if j < near else x1b_ref.at[j - near]
    add_products(
        squares_ref[HD], [(k, own(CHUNKS - 1 - k)) for k in range(CHUNKS)], summed_ref
    )


def second_kernel(squares_ref, before_ref, x1a_ref, x1b_ref, z1_ref, summed_ref):
    summed_ref[...] = before_ref[...]
    near = x1a_ref.shape[0]
    partner = lambda j: x1a_ref.at[j] if j < near else x1b_ref.at[j - near]
    add_products(
        squares_ref[HD - 1], [(j - 1, partner(j)) for j in range(1, CHUNKS)], summed_ref
    )
    add_products(squares_ref[HD + 2], [(j + 2, z1_ref.at[j]) for j in range(5)], summed_ref)


def third_kernel(squares_ref, before_ref, z2a_ref, z2b_ref, x3_ref, summed_ref):
    summed_ref[...] = before_ref[...]
    next_tile = lambda j: z2a_ref.at[j] if j < 5 else z2b_ref.at[j - 5]
    add_products(
        squares_ref[HD + 1], [(j + 1, next_tile(j)) for j in range(6)], summed_ref
    )
    add_products(squares_ref[HD - 3], [(3 - j, x3_ref.at[j]) for j in range(4)], summed_ref)


def last_kernel(
    dims,
    pattern_ref,
    squares_ref,
    before_ref,
    x2_ref,
    z3_ref,
    xt_ref,
    y_ref,
    new_ref,
    middle_ref,
    rim_a_ref,
    rim_b_ref,
    summed_ref,
):
    odd = lax.axis_index("row") % 2
    column = lax.axis_index("col")
    bs, uw = dims.bs, dims.uw
    summed_ref[...] = before_ref[...]
    add_products(squares_ref[HD - 2], [(4 - j, x2_ref.at[j]) for j in range(5)], summed_ref)
    add_products(squares_ref[HD + 3], [(j + 3, z3_ref.at[j]) for j in range(4)], summed_ref)
    half = jnp.zeros((dims.rows, EY), F32)
    for k in range(CHUNKS):
        chunk = jnp.where(odd == 1, k, CHUNKS - 1 - k)
        pieces = []
        for i in range(dims.br):
            mask = block_mask(pattern_ref, i, own_slots(dims, chunk, column), bs, F32)
            pieces.append(summed_ref[k, i * bs : (i + 1) * bs, :] * (2.0 * mask))
        renewed = jnp.concatenate(pieces, axis=0).astype(BF16)
        for lane_odd in (0, 1):
            at = k if lane_odd else CHUNKS - 1 - k

            @pl.when(odd == lane_odd)
            def _():
                new_ref[:, at * uw : (at + 1) * uw] = renewed

        half = half + jnp.dot(renewed, y_ref[k], preferred_element_type=F32)
    extended = jnp.dot(xt_ref[...], half.astype(BF16), preferred_element_type=F32)
    middle_ref[...] = extended[M : M + SX]
    lower, upper = extended[:M], extended[SX + M :]
    rim_a_ref[...] = jnp.where(odd == 1, lower, upper)
    rim_b_ref[...] = jnp.where(odd == 1, upper, lower)


def row_rims_kernel(middle_ref, got_a_ref, got_b_ref, center_ref, rim_a_ref, rim_b_ref):
    odd = lax.axis_index("row") % 2
    col_odd = lax.axis_index("col") % 2
    got_a, got_b = got_a_ref[...], got_b_ref[...]
    low = jnp.where(odd == 1, got_a, got_b)
    high = jnp.where(odd == 1, got_b, got_a)
    interior = jnp.concatenate(
        [middle_ref[:M] + low, middle_ref[M : SX - M], middle_ref[SX - M :] + high], axis=0
    )
    center_ref[...] = interior[:, M : M + SY]
    lower, upper = interior[:, :M], interior[:, SY + M :]
    rim_a_ref[...] = jnp.where(col_odd == 1, lower, upper)
    rim_b_ref[...] = jnp.where(col_odd == 1, upper, lower)


def col_rims_kernel(center_ref, got_a_ref, got_b_ref, grid_ref):
    col_odd = lax.axis_index("col") % 2
    got_a, got_b = got_a_ref[...], got_b_ref[...]
    low = jnp.where(col_odd == 1, got_a, got_b)
    high = jnp.where(col_odd == 1, got_b, got_a)
    none = jnp.zeros((SX, SY - 2 * M), F32)
    grid_ref[...] = center_ref[...] + jnp.concatenate([low, none, high], axis=1)


def swap_partner(value, axis):
    count = lax.axis_size(axis)
    return lax.ppermute(value, axis, [(s, s ^ 1) for s in range(count)])


def swap_other(value, axis):
    count = lax.axis_size(axis)
    pairs = [(s, (s - 1) % count if s % 2 == 0 else (s + 1) % count) for s in range(count)]
    return lax.ppermute(value, axis, pairs)


def shift_level(value):
    count = lax.axis_size("row")
    pairs = [(s, (s + 2) % count if s % 2 == 0 else (s - 2) % count) for s in range(count)]
    return lax.ppermute(value, "row", pairs)


def after(value, *others):
    return lax.optimization_barrier((value,) + others)[0]


def call(kernel, outs, ins, scratch=(), flops=0):
    shapes = [jax.ShapeDtypeStruct(shape, dtype) for shape, dtype in outs]
    specs = [
        SMEM if jnp.issubdtype(value.dtype, jnp.integer) else VMEM for value in ins
    ]
    moved = sum(value.size * value.dtype.itemsize for value in list(ins) + shapes)
    return pl.pallas_call(
        kernel,
        out_shape=shapes,
        in_specs=specs,
        out_specs=[VMEM] * len(shapes),
        scratch_shapes=list(scratch),
        compiler_params=LIMIT,
        cost_estimate=pl.CostEstimate(flops=flops, bytes_accessed=moved, transcendentals=0),
    )(*ins)


def shards(p2_panel, density, pattern, x_basis, x_offset, x_extent, y_basis, y_offset, y_extent):
    dims = Dims(pattern, x_basis, lax.axis_size("col"))
    rows, uw = dims.rows, dims.uw
    per_chunk = 2 * rows * rows * uw
    chunks = lambda count: ((count, rows, uw), BF16)
    total = ((CHUNKS, rows, uw), F32)

    own_a, own_b, own_z = call(
        functools.partial(mask_kernel, dims), [chunks(5), chunks(2), chunks(5)], [pattern, density]
    )
    x1a = swap_partner(own_a, "row")
    z1 = shift_level(own_z)
    squares, summed, xt, y_spread = call(
        functools.partial(spread_kernel, dims),
        [((CHUNKS, rows, rows), BF16), total, ((EX, rows), BF16), ((CHUNKS, uw, EY), BF16)],
        [pattern, x_offset, x_extent, y_offset, y_extent, p2_panel, x_basis, y_basis[0]],
    )
    (summed,) = call(first_kernel, [total], [squares, summed, own_a, own_b], flops=7 * per_chunk)
    x1b = swap_partner(after(own_b, x1a), "row")
    z2a = shift_level(after(x1a, z1))
    x3 = swap_partner(after(z1[:4], x1b), "row")
    z2b = shift_level(after(x1b[:1], z1))
    (summed,) = call(
        second_kernel, [total], [squares, summed, x1a, x1b, z1], flops=11 * per_chunk
    )
    z3 = shift_level(after(z2a[:4], z2b))
    x2 = swap_partner(after(z2a, x3), "row")
    (summed,) = call(
        third_kernel, [total], [squares, summed, z2a, z2b, x3], flops=10 * per_chunk
    )
    new_density, middle, rim_a, rim_b = call(
        functools.partial(last_kernel, dims),
        [
            ((rows, dims.wc * dims.bs), BF16),
            ((SX, EY), F32),
            ((M, EY), F32),
            ((M, EY), F32),
        ],
        [pattern, squares, summed, x2, z3, xt, y_spread],
        scratch=[pltpu.VMEM((CHUNKS, rows, uw), F32)],
        flops=9 * per_chunk,
    )
    got_a = swap_partner(rim_a, "row")
    got_b = swap_other(rim_b, "row")
    center, rim_a, rim_b = call(
        row_rims_kernel,
        [((SX, SY), F32), ((SX, M), F32), ((SX, M), F32)],
        [middle, got_a, got_b],
    )
    got_a = swap_partner(rim_a, "col")
    got_b = swap_other(rim_b, "col")
    (grid_density,) = call(col_rims_kernel, [((SX, SY), F32)], [center, got_a, got_b])
    return new_density, grid_density


def solution(mesh):
    placed = (
        P("row", None),
        P("row", "col"),
        P("row", None),
        P("row", None),
        P("row"),
        P("row"),
        P("row", "col", None),
        P("row", "col"),
        P("row", "col"),
    )
    return jax.shard_map(
        shards,
        mesh=mesh,
        in_specs=placed,
        out_specs=(P("row", "col"), P("row", "col")),
        check_vma=False,
    )
```

time: 127 us -> 76.6 us (0.60)
  local copies, waits for them, and re-layouts: 43.8 us -> 9.96 us
  Pallas kernels: 0 us -> 11.2 us
  matrix products: 10.9 us -> 0 us
  other arithmetic: 9.11 us -> 0 us
  starting transfers between devices: 22.7 us -> 15 us
  waiting for transfers between devices: 37.9 us -> 39.2 us
    mul x10 -> x0, local copies, waits for them, and re-layouts: 27.3 us -> none  [the longest x9 25.6 us: mask_blocks(): shaped * pattern.astype(values.dtype)[:, None, :, None]]
    pallas_call x0 -> x8, Pallas kernels: none -> 11.2 us  [call(): pl.pallas_call(kernel, out_shape=shapes, in_specs=specs, out_specs=[VMEM]...]
    dot_general x10 -> x0, matrix products: 10.9 us -> none  [the longest x7 7.85 us: contribute(): product = jnp.dot(panel_cols, incoming, preferred_element_type=jnp.float32)]
    ppermute x10 -> x12, starting transfers between devices: 22.7 us -> 15 us  [the longest x6 7.35 us: swap_partner(): return lax.ppermute(value, axis, [(s, s ^ 1) for s in range(count)])]
    mul x3 -> x0, other arithmetic: 6.92 us -> none  [the longest x2 5.46 us: mask_blocks(): shaped * pattern.astype(values.dtype)[:, None, :, None]]
    slice x7 -> x3, local copies, waits for them, and re-layouts: 6.37 us -> 0.89 us  [the longest x1 0.84 us: shards(): z3 = shift_level(after(z2a[:4], z2b))]
    add x4 -> x0, other arithmetic: 1.48 us -> none  [the longest x1 0.73 us: shards(): grid_out + jnp.pad(received, ((0, 0), (position, SY - M - position)))]
    ppermute x10 -> x12, waiting for transfers between devices: 37.9 us -> 39.2 us  [the longest x6 17.9 us: swap_partner(): return lax.ppermute(value, axis, [(s, s ^ 1) for s in range(count)])]
  transfers between devices with their start and end apart: 10 -> 12, of which waited for: 5 -> 8; matrix products, arithmetic and copies ran while one was open for 42% -> 4% of each run, Pallas kernels for 0% -> 6%
where the time goes in v1:
time: 76.6 us; the launch traced here: 76.1 us
  waiting for transfers between devices  39.2 us (51%)
  starting transfers between devices  15 us (20%)
  Pallas kernels  11.2 us (15%)
  local copies, waits for them, and re-layouts  9.96 us (13%)
  between operations  0.8 us (1%)
    ppermute x6, waiting for transfers between devices, swap_partner(): return lax.ppermute(value, axis, [(s, s ^ 1) for s in range(count)])  17.9 us
    ppermute x4, waiting for transfers between devices, shift_level(): return lax.ppermute(value, 'row', pairs)  15.4 us
    pallas_call x8, Pallas kernels, call(): pl.pallas_call(kernel, out_shape=shapes, in_specs=specs, out_specs=[VMEM]...  11.2 us
    unnamed x36, local copies, waits for them, and re-layouts  9.07 us
    ppermute x6, starting transfers between devices, swap_partner(): return lax.ppermute(value, axis, [(s, s ^ 1) for s in range(count)])  7.35 us
    ppermute x2, waiting for transfers between devices, swap_other(): return lax.ppermute(value, axis, pairs)  5.95 us
    ppermute x2, starting transfers between devices, swap_other(): return lax.ppermute(value, axis, pairs)  3.96 us
    ppermute x4, starting transfers between devices, shift_level(): return lax.ppermute(value, 'row', pairs)  3.69 us
  transfers between devices with their start and end apart: 12, of which 8 were waited for; matrix products, arithmetic and copies ran while one was open for 4% of the time, Pallas kernels for 6%

profile of v1, /device:TPU:0, one launch (start us, length us, event | category | flops | bytes accessed | tf_op | source)
XLA Modules:
  0.0 76.1 jit_solution(15103785430289613986)
XLA Ops:
  0.6 1.2 %copy-done.1 = bf16[512,896]{1,0:T(8,128)(2,1)S(1)} copy-done((bf16[512,896]{1,0:T(8,128)(2,1)S(1)}, bf16[512,896]{1,0:T(8,128)(2,1)}, u32[]{:S(2)}) %copy-start.1) | copy-done | bytes 917528
  1.8 0.7 copy-done.11
  2.5 1.4 %shard_map.105 = (bf16[5,512,128]{2,1,0:T(8,128)(2,1)S(1)}, bf16[2,512,128]{2,1,0:T(8,128)(2,1)S(1)}, bf16[5,512,128]{2,1,0:T(8,128)(2,1)S(1)}) custom-call(s32[8,56]{1,0:T(8,128)S(1)} %copy-done.11, bf16[512,896]{1,0:T(8,128)(2,1)S(1)} %copy-done.1), custom_call_target="tpu_custom_call" | custom-call | bytes 2492160 | tf_op jit(solution)/shard_map/pallas_call | solution.py:275
  3.9 2.8 %collective-permute-start = (bf16[5,512,128]{2,1,0:T(8,128)(2,1)S(1)}, bf16[5,512,128]{2,1,0:T(8,128)(2,1)S(1)}, u32[]{:S(2)}, u32[]{:S(2)}) collective-permute-start(bf16[5,512,128]{2,1,0:T(8,128)(2,1)S(1)} %get-tuple-element.24.x1a_ref), channel_id=1, source_target_pairs={{0,4},{4,0},{8,12},{12,8},{16,20},{20,16},{24,28},{28,24},{1,5},{5... | collective-permute-start | bytes 1966088 | tf_op jit(solution)/shard_map/ppermute | solution.py:250
  6.7 1.6 %collective-permute-start.2 = (bf16[5,512,128]{2,1,0:T(8,128)(2,1)S(1)}, bf16[5,512,128]{2,1,0:T(8,128)(2,1)S(1)}, u32[]{:S(2)}, u32[]{:S(2)}) collective-permute-start(bf16[5,512,128]{2,1,0:T(8,128)(2,1)S(1)} %get-tuple-element.27), channel_id=1, source_target_pairs={{0,8},{4,28},{8,16},{12,4},{16,24},{20,12},{24,0},{28,20},{1,9},{5... | collective-permute-start | bytes 1966088 | tf_op jit(solution)/shard_map/ppermute | solution.py:262
  8.3 13.2 %collective-permute-done.x1a_ref = bf16[5,512,128]{2,1,0:T(8,128)(2,1)S(1)} collective-permute-done((bf16[5,512,128]{2,1,0:T(8,128)(2,1)S(1)}, bf16[5,512,128]{2,1,0:T(8,128)(2,1)S(1)}, u32[]{:S(2)}, u32[]{:S(2)}) %collective-permute-start) | collective-permute-done | bytes 655392 | tf_op jit(solution)/shard_map/ppermute | solution.py:250
  21.5 1.7 %collective-permute-start.1 = (bf16[2,512,128]{2,1,0:T(8,128)(2,1)S(1)}, bf16[2,512,128]{2,1,0:T(8,128)(2,1)S(1)}, u32[]{:S(2)}, u32[]{:S(2)}) collective-permute-start(bf16[2,512,128]{2,1,0:T(8,128)(2,1)S(1)} %get-tuple-element.26.x1b_ref), channel_id=1, source_target_pairs={{0,4},{4,0},{8,12},{12,8},{16,20},{20,16},{24,28},{28,24},{1,5},{5... | collective-permute-start | bytes 786440 | tf_op jit(solution)/shard_map/ppermute | solution.py:250
  23.2 1.6 %collective-permute-done.2.z1_ref = bf16[5,512,128]{2,1,0:T(8,128)(2,1)S(1)} collective-permute-done((bf16[5,512,128]{2,1,0:T(8,128)(2,1)S(1)}, bf16[5,512,128]{2,1,0:T(8,128)(2,1)S(1)}, u32[]{:S(2)}, u32[]{:S(2)}) %collective-permute-start.2) | collective-permute-done | bytes 655392 | tf_op jit(solution)/shard_map/ppermute | solution.py:262
  24.8 4.1 %collective-permute-done.1.x1b_ref = bf16[2,512,128]{2,1,0:T(8,128)(2,1)S(1)} collective-permute-done((bf16[2,512,128]{2,1,0:T(8,128)(2,1)S(1)}, bf16[2,512,128]{2,1,0:T(8,128)(2,1)S(1)}, u32[]{:S(2)}, u32[]{:S(2)}) %collective-permute-start.1) | collective-permute-done | bytes 262176 | tf_op jit(solution)/shard_map/ppermute | solution.py:250
  29.0 1.4 %collective-permute-start.5 = (bf16[4,512,128]{2,1,0:T(8,128)(2,1)S(1)}, bf16[4,512,128]{2,1,0:T(8,128)(2,1)S(1)}, u32[]{:S(2)}, u32[]{:S(2)}) collective-permute-start(bf16[4,512,128]{2,1,0:T(8,128)(2,1)S(1)} %slice.13), channel_id=1, source_target_pairs={{0,4},{4,0},{8,12},{12,8},{16,20},{20,16},{24,28},{28,24},{1,5},{5... | collective-permute-start | bytes 1572872 | tf_op jit(solution)/shard_map/ppermute | solution.py:250
  30.4 1.6 %collective-permute-start.4 = (bf16[1,512,128]{2,1,0:T(8,128)(2,1)S(1)}, bf16[1,512,128]{2,1,0:T(8,128)(2,1)S(1)}, u32[]{:S(2)}, u32[]{:S(2)}) collective-permute-start(bf16[1,512,128]{2,1,0:T(8,128)(2,1)S(1)} %slice.12), channel_id=1, source_target_pairs={{0,8},{4,28},{8,16},{12,4},{16,24},{20,12},{24,0},{28,20},{1,9},{5... | collective-permute-start | bytes 393224 | tf_op jit(solution)/shard_map/ppermute | solution.py:262
  32.0 11.3 %collective-permute-done.3.z2a_ref = bf16[5,512,128]{2,1,0:T(8,128)(2,1)S(1)} collective-permute-done((bf16[5,512,128]{2,1,0:T(8,128)(2,1)S(1)}, bf16[5,512,128]{2,1,0:T(8,128)(2,1)S(1)}, u32[]{:S(2)}, u32[]{:S(2)}) %collective-permute-start.3) | collective-permute-done | bytes 655392 | tf_op jit(solution)/shard_map/ppermute | solution.py:262
  43.4 0.8 %copy-done.4 = bf16[4,512,128]{2,1,0:T(8,128)(2,1)} copy-done((bf16[4,512,128]{2,1,0:T(8,128)(2,1)}, bf16[4,512,128]{2,1,0:T(8,128)(2,1)S(1)}, u32[]{:S(2)}) %copy-start.4) | copy-done | bytes 524312
  44.1 0.8 %slice.14 = bf16[4,512,128]{2,1,0:T(8,128)(2,1)} slice(bf16[5,512,128]{2,1,0:T(8,128)(2,1)S(1)} %collective-permute-done.3.z2a_ref), slice={[0:4], [0:512], [0:128]} | slice | bytes 1048576 | tf_op jit(solution)/shard_map/slice | solution.py:311
  45.0 0.7 copy-done.9
  46.2 1.0 %copy.11 = bf16[1,896,32]{2,1,0:T(8,128)(2,1)S(1)} copy(bf16[1,896,32]{1,2,0:T(8,128)(2,1)} %param.15) | data formatting | bytes 114688 | tf_op args[6]
  47.1 1.5 %copy.12.x_basis_ref = bf16[512,32]{1,0:T(8,128)(2,1)} copy(bf16[512,32]{0,1:T(8,128)(2,1)} %param.12) | data formatting | bytes 65536 | tf_op args[3]
  48.7 2.0 %copy-done = bf16[512,3584]{1,0:T(8,128)(2,1)S(1)} copy-done((bf16[512,3584]{1,0:T(8,128)(2,1)S(1)}, bf16[512,3584]{1,0:T(8,128)(2,1)}, u32[]{:S(2)}) %copy-start) | copy-done | bytes 3670040
  50.7 0.9 %copy-done.6 = bf16[512,32]{1,0:T(8,128)(2,1)S(1)} copy-done((bf16[512,32]{1,0:T(8,128)(2,1)S(1)}, bf16[512,32]{1,0:T(8,128)(2,1)}, u32[]{:S(2)}) %copy-start.6) | copy-done | bytes 32792
  51.6 2.2 %shard_map.104 = (bf16[7,512,512]{2,1,0:T(8,128)(2,1)S(1)}, f32[7,512,128]{2,1,0:T(8,128)S(1)}, bf16[192,512]{1,0:T(8,128)(2,1)S(1)}, bf16[7,128,192]{2,1,0:T(8,128)(2,1)S(1)}) custom-call(s32[8,56]{1,0:T(8,128)S(1)} %copy-done.12, s32[8]{0:T(128)S(1)} %copy-done.13, s32[8]{0:T(128)S(1)} %copy-done.14, s32[1,14]{1,0:T(1,128)S(1)} %copy-done.15, ...), custom_call_target="tpu_custom_call" | custom-call | bytes 9807792 | tf_op jit(solution)/shard_map/pallas_call | solution.py:275
  53.8 0.7 shard_map.106.before_ref
  54.8 1.0 %shard_map.107.before_ref = f32[7,512,128]{2,1,0:T(8,128)S(1)} custom-call(bf16[7,512,512]{2,1,0:T(8,128)(2,1)S(1)} %get-tuple-element.22.squares_ref, f32[7,512,128]{2,1,0:T(8,128)S(1)} %shard_map.106.before_ref, bf16[5,512,128]{2,1,0:T(8,128)(2,1)S(1)} %collective-permute-done.x1a_ref, bf16[2,512,128]{2,1,0:T(8,128)(2,1)S(1)} %copy-done.3, ...), custom_call_target="tpu_custom_call" | custom-call | flops 738197504 | bytes 8912896 | tf_op jit(solution)/shard_map/pallas_call | solution.py:275
  55.8 0.8 %shard_map.108.before_ref = f32[7,512,128]{2,1,0:T(8,128)S(1)} custom-call(bf16[7,512,512]{2,1,0:T(8,128)(2,1)S(1)} %get-tuple-element.22.squares_ref, f32[7,512,128]{2,1,0:T(8,128)S(1)} %shard_map.107.before_ref, bf16[5,512,128]{2,1,0:T(8,128)(2,1)S(1)} %collective-permute-done.3.z2a_ref, bf16[1,512,128]{2,1,0:T(8,128)(2,1)S(1)} %copy-done.10, ...), custom_call_target="tpu_custom_call" | custom-call | flops 671088640 | bytes 8650752 | tf_op jit(solution)/shard_map/pallas_call | solution.py:275
  56.7 2.5 %collective-permute-done.7.z3_ref = bf16[4,512,128]{2,1,0:T(8,128)(2,1)} collective-permute-done((bf16[4,512,128]{2,1,0:T(8,128)(2,1)}, bf16[4,512,128]{2,1,0:T(8,128)(2,1)}, u32[]{:S(2)}, u32[]{:S(2)}) %collective-permute-start.7) | collective-permute-done | bytes 524320 | tf_op jit(solution)/shard_map/ppermute | solution.py:262
  59.2 4.2 %shard_map.109 = (bf16[512,896]{1,0:T(8,128)(2,1)}, f32[128,192]{1,0:T(8,128)S(1)}, f32[32,192]{1,0:T(8,128)S(1)}, f32[32,192]{1,0:T(8,128)S(1)}) custom-call(s32[8,56]{1,0:T(8,128)S(1)} %copy-done.12, bf16[7,512,512]{2,1,0:T(8,128)(2,1)S(1)} %get-tuple-element.22.squares_ref, f32[7,512,128]{2,1,0:T(8,128)S(1)} %shard_map.108.before_ref, ...), custom_call_target="tpu_custom_call" | custom-call | flops 603979776 | bytes 8292096 | tf_op jit(solution)/shard_map/pallas_call | solution.py:275
  63.4 1.3 %collective-permute-start.8 = (f32[32,192]{1,0:T(8,128)S(1)}, f32[32,192]{1,0:T(8,128)S(1)}, u32[]{:S(2)}, u32[]{:S(2)}) collective-permute-start(f32[32,192]{1,0:T(8,128)S(1)} %get-tuple-element.37), channel_id=1, source_target_pairs={{0,4},{4,0},{8,12},{12,8},{16,20},{20,16},{24,28},{28,24},{1,5},{5... | collective-permute-start | bytes 73736 | tf_op jit(solution)/shard_map/ppermute | solution.py:250
  64.7 2.3 %collective-permute-start.9 = (f32[32,192]{1,0:T(8,128)S(1)}, f32[32,192]{1,0:T(8,128)S(1)}, u32[]{:S(2)}, u32[]{:S(2)}) collective-permute-start(f32[32,192]{1,0:T(8,128)S(1)} %get-tuple-element.38), channel_id=1, source_target_pairs={{0,28},{4,8},{8,4},{12,16},{16,12},{20,24},{24,20},{28,0},{1,29},{... | collective-permute-start | bytes 73736 | tf_op jit(solution)/shard_map/ppermute | solution.py:256
  67.0 0.6 collective-permute-done.8.got_a_ref
  67.6 3.7 %collective-permute-done.9.got_b_ref = f32[32,192]{1,0:T(8,128)S(1)} collective-permute-done((f32[32,192]{1,0:T(8,128)S(1)}, f32[32,192]{1,0:T(8,128)S(1)}, u32[]{:S(2)}, u32[]{:S(2)}) %collective-permute-start.9) | collective-permute-done | bytes 24608 | tf_op jit(solution)/shard_map/ppermute | solution.py:256
  71.5 1.6 %collective-permute-start.11 = (f32[128,32]{1,0:T(8,128)S(1)}, f32[128,32]{1,0:T(8,128)S(1)}, u32[]{:S(2)}, u32[]{:S(2)}) collective-permute-start(f32[128,32]{1,0:T(8,128)S(1)} %get-tuple-element.41), channel_id=1, source_target_pairs={{0,3},{1,2},{2,1},{3,0},{4,7},{5,6},{6,5},{7,4},{8,11},{9,10},{10,... | collective-permute-start | bytes 49160 | tf_op jit(solution)/shard_map/ppermute | solution.py:256
  73.1 2.2 %collective-permute-done.11.got_b_ref = f32[128,32]{1,0:T(8,128)S(1)} collective-permute-done((f32[128,32]{1,0:T(8,128)S(1)}, f32[128,32]{1,0:T(8,128)S(1)}, u32[]{:S(2)}, u32[]{:S(2)}) %collective-permute-start.11) | collective-permute-done | bytes 16416 | tf_op jit(solution)/shard_map/ppermute | solution.py:256
  75.4 0.7 shard_map.111
  (39 shorter events, 1.1 us)
Async XLA Ops:
  0.6 1.2 %copy-start.1 = (bf16[512,896]{1,0:T(8,128)(2,1)S(1)}, bf16[512,896]{1,0:T(8,128)(2,1)}, u32[]{:S(2)}) copy-start(bf16[512,896]{1,0:T(8,128)(2,1)} %density_ref.1) | copy-start | bytes 2752516
  1.8 0.7 copy-start.11
  2.5 46.2 %copy-start.12 = (s32[8,56]{1,0:T(8,128)S(1)}, s32[8,56]{1,0:T(8,128)}, u32[]{:S(2)}) copy-start(s32[8,56]{1,0:T(8,128)} %pattern_ref.5) | copy-start | bytes 5380
  2.5 46.2 %copy-start.13 = (s32[8]{0:T(128)S(1)}, s32[8]{0:T(128)}, u32[]{:S(2)}) copy-start(s32[8]{0:T(128)} %x_offset_ref.1) | copy-start | bytes 100
  2.5 46.2 %copy-start.14 = (s32[8]{0:T(128)S(1)}, s32[8]{0:T(128)}, u32[]{:S(2)}) copy-start(s32[8]{0:T(128)} %x_extent_ref.1) | copy-start | bytes 100
  2.5 46.2 %copy-start.15 = (s32[1,14]{1,0:T(1,128)S(1)}, s32[1,14]{1,0:T(1,128)}, u32[]{:S(2)}) copy-start(s32[1,14]{1,0:T(1,128)} %y_offset_ref.1) | copy-start | bytes 172
  2.5 46.2 %copy-start.16 = (s32[1,14]{1,0:T(1,128)S(1)}, s32[1,14]{1,0:T(1,128)}, u32[]{:S(2)}) copy-start(s32[1,14]{1,0:T(1,128)} %y_extent_ref.1) | copy-start | bytes 172
  3.9 41.1 %copy-start.7 = (bf16[2,512,128]{2,1,0:T(8,128)(2,1)}, bf16[2,512,128]{2,1,0:T(8,128)(2,1)S(1)}, u32[]{:S(2)}) copy-start(bf16[2,512,128]{2,1,0:T(8,128)(2,1)S(1)} %get-tuple-element.26.x1b_ref) | copy-start | bytes 786436
  3.9 17.6 %collective-permute-start = (bf16[5,512,128]{2,1,0:T(8,128)(2,1)S(1)}, bf16[5,512,128]{2,1,0:T(8,128)(2,1)S(1)}, u32[]{:S(2)}, u32[]{:S(2)}) collective-permute-start(bf16[5,512,128]{2,1,0:T(8,128)(2,1)S(1)} %get-tuple-element.24.x1a_ref), channel_id=1, source_target_pairs={{0,4},{4,0},{8,12},{12,8},{16,20},{20,16},{24,28},{28,24},{1,5},{5... | collective-permute-start | bytes 1966088 | tf_op jit(solution)/shard_map/ppermute | solution.py:250
  6.7 18.1 %collective-permute-start.2 = (bf16[5,512,128]{2,1,0:T(8,128)(2,1)S(1)}, bf16[5,512,128]{2,1,0:T(8,128)(2,1)S(1)}, u32[]{:S(2)}, u32[]{:S(2)}) collective-permute-start(bf16[5,512,128]{2,1,0:T(8,128)(2,1)S(1)} %get-tuple-element.27), channel_id=1, source_target_pairs={{0,8},{4,28},{8,16},{12,4},{16,24},{20,12},{24,0},{28,20},{1,9},{5... | collective-permute-start | bytes 1966088 | tf_op jit(solution)/shard_map/ppermute | solution.py:262
  21.5 7.5 %collective-permute-start.1 = (bf16[2,512,128]{2,1,0:T(8,128)(2,1)S(1)}, bf16[2,512,128]{2,1,0:T(8,128)(2,1)S(1)}, u32[]{:S(2)}, u32[]{:S(2)}) collective-permute-start(bf16[2,512,128]{2,1,0:T(8,128)(2,1)S(1)} %get-tuple-element.26.x1b_ref), channel_id=1, source_target_pairs={{0,4},{4,0},{8,12},{12,8},{16,20},{20,16},{24,28},{28,24},{1,5},{5... | collective-permute-start | bytes 786440 | tf_op jit(solution)/shard_map/ppermute | solution.py:250
  24.8 18.6 %collective-permute-start.3 = (bf16[5,512,128]{2,1,0:T(8,128)(2,1)S(1)}, bf16[5,512,128]{2,1,0:T(8,128)(2,1)S(1)}, u32[]{:S(2)}, u32[]{:S(2)}) collective-permute-start(bf16[5,512,128]{2,1,0:T(8,128)(2,1)S(1)} %collective-permute-done.x1a_ref), channel_id=1, source_target_pairs={{0,8},{4,28},{8,16},{12,4},{16,24},{20,12},{24,0},{28,20},{1,9},{5... | collective-permute-start | bytes 1966088 | tf_op jit(solution)/shard_map/ppermute | solution.py:262
  29.0 16.0 %copy-start.2 = (bf16[2,512,128]{2,1,0:T(8,128)(2,1)}, bf16[2,512,128]{2,1,0:T(8,128)(2,1)S(1)}, u32[]{:S(2)}) copy-start(bf16[2,512,128]{2,1,0:T(8,128)(2,1)S(1)} %collective-permute-done.1.x1b_ref) | copy-start | bytes 786436
  29.0 14.4 %collective-permute-start.5 = (bf16[4,512,128]{2,1,0:T(8,128)(2,1)S(1)}, bf16[4,512,128]{2,1,0:T(8,128)(2,1)S(1)}, u32[]{:S(2)}, u32[]{:S(2)}) collective-permute-start(bf16[4,512,128]{2,1,0:T(8,128)(2,1)S(1)} %slice.13), channel_id=1, source_target_pairs={{0,4},{4,0},{8,12},{12,8},{16,20},{20,16},{24,28},{28,24},{1,5},{5... | collective-permute-start | bytes 1572872 | tf_op jit(solution)/shard_map/ppermute | solution.py:250
  30.4 14.6 %collective-permute-start.4 = (bf16[1,512,128]{2,1,0:T(8,128)(2,1)S(1)}, bf16[1,512,128]{2,1,0:T(8,128)(2,1)S(1)}, u32[]{:S(2)}, u32[]{:S(2)}) collective-permute-start(bf16[1,512,128]{2,1,0:T(8,128)(2,1)S(1)} %slice.12), channel_id=1, source_target_pairs={{0,8},{4,28},{8,16},{12,4},{16,24},{20,12},{24,0},{28,20},{1,9},{5... | collective-permute-start | bytes 393224 | tf_op jit(solution)/shard_map/ppermute | solution.py:262
  43.4 0.8 %copy-start.4 = (bf16[4,512,128]{2,1,0:T(8,128)(2,1)}, bf16[4,512,128]{2,1,0:T(8,128)(2,1)S(1)}, u32[]{:S(2)}) copy-start(bf16[4,512,128]{2,1,0:T(8,128)(2,1)S(1)} %collective-permute-done.5.x3_ref) | copy-start | bytes 1572868
  44.1 15.0 %collective-permute-start.6 = (bf16[5,512,128]{2,1,0:T(8,128)(2,1)S(1)}, bf16[5,512,128]{2,1,0:T(8,128)(2,1)S(1)}, u32[]{:S(2)}, u32[]{:S(2)}) collective-permute-start(bf16[5,512,128]{2,1,0:T(8,128)(2,1)S(1)} %collective-permute-done.3.z2a_ref), channel_id=1, source_target_pairs={{0,4},{4,0},{8,12},{12,8},{16,20},{20,16},{24,28},{28,24},{1,5},{5... | collective-permute-start | bytes 1966088 | tf_op jit(solution)/shard_map/ppermute | solution.py:250
  45.0 0.7 copy-start.9
  45.7 13.5 %collective-permute-start.7 = (bf16[4,512,128]{2,1,0:T(8,128)(2,1)}, bf16[4,512,128]{2,1,0:T(8,128)(2,1)}, u32[]{:S(2)}, u32[]{:S(2)}) collective-permute-start(bf16[4,512,128]{2,1,0:T(8,128)(2,1)} %slice.14), channel_id=1, source_target_pairs={{0,8},{4,28},{8,16},{12,4},{16,24},{20,12},{24,0},{28,20},{1,9},{5... | collective-permute-start | bytes 1572872 | tf_op jit(solution)/shard_map/ppermute | solution.py:262
  48.7 2.0 %copy-start = (bf16[512,3584]{1,0:T(8,128)(2,1)S(1)}, bf16[512,3584]{1,0:T(8,128)(2,1)}, u32[]{:S(2)}) copy-start(bf16[512,3584]{1,0:T(8,128)(2,1)} %p2_ref.1) | copy-start | bytes 11010052
  50.7 0.9 %copy-start.6 = (bf16[512,32]{1,0:T(8,128)(2,1)S(1)}, bf16[512,32]{1,0:T(8,128)(2,1)}, u32[]{:S(2)}) copy-start(bf16[512,32]{1,0:T(8,128)(2,1)} %copy.12.x_basis_ref) | copy-start | bytes 98308
  51.6 2.2 %copy-start.8 = (bf16[2,512,128]{2,1,0:T(8,128)(2,1)S(1)}, bf16[2,512,128]{2,1,0:T(8,128)(2,1)}, u32[]{:S(2)}) copy-start(bf16[2,512,128]{2,1,0:T(8,128)(2,1)} %copy-done.7) | copy-start | bytes 786436
  53.8 1.0 %copy-start.3 = (bf16[2,512,128]{2,1,0:T(8,128)(2,1)S(1)}, bf16[2,512,128]{2,1,0:T(8,128)(2,1)}, u32[]{:S(2)}) copy-start(bf16[2,512,128]{2,1,0:T(8,128)(2,1)} %copy-done.2) | copy-start | bytes 786436
  54.8 1.0 %copy-start.5 = (bf16[4,512,128]{2,1,0:T(8,128)(2,1)S(1)}, bf16[4,512,128]{2,1,0:T(8,128)(2,1)}, u32[]{:S(2)}) copy-start(bf16[4,512,128]{2,1,0:T(8,128)(2,1)} %copy-done.4) | copy-start | bytes 1572868
  54.8 1.1 %copy-start.10 = (bf16[1,512,128]{2,1,0:T(8,128)(2,1)S(1)}, bf16[1,512,128]{2,1,0:T(8,128)(2,1)}, u32[]{:S(2)}) copy-start(bf16[1,512,128]{2,1,0:T(8,128)(2,1)} %copy-done.9) | copy-start | bytes 393220
  63.4 4.2 %collective-permute-start.8 = (f32[32,192]{1,0:T(8,128)S(1)}, f32[32,192]{1,0:T(8,128)S(1)}, u32[]{:S(2)}, u32[]{:S(2)}) collective-permute-start(f32[32,192]{1,0:T(8,128)S(1)} %get-tuple-element.37), channel_id=1, source_target_pairs={{0,4},{4,0},{8,12},{12,8},{16,20},{20,16},{24,28},{28,24},{1,5},{5... | collective-permute-start | bytes 73736 | tf_op jit(solution)/shard_map/ppermute | solution.py:250
  64.7 6.6 %collective-permute-start.9 = (f32[32,192]{1,0:T(8,128)S(1)}, f32[32,192]{1,0:T(8,128)S(1)}, u32[]{:S(2)}, u32[]{:S(2)}) collective-permute-start(f32[32,192]{1,0:T(8,128)S(1)} %get-tuple-element.38), channel_id=1, source_target_pairs={{0,28},{4,8},{8,4},{12,16},{16,12},{20,24},{24,20},{28,0},{1,29},{... | collective-permute-start | bytes 73736 | tf_op jit(solution)/shard_map/ppermute | solution.py:256
  71.4 1.7 %collective-permute-start.10 = (f32[128,32]{1,0:T(8,128)S(1)}, f32[128,32]{1,0:T(8,128)S(1)}, u32[]{:S(2)}, u32[]{:S(2)}) collective-permute-start(f32[128,32]{1,0:T(8,128)S(1)} %get-tuple-element.40), channel_id=1, source_target_pairs={{0,1},{1,0},{2,3},{3,2},{4,5},{5,4},{6,7},{7,6},{8,9},{9,8},{10,11... | collective-permute-start | bytes 49160 | tf_op jit(solution)/shard_map/ppermute | solution.py:250
  71.5 3.9 %collective-permute-start.11 = (f32[128,32]{1,0:T(8,128)S(1)}, f32[128,32]{1,0:T(8,128)S(1)}, u32[]{:S(2)}, u32[]{:S(2)}) collective-permute-start(f32[128,32]{1,0:T(8,128)S(1)} %get-tuple-element.41), channel_id=1, source_target_pairs={{0,3},{1,2},{2,1},{3,0},{4,7},{5,6},{6,5},{7,4},{8,11},{9,10},{10,... | collective-permute-start | bytes 49160 | tf_op jit(solution)/shard_map/ppermute | solution.py:256

commit v2 on v1

--- a/solution.py
+++ b/solution.py
@@ -16,7 +16,6 @@
 CHUNKS = 2 * HD + 1
 VMEM = pl.BlockSpec(memory_space=pltpu.VMEM)
 SMEM = pl.BlockSpec(memory_space=pltpu.SMEM)
-LIMIT = pltpu.CompilerParams(vmem_limit_bytes=40 * 1024 * 1024)
 F32 = jnp.float32
 BF16 = jnp.bfloat16
 
@@ -45,16 +44,34 @@
     return [dims.n_col * (chunk * dims.stride + s) + column for s in range(dims.stride)]
 
 
-def mask_kernel(dims, pattern_ref, density_ref, x1a_ref, x1b_ref, z1_ref):
+def mask_kernel(
+    dims, pattern_hbm, density_hbm, x1a_ref, x1b_ref, z1_ref, pattern_ref, tile_ref, pattern_sem, sems
+):
     odd = lax.axis_index("row") % 2
     column = lax.axis_index("col")
     bs, uw = dims.bs, dims.uw
     near = x1a_ref.shape[0]
+    wide = tile_ref.shape[2]
+    fetch_pattern = pltpu.make_async_copy(pattern_hbm, pattern_ref, pattern_sem)
+    fetch_pattern.start()
+    parts = tile_ref.shape[0]
+    fetches = []
+    for part in range(parts):
+        cols = pl.ds(part * wide, wide)
+        fetch = pltpu.make_async_copy(density_hbm.at[:, cols], tile_ref.at[part], sems.at[part])
+        fetch.start()
+        fetches.append(fetch)
+    fetch_pattern.wait()
+    arrived = 0
     for chunk in range(CHUNKS):
+        part, start = divmod(chunk * uw, wide)
+        if part == arrived:
+            fetches[part].wait()
+            arrived += 1
         for i in range(dims.br):
             rows = slice(i * bs, (i + 1) * bs)
             mask = block_mask(pattern_ref, i, own_slots(dims, chunk, column), bs, BF16)
-            kept = density_ref[rows, chunk * uw : (chunk + 1) * uw] * mask
+            kept = tile_ref[part, rows, start : start + uw] * mask
             for lane_odd in (0, 1):
                 own = chunk if lane_odd else CHUNKS - 1 - chunk
                 sent = CHUNKS - 1 - own
@@ -89,6 +106,7 @@
     summed_ref,
     xt_ref,
     y_ref,
+    mask_ref,
 ):
     odd = lax.axis_index("row") % 2
     column = lax.axis_index("col")
@@ -109,6 +127,9 @@
         ]
         own = parts[0] if len(parts) == 1 else jnp.concatenate(parts, axis=1)
         summed_ref[place] = 1.5 * own
+        for i in range(br):
+            slots = own_slots(dims, chunk, column)
+            mask_ref[place, i : i + 1, :] = 2.0 * block_mask(pattern_ref, i, slots, bs, F32)
         for s in range(dims.stride):
             m = chunk * dims.stride + s
             tx = y_basis_ref.shape[1]
@@ -158,67 +179,78 @@
     )
 
 
-def second_kernel(squares_ref, before_ref, x1a_ref, x1b_ref, z1_ref, summed_ref):
+def second_kernel(squares_ref, before_ref, x1a_ref, z1_ref, summed_ref):
     summed_ref[...] = before_ref[...]
-    near = x1a_ref.shape[0]
-    partner = lambda j: x1a_ref.at[j] if j < near else x1b_ref.at[j - near]
-    add_products(
-        squares_ref[HD - 1], [(j - 1, partner(j)) for j in range(1, CHUNKS)], summed_ref
-    )
+    add_products(squares_ref[HD - 1], [(j - 1, x1a_ref.at[j]) for j in range(1, 5)], summed_ref)
     add_products(squares_ref[HD + 2], [(j + 2, z1_ref.at[j]) for j in range(5)], summed_ref)
 
 
-def third_kernel(squares_ref, before_ref, z2a_ref, z2b_ref, x3_ref, summed_ref):
+def third_kernel(squares_ref, before_ref, z2a_ref, x1b_ref, x3_ref, summed_ref):
     summed_ref[...] = before_ref[...]
-    next_tile = lambda j: z2a_ref.at[j] if j < 5 else z2b_ref.at[j - 5]
-    add_products(
-        squares_ref[HD + 1], [(j + 1, next_tile(j)) for j in range(6)], summed_ref
-    )
+    add_products(squares_ref[HD + 1], [(j + 1, z2a_ref.at[j]) for j in range(5)], summed_ref)
+    add_products(squares_ref[HD - 1], [(4 + j, x1b_ref.at[j]) for j in range(2)], summed_ref)
     add_products(squares_ref[HD - 3], [(3 - j, x3_ref.at[j]) for j in range(4)], summed_ref)
+
+
+def fourth_kernel(squares_ref, before_ref, z2b_ref, z3_ref, summed_ref):
+    summed_ref[...] = before_ref[...]
+    add_products(squares_ref[HD + 1], [(6, z2b_ref.at[0])], summed_ref)
+    add_products(squares_ref[HD + 3], [(j + 3, z3_ref.at[j]) for j in range(4)], summed_ref)
 
 
 def last_kernel(
     dims,
-    pattern_ref,
+    mask_ref,
     squares_ref,
     before_ref,
     x2_ref,
-    z3_ref,
     xt_ref,
     y_ref,
     new_ref,
     middle_ref,
     rim_a_ref,
     rim_b_ref,
-    summed_ref,
 ):
     odd = lax.axis_index("row") % 2
-    column = lax.axis_index("col")
     bs, uw = dims.bs, dims.uw
-    summed_ref[...] = before_ref[...]
-    add_products(squares_ref[HD - 2], [(4 - j, x2_ref.at[j]) for j in range(5)], summed_ref)
-    add_products(squares_ref[HD + 3], [(j + 3, z3_ref.at[j]) for j in range(4)], summed_ref)
-    half = jnp.zeros((dims.rows, EY), F32)
-    for k in range(CHUNKS):
-        chunk = jnp.where(odd == 1, k, CHUNKS - 1 - k)
-        pieces = []
+
+    def finish(k, total):
         for i in range(dims.br):
-            mask = block_mask(pattern_ref, i, own_slots(dims, chunk, column), bs, F32)
-            pieces.append(summed_ref[k, i * bs : (i + 1) * bs, :] * (2.0 * mask))
-        renewed = jnp.concatenate(pieces, axis=0).astype(BF16)
-        for lane_odd in (0, 1):
-            at = k if lane_odd else CHUNKS - 1 - k
-
-            @pl.when(odd == lane_odd)
-            def _():
-                new_ref[:, at * uw : (at + 1) * uw] = renewed
-
-        half = half + jnp.dot(renewed, y_ref[k], preferred_element_type=F32)
+            rows = slice(i * bs, (i + 1) * bs)
+            kept = total[rows] * mask_ref[k, i : i + 1, :]
+            new_ref[rows, k * uw : (k + 1) * uw] = kept.astype(BF16)
+
+    for group in ((0, 1), (2, 3), (4,)):
+        tiles = [x2_ref[4 - k] for k in group]
+        wide = tiles[0] if len(tiles) == 1 else jnp.concatenate(tiles, axis=1)
+        product = jnp.dot(squares_ref[HD - 2], wide, preferred_element_type=F32)
+        for at, k in enumerate(group):
+            finish(k, before_ref[k] - product[:, at * uw : (at + 1) * uw])
+    for k in (5, 6):
+        finish(k, before_ref[k])
+    half = jnp.dot(
+        new_ref[...], y_ref[...].reshape(CHUNKS * uw, EY), preferred_element_type=F32
+    )
     extended = jnp.dot(xt_ref[...], half.astype(BF16), preferred_element_type=F32)
     middle_ref[...] = extended[M : M + SX]
     lower, upper = extended[:M], extended[SX + M :]
     rim_a_ref[...] = jnp.where(odd == 1, lower, upper)
     rim_b_ref[...] = jnp.where(odd == 1, upper, lower)
+
+
+def order_kernel(dims, own_ref, new_ref):
+    odd = lax.axis_index("row") % 2
+    uw = dims.uw
+
+    @pl.when(odd == 1)
+    def _():
+        new_ref[...] = own_ref[...]
+
+    @pl.when(odd == 0)
+    def _():
+        for k in range(CHUNKS):
+            at = CHUNKS - 1 - k
+            new_ref[:, at * uw : (at + 1) * uw] = own_ref[:, k * uw : (k + 1) * uw]
 
 
 def row_rims_kernel(middle_ref, got_a_ref, got_b_ref, center_ref, rim_a_ref, rim_b_ref):
@@ -266,10 +298,15 @@
     return lax.optimization_barrier((value,) + others)[0]
 
 
-def call(kernel, outs, ins, scratch=(), flops=0):
+def call(kernel, outs, ins, scratch=(), beside=0, stay=(), limit=24):
     shapes = [jax.ShapeDtypeStruct(shape, dtype) for shape, dtype in outs]
     specs = [
-        SMEM if jnp.issubdtype(value.dtype, jnp.integer) else VMEM for value in ins
+        pl.BlockSpec(memory_space=pltpu.HBM)
+        if at in stay
+        else SMEM
+        if jnp.issubdtype(value.dtype, jnp.integer)
+        else VMEM
+        for at, value in enumerate(ins)
     ]
     moved = sum(value.size * value.dtype.itemsize for value in list(ins) + shapes)
     return pl.pallas_call(
@@ -278,42 +315,58 @@
         in_specs=specs,
         out_specs=[VMEM] * len(shapes),
         scratch_shapes=list(scratch),
-        compiler_params=LIMIT,
-        cost_estimate=pl.CostEstimate(flops=flops, bytes_accessed=moved, transcendentals=0),
+        compiler_params=pltpu.CompilerParams(vmem_limit_bytes=limit * 2**20),
+        cost_estimate=pl.CostEstimate(
+            flops=beside * 10**9, bytes_accessed=moved, transcendentals=0
+        ),
     )(*ins)
 
 
 def shards(p2_panel, density, pattern, x_basis, x_offset, x_extent, y_basis, y_offset, y_extent):
     dims = Dims(pattern, x_basis, lax.axis_size("col"))
     rows, uw = dims.rows, dims.uw
-    per_chunk = 2 * rows * rows * uw
     chunks = lambda count: ((count, rows, uw), BF16)
     total = ((CHUNKS, rows, uw), F32)
 
+    parts = CHUNKS if uw % 128 == 0 else 1
     own_a, own_b, own_z = call(
-        functools.partial(mask_kernel, dims), [chunks(5), chunks(2), chunks(5)], [pattern, density]
+        functools.partial(mask_kernel, dims),
+        [chunks(5), chunks(2), chunks(5)],
+        [pattern, density],
+        scratch=[
+            pltpu.SMEM(pattern.shape, jnp.int32),
+            pltpu.VMEM((parts, rows, CHUNKS * uw // parts), BF16),
+            pltpu.SemaphoreType.DMA(()),
+            pltpu.SemaphoreType.DMA((parts,)),
+        ],
+        stay=(0, 1),
+        limit=60,
     )
     x1a = swap_partner(own_a, "row")
     z1 = shift_level(own_z)
-    squares, summed, xt, y_spread = call(
+    squares, summed, xt, y_spread, mask = call(
         functools.partial(spread_kernel, dims),
-        [((CHUNKS, rows, rows), BF16), total, ((EX, rows), BF16), ((CHUNKS, uw, EY), BF16)],
+        [
+            ((CHUNKS, rows, rows), BF16),
+            total,
+            ((EX, rows), BF16),
+            ((CHUNKS, uw, EY), BF16),
+            ((CHUNKS, dims.br, uw), F32),
+        ],
         [pattern, x_offset, x_extent, y_offset, y_extent, p2_panel, x_basis, y_basis[0]],
-    )
-    (summed,) = call(first_kernel, [total], [squares, summed, own_a, own_b], flops=7 * per_chunk)
-    x1b = swap_partner(after(own_b, x1a), "row")
-    z2a = shift_level(after(x1a, z1))
-    x3 = swap_partner(after(z1[:4], x1b), "row")
-    z2b = shift_level(after(x1b[:1], z1))
-    (summed,) = call(
-        second_kernel, [total], [squares, summed, x1a, x1b, z1], flops=11 * per_chunk
-    )
-    z3 = shift_level(after(z2a[:4], z2b))
-    x2 = swap_partner(after(z2a, x3), "row")
-    (summed,) = call(
-        third_kernel, [total], [squares, summed, z2a, z2b, x3], flops=10 * per_chunk
-    )
-    new_density, middle, rim_a, rim_b = call(
+        beside=12,
+    )
+    (summed,) = call(first_kernel, [total], [squares, summed, own_a, own_b])
+    z2a = shift_level(after(x1a, summed))
+    x1b = swap_partner(after(own_b, x1a, summed), "row")
+    x3 = swap_partner(z1[:4], "row")
+    (summed,) = call(second_kernel, [total], [squares, summed, x1a, z1], beside=12)
+    x2 = swap_partner(z2a, "row")
+    z3 = shift_level(z2a[:4])
+    z2b = shift_level(after(x1b[:1], z2a))
+    (summed,) = call(third_kernel, [total], [squares, summed, z2a, x1b, x3], beside=12)
+    (summed,) = call(fourth_kernel, [total], [squares, summed, z2b, z3])
+    new_own, middle, rim_a, rim_b = call(
         functools.partial(last_kernel, dims),
         [
             ((rows, dims.wc * dims.bs), BF16),
@@ -321,9 +374,10 @@
             ((M, EY), F32),
             ((M, EY), F32),
         ],
-        [pattern, squares, summed, x2, z3, xt, y_spread],
-        scratch=[pltpu.VMEM((CHUNKS, rows, uw), F32)],
-        flops=9 * per_chunk,
+        [mask, squares, summed, x2, xt, y_spread],
+    )
+    (new_density,) = call(
+        functools.partial(order_kernel, dims), [(new_own.shape, BF16)], [new_own]
     )
     got_a = swap_partner(rim_a, "row")
     got_b = swap_other(rim_b, "row")

time: 76.6 us -> 72 us (0.940)
  waiting for transfers between devices: 39.2 us -> 31.7 us
  starting transfers between devices: 15 us -> 20.4 us
  local copies, waits for them, and re-layouts: 9.96 us -> 7.29 us
    ppermute x6, waiting for transfers between devices: 17.9 us -> 5.7 us  [swap_partner(): return lax.ppermute(value, axis, [(s, s ^ 1) for s in range(count)])]
    ppermute x4, waiting for transfers between devices: 15.4 us -> 20.5 us  [shift_level(): return lax.ppermute(value, 'row', pairs)]
    ppermute x6, starting transfers between devices: 7.35 us -> 12.2 us  [swap_partner(): return lax.ppermute(value, axis, [(s, s ^ 1) for s in range(count)])]
    unnamed x36 -> x18, local copies, waits for them, and re-layouts: 9.07 us -> 7.21 us
    slice x3, local copies, waits for them, and re-layouts: 0.89 us -> 0.08 us  [the longest x1 0.03 us: shards(): x3 = swap_partner(z1[:4], 'row')]
    ppermute x4, starting transfers between devices: 3.69 us -> 4.5 us  [shift_level(): return lax.ppermute(value, 'row', pairs)]
    pallas_call x8 -> x10, Pallas kernels: 11.2 us -> 11.5 us  [call(): pl.pallas_call(kernel, out_shape=shapes, in_specs=specs, out_specs=[VMEM]...]
  transfers between devices with their start and end apart: 12 -> 12, of which waited for: 8 -> 8; matrix products, arithmetic and copies ran while one was open for 4% -> 3% of each run, Pallas kernels for 6% -> 9%
where the time goes in v2:
time: 72 us; the launch traced here: 71.7 us
  waiting for transfers between devices  31.7 us (44%)
  starting transfers between devices  20.4 us (28%)
  Pallas kernels  11.5 us (16%)
  local copies, waits for them, and re-layouts  7.29 us (10%)
  between operations  0.76 us (1%)
    ppermute x4, waiting for transfers between devices, shift_level(): return lax.ppermute(value, 'row', pairs)  20.5 us
    ppermute x6, starting transfers between devices, swap_partner(): return lax.ppermute(value, axis, [(s, s ^ 1) for s in range(count)])  12.2 us
    pallas_call x10, Pallas kernels, call(): pl.pallas_call(kernel, out_shape=shapes, in_specs=specs, out_specs=[VMEM]...  11.5 us
    unnamed x18, local copies, waits for them, and re-layouts  7.21 us
    ppermute x6, waiting for transfers between devices, swap_partner(): return lax.ppermute(value, axis, [(s, s ^ 1) for s in range(count)])  5.7 us
    ppermute x2, waiting for transfers between devices, swap_other(): return lax.ppermute(value, axis, pairs)  5.51 us
    ppermute x4, starting transfers between devices, shift_level(): return lax.ppermute(value, 'row', pairs)  4.5 us
    ppermute x2, starting transfers between devices, swap_other(): return lax.ppermute(value, axis, pairs)  3.65 us
  transfers between devices with their start and end apart: 12, of which 8 were waited for; matrix products, arithmetic and copies ran while one was open for 3% of the time, Pallas kernels for 9%

profile of v2, /device:TPU:0, one launch (start us, length us, event | category | flops | bytes accessed | tf_op | source)
XLA Modules:
  0.0 71.7 jit_solution(18303883928638423451)
XLA Ops:
  0.6 2.9 %shard_map.105 = (bf16[5,512,128]{2,1,0:T(8,128)(2,1)}, bf16[2,512,128]{2,1,0:T(8,128)(2,1)}, bf16[5,512,128]{2,1,0:T(8,128)(2,1)}) custom-call(s32[8,56]{1,0:T(8,128)} %pattern_hbm.1, bf16[512,896]{1,0:T(8,128)(2,1)} %density_hbm.1), custom_call_target="tpu_custom_call" | custom-call | bytes 2492160 | tf_op jit(solution)/shard_map/pallas_call | solution.py:312
  3.5 2.8 %collective-permute-start = (bf16[5,512,128]{2,1,0:T(8,128)(2,1)}, bf16[5,512,128]{2,1,0:T(8,128)(2,1)S(1)}, u32[]{:S(2)}, u32[]{:S(2)}) collective-permute-start(bf16[5,512,128]{2,1,0:T(8,128)(2,1)} %get-tuple-element.23.x1a_ref), channel_id=1, source_target_pairs={{0,4},{4,0},{8,12},{12,8},{16,20},{20,16},{24,28},{28,24},{1,5},{5... | collective-permute-start | bytes 1966088 | tf_op jit(solution)/shard_map/ppermute | solution.py:282
  6.4 1.6 %collective-permute-start.1 = (bf16[5,512,128]{2,1,0:T(8,128)(2,1)}, bf16[5,512,128]{2,1,0:T(8,128)(2,1)S(1)}, u32[]{:S(2)}, u32[]{:S(2)}) collective-permute-start(bf16[5,512,128]{2,1,0:T(8,128)(2,1)} %get-tuple-element.25), channel_id=1, source_target_pairs={{0,8},{4,28},{8,16},{12,4},{16,24},{20,12},{24,0},{28,20},{1,9},{5... | collective-permute-start | bytes 1966088 | tf_op jit(solution)/shard_map/ppermute | solution.py:294
  7.9 1.0 %copy.11 = bf16[1,896,32]{2,1,0:T(8,128)(2,1)S(1)} copy(bf16[1,896,32]{1,2,0:T(8,128)(2,1)} %param.15) | data formatting | bytes 114688 | tf_op args[6]
  8.9 0.9 %copy.12.x_basis_ref = bf16[512,32]{1,0:T(8,128)(2,1)S(1)} copy(bf16[512,32]{0,1:T(8,128)(2,1)} %param.12) | data formatting | bytes 65536 | tf_op args[3]
  9.8 0.7 copy-done.2
  10.5 2.0 %copy-done.3 = bf16[512,3584]{1,0:T(8,128)(2,1)S(1)} copy-done((bf16[512,3584]{1,0:T(8,128)(2,1)S(1)}, bf16[512,3584]{1,0:T(8,128)(2,1)}, u32[]{:S(2)}) %copy-start.3) | copy-done | bytes 3670040
  12.6 0.7 copy-done.4
  13.2 0.7 copy-done.5
  13.9 0.7 copy-done.6
  15.2 2.2 %shard_map.104 = (bf16[7,512,512]{2,1,0:T(8,128)(2,1)S(1)}, f32[7,512,128]{2,1,0:T(8,128)S(1)}, bf16[192,512]{1,0:T(8,128)(2,1)S(1)}, bf16[7,128,192]{2,1,0:T(8,128)(2,1)S(1)}, f32[7,8,128]{2,1,0:T(8,128)S(1)}) custom-call(s32[8,56]{1,0:T(8,128)S(1)} %copy-done.2, s32[8]{0:T(128)S(1)} %copy-done.4, s32[8]{0:T(128)S(1)} %copy-done.5, s32[1,14]{1,0:T(1,128)S(1)} %copy-done.6, ...), custom_call_target="tpu_custom_call" | custom-call | flops 12000000000 | bytes 9836464 | tf_op jit(solution)/shard_map/pallas_call | solution.py:312
  17.4 0.7 shard_map.106.before_ref
  18.1 3.2 %collective-permute-done.x1a_ref = bf16[5,512,128]{2,1,0:T(8,128)(2,1)S(1)} collective-permute-done((bf16[5,512,128]{2,1,0:T(8,128)(2,1)}, bf16[5,512,128]{2,1,0:T(8,128)(2,1)S(1)}, u32[]{:S(2)}, u32[]{:S(2)}) %collective-permute-start) | collective-permute-done | bytes 655392 | tf_op jit(solution)/shard_map/ppermute | solution.py:282
  21.3 1.7 %collective-permute-start.3 = (bf16[2,512,128]{2,1,0:T(8,128)(2,1)S(1)}, bf16[2,512,128]{2,1,0:T(8,128)(2,1)S(1)}, u32[]{:S(2)}, u32[]{:S(2)}) collective-permute-start(bf16[2,512,128]{2,1,0:T(8,128)(2,1)S(1)} %copy-done.1), channel_id=1, source_target_pairs={{0,4},{4,0},{8,12},{12,8},{16,20},{20,16},{24,28},{28,24},{1,5},{5... | collective-permute-start | bytes 786440 | tf_op jit(solution)/shard_map/ppermute | solution.py:282
  23.1 1.6 %collective-permute-start.2 = (bf16[5,512,128]{2,1,0:T(8,128)(2,1)S(1)}, bf16[5,512,128]{2,1,0:T(8,128)(2,1)S(1)}, u32[]{:S(2)}, u32[]{:S(2)}) collective-permute-start(bf16[5,512,128]{2,1,0:T(8,128)(2,1)S(1)} %collective-permute-done.x1a_ref), channel_id=1, source_target_pairs={{0,8},{4,28},{8,16},{12,4},{16,24},{20,12},{24,0},{28,20},{1,9},{5... | collective-permute-start | bytes 1966088 | tf_op jit(solution)/shard_map/ppermute | solution.py:294
  24.7 2.8 %collective-permute-start.4 = (bf16[4,512,128]{2,1,0:T(8,128)(2,1)S(1)}, bf16[4,512,128]{2,1,0:T(8,128)(2,1)S(1)}, u32[]{:S(2)}, u32[]{:S(2)}) collective-permute-start(bf16[4,512,128]{2,1,0:T(8,128)(2,1)S(1)} %slice.12), channel_id=1, source_target_pairs={{0,4},{4,0},{8,12},{12,8},{16,20},{20,16},{24,28},{28,24},{1,5},{5... | collective-permute-start | bytes 1572872 | tf_op jit(solution)/shard_map/ppermute | solution.py:282
  27.5 0.8 %shard_map.107.before_ref = f32[7,512,128]{2,1,0:T(8,128)S(1)} custom-call(bf16[7,512,512]{2,1,0:T(8,128)(2,1)S(1)} %get-tuple-element.21.squares_ref, f32[7,512,128]{2,1,0:T(8,128)S(1)} %shard_map.106.before_ref, bf16[5,512,128]{2,1,0:T(8,128)(2,1)S(1)} %collective-permute-done.x1a_ref, bf16[5,512,128]{2,1,0:T(8,128)(2,1)S(1)} %collective-permute-done.1.z1_ref), custom_call_target="tpu_custom_call" | custom-call | flops 12000000000 | bytes 8650752 | tf_op jit(solution)/shard_map/pallas_call | solution.py:312
  28.3 2.2 %collective-permute-done.3.x1b_ref = bf16[2,512,128]{2,1,0:T(8,128)(2,1)S(1)} collective-permute-done((bf16[2,512,128]{2,1,0:T(8,128)(2,1)S(1)}, bf16[2,512,128]{2,1,0:T(8,128)(2,1)S(1)}, u32[]{:S(2)}, u32[]{:S(2)}) %collective-permute-start.3) | collective-permute-done | bytes 262176 | tf_op jit(solution)/shard_map/ppermute | solution.py:282
  30.6 9.7 %collective-permute-done.2.z2a_ref = bf16[5,512,128]{2,1,0:T(8,128)(2,1)S(1)} collective-permute-done((bf16[5,512,128]{2,1,0:T(8,128)(2,1)S(1)}, bf16[5,512,128]{2,1,0:T(8,128)(2,1)S(1)}, u32[]{:S(2)}, u32[]{:S(2)}) %collective-permute-start.2) | collective-permute-done | bytes 655392 | tf_op jit(solution)/shard_map/ppermute | solution.py:294
  40.3 1.3 %collective-permute-start.6 = (bf16[4,512,128]{2,1,0:T(8,128)(2,1)S(1)}, bf16[4,512,128]{2,1,0:T(8,128)(2,1)S(1)}, u32[]{:S(2)}, u32[]{:S(2)}) collective-permute-start(bf16[4,512,128]{2,1,0:T(8,128)(2,1)S(1)} %slice.14), channel_id=1, source_target_pairs={{0,8},{4,28},{8,16},{12,4},{16,24},{20,12},{24,0},{28,20},{1,9},{5... | collective-permute-start | bytes 1572872 | tf_op jit(solution)/shard_map/ppermute | solution.py:294
  41.6 3.0 %collective-permute-start.7 = (bf16[5,512,128]{2,1,0:T(8,128)(2,1)S(1)}, bf16[5,512,128]{2,1,0:T(8,128)(2,1)S(1)}, u32[]{:S(2)}, u32[]{:S(2)}) collective-permute-start(bf16[5,512,128]{2,1,0:T(8,128)(2,1)S(1)} %collective-permute-done.2.z2a_ref), channel_id=1, source_target_pairs={{0,4},{4,0},{8,12},{12,8},{16,20},{20,16},{24,28},{28,24},{1,5},{5... | collective-permute-start | bytes 1966088 | tf_op jit(solution)/shard_map/ppermute | solution.py:282
  44.7 1.0 %shard_map.108.before_ref = f32[7,512,128]{2,1,0:T(8,128)S(1)} custom-call(bf16[7,512,512]{2,1,0:T(8,128)(2,1)S(1)} %get-tuple-element.21.squares_ref, f32[7,512,128]{2,1,0:T(8,128)S(1)} %shard_map.107.before_ref, bf16[5,512,128]{2,1,0:T(8,128)(2,1)S(1)} %collective-permute-done.2.z2a_ref, bf16[2,512,128]{2,1,0:T(8,128)(2,1)S(1)} %collective-permute-done.3.x1b_ref, ...), custom_call_target="tpu_custom_call" | custom-call | flops 12000000000 | bytes 8781824 | tf_op jit(solution)/shard_map/pallas_call | solution.py:312
  45.7 2.8 %collective-permute-done.5.z2b_ref = bf16[1,512,128]{2,1,0:T(8,128)(2,1)S(1)} collective-permute-done((bf16[1,512,128]{2,1,0:T(8,128)(2,1)S(1)}, bf16[1,512,128]{2,1,0:T(8,128)(2,1)S(1)}, u32[]{:S(2)}, u32[]{:S(2)}) %collective-permute-start.5) | collective-permute-done | bytes 131104 | tf_op jit(solution)/shard_map/ppermute | solution.py:294
  48.5 8.0 %collective-permute-done.6.z3_ref = bf16[4,512,128]{2,1,0:T(8,128)(2,1)S(1)} collective-permute-done((bf16[4,512,128]{2,1,0:T(8,128)(2,1)S(1)}, bf16[4,512,128]{2,1,0:T(8,128)(2,1)S(1)}, u32[]{:S(2)}, u32[]{:S(2)}) %collective-permute-start.6) | collective-permute-done | bytes 524320 | tf_op jit(solution)/shard_map/ppermute | solution.py:294
  57.1 1.4 %shard_map.110 = (bf16[512,896]{1,0:T(8,128)(2,1)S(1)}, f32[128,192]{1,0:T(8,128)S(1)}, f32[32,192]{1,0:T(8,128)S(1)}, f32[32,192]{1,0:T(8,128)S(1)}) custom-call(f32[7,8,128]{2,1,0:T(8,128)S(1)} %get-tuple-element.20.mask_ref, bf16[7,512,512]{2,1,0:T(8,128)(2,1)S(1)} %get-tuple-element.21.squares_ref, f32[7,512,128]{2,1,0:T(8,128)S(1)} %shard_map.109.before_ref, ...), custom_call_target="tpu_custom_call" | custom-call | bytes 7794688 | tf_op jit(solution)/shard_map/pallas_call | solution.py:312
  58.5 1.7 %collective-permute-start.8 = (f32[32,192]{1,0:T(8,128)S(1)}, f32[32,192]{1,0:T(8,128)S(1)}, u32[]{:S(2)}, u32[]{:S(2)}) collective-permute-start(f32[32,192]{1,0:T(8,128)S(1)} %get-tuple-element.33), channel_id=1, source_target_pairs={{0,4},{4,0},{8,12},{12,8},{16,20},{20,16},{24,28},{28,24},{1,5},{5... | collective-permute-start | bytes 73736 | tf_op jit(solution)/shard_map/ppermute | solution.py:282
  60.2 2.0 %collective-permute-start.9 = (f32[32,192]{1,0:T(8,128)S(1)}, f32[32,192]{1,0:T(8,128)S(1)}, u32[]{:S(2)}, u32[]{:S(2)}) collective-permute-start(f32[32,192]{1,0:T(8,128)S(1)} %get-tuple-element.34), channel_id=1, source_target_pairs={{0,28},{4,8},{8,4},{12,16},{16,12},{20,24},{24,20},{28,0},{1,29},{... | collective-permute-start | bytes 73736 | tf_op jit(solution)/shard_map/ppermute | solution.py:288
  62.5 4.3 %collective-permute-done.9.got_b_ref = f32[32,192]{1,0:T(8,128)S(1)} collective-permute-done((f32[32,192]{1,0:T(8,128)S(1)}, f32[32,192]{1,0:T(8,128)S(1)}, u32[]{:S(2)}, u32[]{:S(2)}) %collective-permute-start.9) | collective-permute-done | bytes 24608 | tf_op jit(solution)/shard_map/ppermute | solution.py:288
  67.1 1.6 %collective-permute-start.11 = (f32[128,32]{1,0:T(8,128)S(1)}, f32[128,32]{1,0:T(8,128)S(1)}, u32[]{:S(2)}, u32[]{:S(2)}) collective-permute-start(f32[128,32]{1,0:T(8,128)S(1)} %get-tuple-element.37), channel_id=1, source_target_pairs={{0,3},{1,2},{2,1},{3,0},{4,7},{5,6},{6,5},{7,4},{8,11},{9,10},{10,... | collective-permute-start | bytes 49160 | tf_op jit(solution)/shard_map/ppermute | solution.py:288
  68.7 1.1 %shard_map.111 = bf16[512,896]{1,0:T(8,128)(2,1)} custom-call(bf16[512,896]{1,0:T(8,128)(2,1)S(1)} %get-tuple-element.31.own_ref), custom_call_target="tpu_custom_call" | custom-call | bytes 1835008 | tf_op jit(solution)/shard_map/pallas_call | solution.py:312
  69.8 1.2 %collective-permute-done.11.got_b_ref = f32[128,32]{1,0:T(8,128)S(1)} collective-permute-done((f32[128,32]{1,0:T(8,128)S(1)}, f32[128,32]{1,0:T(8,128)S(1)}, u32[]{:S(2)}, u32[]{:S(2)}) %collective-permute-start.11) | collective-permute-done | bytes 16416 | tf_op jit(solution)/shard_map/ppermute | solution.py:288
  70.9 0.7 %shard_map.113 = f32[128,128]{1,0:T(8,128)} custom-call(f32[128,128]{1,0:T(8,128)S(1)} %get-tuple-element.35.center_ref, f32[128,32]{1,0:T(8,128)S(1)} %collective-permute-done.10.got_a_ref, f32[128,32]{1,0:T(8,128)S(1)} %collective-permute-done.11.got_b_ref), custom_call_target="tpu_custom_call" | custom-call | bytes 163840 | tf_op jit(solution)/shard_map/pallas_call | solution.py:312
  (23 shorter events, 1.8 us)
Async XLA Ops:
  3.5 17.8 %collective-permute-start = (bf16[5,512,128]{2,1,0:T(8,128)(2,1)}, bf16[5,512,128]{2,1,0:T(8,128)(2,1)S(1)}, u32[]{:S(2)}, u32[]{:S(2)}) collective-permute-start(bf16[5,512,128]{2,1,0:T(8,128)(2,1)} %get-tuple-element.23.x1a_ref), channel_id=1, source_target_pairs={{0,4},{4,0},{8,12},{12,8},{16,20},{20,16},{24,28},{28,24},{1,5},{5... | collective-permute-start | bytes 1966088 | tf_op jit(solution)/shard_map/ppermute | solution.py:282
  6.4 18.3 %collective-permute-start.1 = (bf16[5,512,128]{2,1,0:T(8,128)(2,1)}, bf16[5,512,128]{2,1,0:T(8,128)(2,1)S(1)}, u32[]{:S(2)}, u32[]{:S(2)}) collective-permute-start(bf16[5,512,128]{2,1,0:T(8,128)(2,1)} %get-tuple-element.25), channel_id=1, source_target_pairs={{0,8},{4,28},{8,16},{12,4},{16,24},{20,12},{24,0},{28,20},{1,9},{5... | collective-permute-start | bytes 1966088 | tf_op jit(solution)/shard_map/ppermute | solution.py:294
  9.8 0.7 copy-start.2
  10.5 2.0 %copy-start.3 = (bf16[512,3584]{1,0:T(8,128)(2,1)S(1)}, bf16[512,3584]{1,0:T(8,128)(2,1)}, u32[]{:S(2)}) copy-start(bf16[512,3584]{1,0:T(8,128)(2,1)} %p2_ref.1) | copy-start | bytes 11010052
  12.6 0.7 copy-start.4
  13.2 0.7 copy-start.5
  13.9 0.7 copy-start.6
  14.5 0.7 copy-start.7
  15.2 2.2 %copy-start = (bf16[5,512,128]{2,1,0:T(8,128)(2,1)S(1)}, bf16[5,512,128]{2,1,0:T(8,128)(2,1)}, u32[]{:S(2)}) copy-start(bf16[5,512,128]{2,1,0:T(8,128)(2,1)} %get-tuple-element.23.x1a_ref) | copy-start | bytes 1966084
  15.2 2.2 %copy-start.1 = (bf16[2,512,128]{2,1,0:T(8,128)(2,1)S(1)}, bf16[2,512,128]{2,1,0:T(8,128)(2,1)}, u32[]{:S(2)}) copy-start(bf16[2,512,128]{2,1,0:T(8,128)(2,1)} %get-tuple-element.27.x1b_ref) | copy-start | bytes 786436
  21.3 9.2 %collective-permute-start.3 = (bf16[2,512,128]{2,1,0:T(8,128)(2,1)S(1)}, bf16[2,512,128]{2,1,0:T(8,128)(2,1)S(1)}, u32[]{:S(2)}, u32[]{:S(2)}) collective-permute-start(bf16[2,512,128]{2,1,0:T(8,128)(2,1)S(1)} %copy-done.1), channel_id=1, source_target_pairs={{0,4},{4,0},{8,12},{12,8},{16,20},{20,16},{24,28},{28,24},{1,5},{5... | collective-permute-start | bytes 786440 | tf_op jit(solution)/shard_map/ppermute | solution.py:282
  23.1 17.2 %collective-permute-start.2 = (bf16[5,512,128]{2,1,0:T(8,128)(2,1)S(1)}, bf16[5,512,128]{2,1,0:T(8,128)(2,1)S(1)}, u32[]{:S(2)}, u32[]{:S(2)}) collective-permute-start(bf16[5,512,128]{2,1,0:T(8,128)(2,1)S(1)} %collective-permute-done.x1a_ref), channel_id=1, source_target_pairs={{0,8},{4,28},{8,16},{12,4},{16,24},{20,12},{24,0},{28,20},{1,9},{5... | collective-permute-start | bytes 1966088 | tf_op jit(solution)/shard_map/ppermute | solution.py:294
  24.7 20.0 %collective-permute-start.4 = (bf16[4,512,128]{2,1,0:T(8,128)(2,1)S(1)}, bf16[4,512,128]{2,1,0:T(8,128)(2,1)S(1)}, u32[]{:S(2)}, u32[]{:S(2)}) collective-permute-start(bf16[4,512,128]{2,1,0:T(8,128)(2,1)S(1)} %slice.12), channel_id=1, source_target_pairs={{0,4},{4,0},{8,12},{12,8},{16,20},{20,16},{24,28},{28,24},{1,5},{5... | collective-permute-start | bytes 1572872 | tf_op jit(solution)/shard_map/ppermute | solution.py:282
  40.2 8.2 %collective-permute-start.5 = (bf16[1,512,128]{2,1,0:T(8,128)(2,1)S(1)}, bf16[1,512,128]{2,1,0:T(8,128)(2,1)S(1)}, u32[]{:S(2)}, u32[]{:S(2)}) collective-permute-start(bf16[1,512,128]{2,1,0:T(8,128)(2,1)S(1)} %slice.13), channel_id=1, source_target_pairs={{0,8},{4,28},{8,16},{12,4},{16,24},{20,12},{24,0},{28,20},{1,9},{5... | collective-permute-start | bytes 393224 | tf_op jit(solution)/shard_map/ppermute | solution.py:294
  40.3 16.2 %collective-permute-start.6 = (bf16[4,512,128]{2,1,0:T(8,128)(2,1)S(1)}, bf16[4,512,128]{2,1,0:T(8,128)(2,1)S(1)}, u32[]{:S(2)}, u32[]{:S(2)}) collective-permute-start(bf16[4,512,128]{2,1,0:T(8,128)(2,1)S(1)} %slice.14), channel_id=1, source_target_pairs={{0,8},{4,28},{8,16},{12,4},{16,24},{20,12},{24,0},{28,20},{1,9},{5... | collective-permute-start | bytes 1572872 | tf_op jit(solution)/shard_map/ppermute | solution.py:294
  41.6 15.5 %collective-permute-start.7 = (bf16[5,512,128]{2,1,0:T(8,128)(2,1)S(1)}, bf16[5,512,128]{2,1,0:T(8,128)(2,1)S(1)}, u32[]{:S(2)}, u32[]{:S(2)}) collective-permute-start(bf16[5,512,128]{2,1,0:T(8,128)(2,1)S(1)} %collective-permute-done.2.z2a_ref), channel_id=1, source_target_pairs={{0,4},{4,0},{8,12},{12,8},{16,20},{20,16},{24,28},{28,24},{1,5},{5... | collective-permute-start | bytes 1966088 | tf_op jit(solution)/shard_map/ppermute | solution.py:282
  58.5 4.0 %collective-permute-start.8 = (f32[32,192]{1,0:T(8,128)S(1)}, f32[32,192]{1,0:T(8,128)S(1)}, u32[]{:S(2)}, u32[]{:S(2)}) collective-permute-start(f32[32,192]{1,0:T(8,128)S(1)} %get-tuple-element.33), channel_id=1, source_target_pairs={{0,4},{4,0},{8,12},{12,8},{16,20},{20,16},{24,28},{28,24},{1,5},{5... | collective-permute-start | bytes 73736 | tf_op jit(solution)/shard_map/ppermute | solution.py:282
  60.2 6.6 %collective-permute-start.9 = (f32[32,192]{1,0:T(8,128)S(1)}, f32[32,192]{1,0:T(8,128)S(1)}, u32[]{:S(2)}, u32[]{:S(2)}) collective-permute-start(f32[32,192]{1,0:T(8,128)S(1)} %get-tuple-element.34), channel_id=1, source_target_pairs={{0,28},{4,8},{8,4},{12,16},{16,12},{20,24},{24,20},{28,0},{1,29},{... | collective-permute-start | bytes 73736 | tf_op jit(solution)/shard_map/ppermute | solution.py:288
  67.0 2.8 %collective-permute-start.10 = (f32[128,32]{1,0:T(8,128)S(1)}, f32[128,32]{1,0:T(8,128)S(1)}, u32[]{:S(2)}, u32[]{:S(2)}) collective-permute-start(f32[128,32]{1,0:T(8,128)S(1)} %get-tuple-element.36), channel_id=1, source_target_pairs={{0,1},{1,0},{2,3},{3,2},{4,5},{5,4},{6,7},{7,6},{8,9},{9,8},{10,11... | collective-permute-start | bytes 49160 | tf_op jit(solution)/shard_map/ppermute | solution.py:282
  67.1 3.9 %collective-permute-start.11 = (f32[128,32]{1,0:T(8,128)S(1)}, f32[128,32]{1,0:T(8,128)S(1)}, u32[]{:S(2)}, u32[]{:S(2)}) collective-permute-start(f32[128,32]{1,0:T(8,128)S(1)} %get-tuple-element.37), channel_id=1, source_target_pairs={{0,3},{1,2},{2,1},{3,0},{4,7},{5,6},{6,5},{7,4},{8,11},{9,10},{10,... | collective-permute-start | bytes 49160 | tf_op jit(solution)/shard_map/ppermute | solution.py:288

commit v3 on v2

--- a/solution.py
+++ b/solution.py
@@ -14,6 +14,9 @@
 EX = SX + 2 * M
 EY = SY + 2 * M
 CHUNKS = 2 * HD + 1
+NEAR = 4
+KA, K1, KE, KB, KC = 12, 4, 1, 0, 5
+D_Z2P, D_X1Q, D_X3, D_X2Q, D_Z2Q, D_X2P, D_KE, D_ZB, D_ORD, D_Z1 = 1, 0, 1, 0, 0, 1, 0, 1, 1, 0
 VMEM = pl.BlockSpec(memory_space=pltpu.VMEM)
 SMEM = pl.BlockSpec(memory_space=pltpu.SMEM)
 F32 = jnp.float32
@@ -45,20 +48,25 @@
 
 
 def mask_kernel(
-    dims, pattern_hbm, density_hbm, x1a_ref, x1b_ref, z1_ref, pattern_ref, tile_ref, pattern_sem, sems
+    dims,
+    pattern_hbm,
+    density_hbm,
+    x1a_ref,
+    x1b_ref,
+    *refs,
 ):
+    z1_refs, refs = refs[:-8], refs[-8:]
+    pattern_ref, tile_ref, kept_ref, pattern_sem, tile_sems, x1a_sem, x1b_sem, z1_sem = refs
     odd = lax.axis_index("row") % 2
     column = lax.axis_index("col")
     bs, uw = dims.bs, dims.uw
-    near = x1a_ref.shape[0]
     wide = tile_ref.shape[2]
     fetch_pattern = pltpu.make_async_copy(pattern_hbm, pattern_ref, pattern_sem)
     fetch_pattern.start()
-    parts = tile_ref.shape[0]
     fetches = []
-    for part in range(parts):
+    for part in range(tile_ref.shape[0]):
         cols = pl.ds(part * wide, wide)
-        fetch = pltpu.make_async_copy(density_hbm.at[:, cols], tile_ref.at[part], sems.at[part])
+        fetch = pltpu.make_async_copy(density_hbm.at[:, cols], tile_ref.at[part], tile_sems.at[part])
         fetch.start()
         fetches.append(fetch)
     fetch_pattern.wait()
@@ -71,19 +79,21 @@
         for i in range(dims.br):
             rows = slice(i * bs, (i + 1) * bs)
             mask = block_mask(pattern_ref, i, own_slots(dims, chunk, column), bs, BF16)
-            kept = tile_ref[part, rows, start : start + uw] * mask
-            for lane_odd in (0, 1):
-                own = chunk if lane_odd else CHUNKS - 1 - chunk
-                sent = CHUNKS - 1 - own
-
-                @pl.when(odd == lane_odd)
-                def _():
-                    if sent < near:
-                        x1a_ref[sent, rows, :] = kept
-                    else:
-                        x1b_ref[sent - near, rows, :] = kept
-                    if own < near:
-                        z1_ref[own, rows, :] = kept
+            kept_ref[chunk, rows, :] = tile_ref[part, rows, start : start + uw] * mask
+    own = lambda k: jnp.where(odd == 1, k, CHUNKS - 1 - k)
+    copies = []
+    for j in range(CHUNKS):
+        near = x1a_ref.shape[0]
+        dest, sem = (x1a_ref.at[j], x1a_sem.at[j]) if j < near else (x1b_ref.at[j - near], x1b_sem.at[j - near])
+        copies.append(pltpu.make_async_copy(kept_ref.at[own(CHUNKS - 1 - j)], dest, sem))
+        copies[-1].start()
+    first = z1_refs[0].shape[0]
+    for k in range(5):
+        dest = z1_refs[0].at[k] if k < first else z1_refs[1].at[k - first]
+        copies.append(pltpu.make_async_copy(kept_ref.at[own(k)], dest, z1_sem.at[k]))
+        copies[-1].start()
+    for copy in copies:
+        copy.wait()
 
 
 def own_block_cols(dims, p2_ref, slot, column):
@@ -179,23 +189,15 @@
     )
 
 
-def second_kernel(squares_ref, before_ref, x1a_ref, z1_ref, summed_ref):
+def stage_kernel(counts, terms, squares_ref, before_ref, *refs):
+    summed_ref = refs[-1]
     summed_ref[...] = before_ref[...]
-    add_products(squares_ref[HD - 1], [(j - 1, x1a_ref.at[j]) for j in range(1, 5)], summed_ref)
-    add_products(squares_ref[HD + 2], [(j + 2, z1_ref.at[j]) for j in range(5)], summed_ref)
-
-
-def third_kernel(squares_ref, before_ref, z2a_ref, x1b_ref, x3_ref, summed_ref):
-    summed_ref[...] = before_ref[...]
-    add_products(squares_ref[HD + 1], [(j + 1, z2a_ref.at[j]) for j in range(5)], summed_ref)
-    add_products(squares_ref[HD - 1], [(4 + j, x1b_ref.at[j]) for j in range(2)], summed_ref)
-    add_products(squares_ref[HD - 3], [(3 - j, x3_ref.at[j]) for j in range(4)], summed_ref)
-
-
-def fourth_kernel(squares_ref, before_ref, z2b_ref, z3_ref, summed_ref):
-    summed_ref[...] = before_ref[...]
-    add_products(squares_ref[HD + 1], [(6, z2b_ref.at[0])], summed_ref)
-    add_products(squares_ref[HD + 3], [(j + 3, z3_ref.at[j]) for j in range(4)], summed_ref)
+    for distance, pairs in terms:
+        add_products(
+            squares_ref[HD + distance],
+            [(place, refs[which].at[at]) for place, which, at in pairs],
+            summed_ref,
+        )
 
 
 def last_kernel(
@@ -203,16 +205,14 @@
     mask_ref,
     squares_ref,
     before_ref,
-    x2_ref,
-    xt_ref,
-    y_ref,
-    new_ref,
-    middle_ref,
-    rim_a_ref,
-    rim_b_ref,
+    *refs,
 ):
+    xt_ref, y_ref, new_ref, middle_ref, rim_a_ref, rim_b_ref = refs[-6:]
+    x2_refs = refs[:-6]
     odd = lax.axis_index("row") % 2
     bs, uw = dims.bs, dims.uw
+
+    x2_tile = lambda j: x2_refs[0][j] if j < NEAR else x2_refs[1][j - NEAR]
 
     def finish(k, total):
         for i in range(dims.br):
@@ -221,7 +221,7 @@
             new_ref[rows, k * uw : (k + 1) * uw] = kept.astype(BF16)
 
     for group in ((0, 1), (2, 3), (4,)):
-        tiles = [x2_ref[4 - k] for k in group]
+        tiles = [x2_tile(4 - k) for k in group]
         wide = tiles[0] if len(tiles) == 1 else jnp.concatenate(tiles, axis=1)
         product = jnp.dot(squares_ref[HD - 2], wide, preferred_element_type=F32)
         for at, k in enumerate(group):
@@ -298,7 +298,7 @@
     return lax.optimization_barrier((value,) + others)[0]
 
 
-def call(kernel, outs, ins, scratch=(), beside=0, stay=(), limit=24):
+def call(kernel, outs, ins, scratch=(), beside=0, stay=(), limit=24, out_stay=False, light=False):
     shapes = [jax.ShapeDtypeStruct(shape, dtype) for shape, dtype in outs]
     specs = [
         pl.BlockSpec(memory_space=pltpu.HBM)
@@ -313,11 +313,11 @@
         kernel,
         out_shape=shapes,
         in_specs=specs,
-        out_specs=[VMEM] * len(shapes),
+        out_specs=[pl.BlockSpec(memory_space=pltpu.HBM if out_stay else VMEM.memory_space)] * len(shapes),
         scratch_shapes=list(scratch),
         compiler_params=pltpu.CompilerParams(vmem_limit_bytes=limit * 2**20),
         cost_estimate=pl.CostEstimate(
-            flops=beside * 10**9, bytes_accessed=moved, transcendentals=0
+            flops=beside * 10**9, bytes_accessed=0 if light else moved, transcendentals=0
         ),
     )(*ins)
 
@@ -329,21 +329,32 @@
     total = ((CHUNKS, rows, uw), F32)
 
     parts = CHUNKS if uw % 128 == 0 else 1
-    own_a, own_b, own_z = call(
+    own_a, own_b, *own_z = call(
         functools.partial(mask_kernel, dims),
-        [chunks(5), chunks(2), chunks(5)],
+        [chunks(NEAR), chunks(CHUNKS - NEAR)] + ([chunks(4), chunks(1)] if D_ZB else [chunks(5)]),
         [pattern, density],
         scratch=[
             pltpu.SMEM(pattern.shape, jnp.int32),
             pltpu.VMEM((parts, rows, CHUNKS * uw // parts), BF16),
+            pltpu.VMEM((CHUNKS, rows, uw), BF16),
             pltpu.SemaphoreType.DMA(()),
             pltpu.SemaphoreType.DMA((parts,)),
+            pltpu.SemaphoreType.DMA((NEAR,)),
+            pltpu.SemaphoreType.DMA((CHUNKS - NEAR,)),
+            pltpu.SemaphoreType.DMA((5,)),
         ],
         stay=(0, 1),
         limit=60,
-    )
-    x1a = swap_partner(own_a, "row")
-    z1 = shift_level(own_z)
+        out_stay=True,
+    )
+    if D_ORD == 0:
+        x1p = swap_partner(own_a, "row")
+        z1 = shift_level(own_z[0])
+        x1q = swap_partner(own_b, "row") if D_X1Q == 0 else None
+    else:
+        x1q = swap_partner(own_b, "row") if D_X1Q == 0 else None
+        z1 = shift_level(own_z[0])
+        x1p = swap_partner(own_a, "row")
     squares, summed, xt, y_spread, mask = call(
         functools.partial(spread_kernel, dims),
         [
@@ -354,18 +365,55 @@
             ((CHUNKS, dims.br, uw), F32),
         ],
         [pattern, x_offset, x_extent, y_offset, y_extent, p2_panel, x_basis, y_basis[0]],
-        beside=12,
-    )
-    (summed,) = call(first_kernel, [total], [squares, summed, own_a, own_b])
-    z2a = shift_level(after(x1a, summed))
-    x1b = swap_partner(after(own_b, x1a, summed), "row")
-    x3 = swap_partner(z1[:4], "row")
-    (summed,) = call(second_kernel, [total], [squares, summed, x1a, z1], beside=12)
-    x2 = swap_partner(z2a, "row")
-    z3 = shift_level(z2a[:4])
-    z2b = shift_level(after(x1b[:1], z2a))
-    (summed,) = call(third_kernel, [total], [squares, summed, z2a, x1b, x3], beside=12)
-    (summed,) = call(fourth_kernel, [total], [squares, summed, z2b, z3])
+        beside=KA,
+    )
+    if D_X1Q == 1:
+        x1q = swap_partner(after(own_b, summed), "row")
+    (summed,) = call(first_kernel, [total], [squares, summed, own_a, own_b], beside=K1)
+    if D_X1Q == 2:
+        x1q = swap_partner(after(own_b, x1p), "row")
+    z2p = shift_level(after(x1p, *([[], [summed], [z1], [summed, z1]][D_Z2P])))
+    x3 = swap_partner(after(z1[:4], *([[], [x1p], [summed]][D_X3])), "row")
+    z2q = shift_level(after(x1q[: 6 - NEAR], *([[], [z1], [summed], [z1, summed]][D_Z2Q])))
+    z1b = shift_level(own_z[1]) if D_ZB else None
+
+    def stage(summed, beside, ins, terms):
+        which = {id(value): at for at, value in enumerate(ins)}
+        listed = [
+            (distance, [(place, which[id(value)], at) for place, value, at in pairs])
+            for distance, pairs in terms
+        ]
+        return call(
+            functools.partial(stage_kernel, None, listed),
+            [total],
+            [squares, summed] + ins,
+            beside=beside,
+        )[0]
+
+    near_terms = [(j - 1, x1p, j) for j in range(1, NEAR)]
+    rest_terms = [(j - 1, x1q, j - NEAR) for j in range(NEAR, CHUNKS)]
+    z1_terms = [(j + 2, z1, j) for j in range(4)]
+    z1_rest = (6, z1b, 0) if D_ZB else (6, z1, 4)
+    if D_KE:
+        summed = stage(summed, KE, [x1p, x1q, z1], [(-1, near_terms + rest_terms), (2, z1_terms)])
+    else:
+        summed = stage(summed, KE, [x1p, z1], [(-1, near_terms), (2, z1_terms)])
+    x2p = swap_partner(after(z2p, *([[], [x3], [summed]][D_X2P])), "row")
+    z3 = shift_level(z2p[:4])
+    summed = stage(summed, KB, [z2p], [(1, [(j + 1, z2p, j) for j in range(NEAR)])])
+    x2 = [x2p]
+    if NEAR < 5:
+        x2.append(
+            swap_partner(after(z2q[: 5 - NEAR], *([[], [x3], [z2p], [x3, summed]][D_X2Q])), "row")
+        )
+    late = [(1, [(j + 1, z2q, j - NEAR) for j in range(NEAR, 6)]), (2, [z1_rest])]
+    late.append((-3, [(3 - j, x3, j) for j in range(4)]))
+    ins = [z2q, x3, z1b if D_ZB else z1]
+    if not D_KE:
+        late.append((-1, rest_terms))
+        ins.append(x1q)
+    summed = stage(summed, KC, ins, late)
+    summed = stage(summed, 0, [z3], [(3, [(j + 3, z3, j) for j in range(4)])])
     new_own, middle, rim_a, rim_b = call(
         functools.partial(last_kernel, dims),
         [
@@ -374,7 +422,7 @@
             ((M, EY), F32),
             ((M, EY), F32),
         ],
-        [mask, squares, summed, x2, xt, y_spread],
+        [mask, squares, summed, *x2, xt, y_spread],
     )
     (new_density,) = call(
         functools.partial(order_kernel, dims), [(new_own.shape, BF16)], [new_own]

time: 72 us -> 68.7 us (0.954)
  waiting for transfers between devices: 31.7 us -> 22.9 us
  starting transfers between devices: 20.4 us -> 26 us
    ppermute x4 -> x5, waiting for transfers between devices: 20.5 us -> 15.1 us  [shift_level(): return lax.ppermute(value, 'row', pairs)]
    ppermute x4 -> x5, starting transfers between devices: 4.5 us -> 7.7 us  [shift_level(): return lax.ppermute(value, 'row', pairs)]
    ppermute x6 -> x7, waiting for transfers between devices: 5.7 us -> 3.86 us  [swap_partner(): return lax.ppermute(value, axis, [(s, s ^ 1) for s in range(count)])]
    ppermute x2, waiting for transfers between devices: 5.51 us -> 3.94 us  [swap_other(): return lax.ppermute(value, axis, pairs)]
    ppermute x2, starting transfers between devices: 3.65 us -> 5.2 us  [swap_other(): return lax.ppermute(value, axis, pairs)]
    ppermute x6 -> x7, starting transfers between devices: 12.2 us -> 13.1 us  [swap_partner(): return lax.ppermute(value, axis, [(s, s ^ 1) for s in range(count)])]
    pallas_call x10 -> x11, Pallas kernels: 11.5 us -> 11.4 us  [call(): pl.pallas_call(kernel, out_shape=shapes, in_specs=specs, out_specs=[pl.Bl...]
    unnamed x18 -> x20, local copies, waits for them, and re-layouts: 7.21 us -> 7.21 us
  transfers between devices with their start and end apart: 12 -> 14, of which waited for: 8 -> 9; matrix products, arithmetic and copies ran while one was open for 3% -> 3% of each run, Pallas kernels for 9% -> 10%
where the time goes in v3:
time: 68.7 us; the launch traced here: 68.3 us
  starting transfers between devices  26 us (38%)
  waiting for transfers between devices  22.9 us (33%)
  Pallas kernels  11.4 us (17%)
  local copies, waits for them, and re-layouts  7.24 us (11%)
  between operations  0.8 us (1%)
    ppermute x5, waiting for transfers between devices, shift_level(): return lax.ppermute(value, 'row', pairs)  15.1 us
    ppermute x7, starting transfers between devices, swap_partner(): return lax.ppermute(value, axis, [(s, s ^ 1) for s in range(count)])  13.1 us
    pallas_call x11, Pallas kernels, call(): pl.pallas_call(kernel, out_shape=shapes, in_specs=specs, out_specs=[pl.Bl...  11.4 us
    ppermute x5, starting transfers between devices, shift_level(): return lax.ppermute(value, 'row', pairs)  7.7 us
    unnamed x20, local copies, waits for them, and re-layouts  7.21 us
    ppermute x2, starting transfers between devices, swap_other(): return lax.ppermute(value, axis, pairs)  5.2 us
    ppermute x2, waiting for transfers between devices, swap_other(): return lax.ppermute(value, axis, pairs)  3.94 us
    ppermute x7, waiting for transfers between devices, swap_partner(): return lax.ppermute(value, axis, [(s, s ^ 1) for s in range(count)])  3.86 us
  transfers between devices with their start and end apart: 14, of which 9 were waited for; matrix products, arithmetic and copies ran while one was open for 3% of the time, Pallas kernels for 10%

profile of v3, /device:TPU:0, one launch (start us, length us, event | category | flops | bytes accessed | tf_op | source)
XLA Modules:
  0.0 68.3 jit_solution(14960676504957168630)
XLA Ops:
  0.6 2.6 %shard_map.105 = (bf16[4,512,128]{2,1,0:T(8,128)(2,1)}, bf16[3,512,128]{2,1,0:T(8,128)(2,1)}, bf16[4,512,128]{2,1,0:T(8,128)(2,1)}, bf16[1,512,128]{2,1,0:T(8,128)(2,1)}) custom-call(s32[8,56]{1,0:T(8,128)} %pattern_hbm.1, bf16[512,896]{1,0:T(8,128)(2,1)} %density_hbm.1), custom_call_target="tpu_custom_call" | custom-call | bytes 2492160 | tf_op jit(solution)/shard_map/pallas_call | solution.py:312
  3.2 3.0 %collective-permute-start = (bf16[4,512,128]{2,1,0:T(8,128)(2,1)}, bf16[4,512,128]{2,1,0:T(8,128)(2,1)S(1)}, u32[]{:S(2)}, u32[]{:S(2)}) collective-permute-start(bf16[4,512,128]{2,1,0:T(8,128)(2,1)} %get-tuple-element.24.x1a_ref), channel_id=1, source_target_pairs={{0,4},{4,0},{8,12},{12,8},{16,20},{20,16},{24,28},{28,24},{1,5},{5... | collective-permute-start | bytes 1572872 | tf_op jit(solution)/shard_map/ppermute | solution.py:282
  6.2 1.6 %collective-permute-start.1 = (bf16[4,512,128]{2,1,0:T(8,128)(2,1)}, bf16[4,512,128]{2,1,0:T(8,128)(2,1)S(1)}, u32[]{:S(2)}, u32[]{:S(2)}) collective-permute-start(bf16[4,512,128]{2,1,0:T(8,128)(2,1)} %get-tuple-element.26), channel_id=1, source_target_pairs={{0,8},{4,28},{8,16},{12,4},{16,24},{20,12},{24,0},{28,20},{1,9},{5... | collective-permute-start | bytes 1572872 | tf_op jit(solution)/shard_map/ppermute | solution.py:294
  7.8 2.6 %collective-permute-start.3 = (bf16[3,512,128]{2,1,0:T(8,128)(2,1)}, bf16[3,512,128]{2,1,0:T(8,128)(2,1)S(1)}, u32[]{:S(2)}, u32[]{:S(2)}) collective-permute-start(bf16[3,512,128]{2,1,0:T(8,128)(2,1)} %get-tuple-element.25.x1b_ref), channel_id=1, source_target_pairs={{0,4},{4,0},{8,12},{12,8},{16,20},{20,16},{24,28},{28,24},{1,5},{5... | collective-permute-start | bytes 1179656 | tf_op jit(solution)/shard_map/ppermute | solution.py:282
  10.4 1.0 %copy.11 = bf16[1,896,32]{2,1,0:T(8,128)(2,1)S(1)} copy(bf16[1,896,32]{1,2,0:T(8,128)(2,1)} %param.15) | data formatting | bytes 114688 | tf_op args[6]
  11.4 0.9 %copy.12.x_basis_ref = bf16[512,32]{1,0:T(8,128)(2,1)S(1)} copy(bf16[512,32]{0,1:T(8,128)(2,1)} %param.12) | data formatting | bytes 65536 | tf_op args[3]
  12.3 0.7 copy-done
  13.0 2.0 %copy-done.1 = bf16[512,3584]{1,0:T(8,128)(2,1)S(1)} copy-done((bf16[512,3584]{1,0:T(8,128)(2,1)S(1)}, bf16[512,3584]{1,0:T(8,128)(2,1)}, u32[]{:S(2)}) %copy-start.1) | copy-done | bytes 3670040
  15.0 0.7 copy-done.4
  15.6 0.7 copy-done.5
  17.6 2.2 %shard_map.104 = (bf16[7,512,512]{2,1,0:T(8,128)(2,1)S(1)}, f32[7,512,128]{2,1,0:T(8,128)S(1)}, bf16[192,512]{1,0:T(8,128)(2,1)S(1)}, bf16[7,128,192]{2,1,0:T(8,128)(2,1)S(1)}, f32[7,8,128]{2,1,0:T(8,128)S(1)}) custom-call(s32[8,56]{1,0:T(8,128)S(1)} %copy-done, s32[8]{0:T(128)S(1)} %copy-done.4, s32[8]{0:T(128)S(1)} %copy-done.5, s32[1,14]{1,0:T(1,128)S(1)} %copy-done.6, ...), custom_call_target="tpu_custom_call" | custom-call | flops 12000000000 | bytes 9836464 | tf_op jit(solution)/shard_map/pallas_call | solution.py:312
  19.8 0.7 %shard_map.106.before_ref = f32[7,512,128]{2,1,0:T(8,128)S(1)} custom-call(bf16[7,512,512]{2,1,0:T(8,128)(2,1)S(1)} %get-tuple-element.22.squares_ref, f32[7,512,128]{2,1,0:T(8,128)S(1)} %get-tuple-element.23.before_ref, bf16[4,512,128]{2,1,0:T(8,128)(2,1)S(1)} %copy-done.2, bf16[3,512,128]{2,1,0:T(8,128)(2,1)S(1)} %copy-done.3), custom_call_target="tpu_custom_call" | custom-call | flops 4000000000 | bytes 8257536 | tf_op jit(solution)/shard_map/pallas_call | solution.py:312
  20.6 0.8 %collective-permute-start.2 = (bf16[4,512,128]{2,1,0:T(8,128)(2,1)S(1)}, bf16[4,512,128]{2,1,0:T(8,128)(2,1)S(1)}, u32[]{:S(2)}, u32[]{:S(2)}) collective-permute-start(bf16[4,512,128]{2,1,0:T(8,128)(2,1)S(1)} %collective-permute-done.refs_0_), channel_id=1, source_target_pairs={{0,8},{4,28},{8,16},{12,4},{16,24},{20,12},{24,0},{28,20},{1,9},{5... | collective-permute-start | bytes 1572872 | tf_op jit(solution)/shard_map/ppermute | solution.py:294
  21.7 3.2 %collective-permute-start.5 = (bf16[4,512,128]{2,1,0:T(8,128)(2,1)S(1)}, bf16[4,512,128]{2,1,0:T(8,128)(2,1)S(1)}, u32[]{:S(2)}, u32[]{:S(2)}) collective-permute-start(bf16[4,512,128]{2,1,0:T(8,128)(2,1)S(1)} %collective-permute-done.1.refs_1_), channel_id=1, source_target_pairs={{0,4},{4,0},{8,12},{12,8},{16,20},{20,16},{24,28},{28,24},{1,5},{5... | collective-permute-start | bytes 1572872 | tf_op jit(solution)/shard_map/ppermute | solution.py:282
  24.9 2.8 %collective-permute-done.3.refs_3_ = bf16[3,512,128]{2,1,0:T(8,128)(2,1)S(1)} collective-permute-done((bf16[3,512,128]{2,1,0:T(8,128)(2,1)}, bf16[3,512,128]{2,1,0:T(8,128)(2,1)S(1)}, u32[]{:S(2)}, u32[]{:S(2)}) %collective-permute-start.3) | collective-permute-done | bytes 393248 | tf_op jit(solution)/shard_map/ppermute | solution.py:282
  27.7 2.2 %collective-permute-start.4 = (bf16[2,512,128]{2,1,0:T(8,128)(2,1)S(1)}, bf16[2,512,128]{2,1,0:T(8,128)(2,1)S(1)}, u32[]{:S(2)}, u32[]{:S(2)}) collective-permute-start(bf16[2,512,128]{2,1,0:T(8,128)(2,1)S(1)} %slice.8), channel_id=1, source_target_pairs={{0,8},{4,28},{8,16},{12,4},{16,24},{20,12},{24,0},{28,20},{1,9},{5... | collective-permute-start | bytes 786440 | tf_op jit(solution)/shard_map/ppermute | solution.py:294
  29.9 1.6 %collective-permute-start.6 = (bf16[1,512,128]{2,1,0:T(8,128)(2,1)S(1)}, bf16[1,512,128]{2,1,0:T(8,128)(2,1)S(1)}, u32[]{:S(2)}, u32[]{:S(2)}) collective-permute-start(bf16[1,512,128]{2,1,0:T(8,128)(2,1)S(1)} %copy-done.8), channel_id=1, source_target_pairs={{0,8},{4,28},{8,16},{12,4},{16,24},{20,12},{24,0},{28,20},{1,9},{5... | collective-permute-start | bytes 393224 | tf_op jit(solution)/shard_map/ppermute | solution.py:294
  31.4 5.9 %collective-permute-done.2.refs_0_ = bf16[4,512,128]{2,1,0:T(8,128)(2,1)S(1)} collective-permute-done((bf16[4,512,128]{2,1,0:T(8,128)(2,1)S(1)}, bf16[4,512,128]{2,1,0:T(8,128)(2,1)S(1)}, u32[]{:S(2)}, u32[]{:S(2)}) %collective-permute-start.2) | collective-permute-done | bytes 524320 | tf_op jit(solution)/shard_map/ppermute | solution.py:294
  37.3 0.8 %collective-permute-done.5.refs_1_ = bf16[4,512,128]{2,1,0:T(8,128)(2,1)S(1)} collective-permute-done((bf16[4,512,128]{2,1,0:T(8,128)(2,1)S(1)}, bf16[4,512,128]{2,1,0:T(8,128)(2,1)S(1)}, u32[]{:S(2)}, u32[]{:S(2)}) %collective-permute-start.5) | collective-permute-done | bytes 524320 | tf_op jit(solution)/shard_map/ppermute | solution.py:282
  38.0 1.7 %collective-permute-start.8 = (bf16[4,512,128]{2,1,0:T(8,128)(2,1)S(1)}, bf16[4,512,128]{2,1,0:T(8,128)(2,1)S(1)}, u32[]{:S(2)}, u32[]{:S(2)}) collective-permute-start(bf16[4,512,128]{2,1,0:T(8,128)(2,1)S(1)} %collective-permute-done.2.refs_0_), channel_id=1, source_target_pairs={{0,4},{4,0},{8,12},{12,8},{16,20},{20,16},{24,28},{28,24},{1,5},{5... | collective-permute-start | bytes 1572872 | tf_op jit(solution)/shard_map/ppermute | solution.py:282
  39.8 1.6 %collective-permute-start.7 = (bf16[4,512,128]{2,1,0:T(8,128)(2,1)S(1)}, bf16[4,512,128]{2,1,0:T(8,128)(2,1)S(1)}, u32[]{:S(2)}, u32[]{:S(2)}) collective-permute-start(bf16[4,512,128]{2,1,0:T(8,128)(2,1)S(1)} %collective-permute-done.2.refs_0_), channel_id=1, source_target_pairs={{0,8},{4,28},{8,16},{12,4},{16,24},{20,12},{24,0},{28,20},{1,9},{5... | collective-permute-start | bytes 1572872 | tf_op jit(solution)/shard_map/ppermute | solution.py:294
  41.4 0.7 %shard_map.107.before_ref = f32[7,512,128]{2,1,0:T(8,128)S(1)} custom-call(bf16[7,512,512]{2,1,0:T(8,128)(2,1)S(1)} %get-tuple-element.22.squares_ref, f32[7,512,128]{2,1,0:T(8,128)S(1)} %shard_map.106.before_ref, bf16[4,512,128]{2,1,0:T(8,128)(2,1)S(1)} %collective-permute-done.refs_0_, bf16[4,512,128]{2,1,0:T(8,128)(2,1)S(1)} %collective-permute-done.1.refs_1_), custom_call_target="tpu_custom_call" | custom-call | flops 1000000000 | bytes 8388608 | tf_op jit(solution)/shard_map/pallas_call | solution.py:312
  42.3 2.4 %collective-permute-start.9 = (bf16[1,512,128]{2,1,0:T(8,128)(2,1)S(1)}, bf16[1,512,128]{2,1,0:T(8,128)(2,1)S(1)}, u32[]{:S(2)}, u32[]{:S(2)}) collective-permute-start(bf16[1,512,128]{2,1,0:T(8,128)(2,1)S(1)} %slice.9), channel_id=1, source_target_pairs={{0,4},{4,0},{8,12},{12,8},{16,20},{20,16},{24,28},{28,24},{1,5},{5... | collective-permute-start | bytes 393224 | tf_op jit(solution)/shard_map/ppermute | solution.py:282
  45.2 1.0 %shard_map.109.before_ref = f32[7,512,128]{2,1,0:T(8,128)S(1)} custom-call(bf16[7,512,512]{2,1,0:T(8,128)(2,1)S(1)} %get-tuple-element.22.squares_ref, f32[7,512,128]{2,1,0:T(8,128)S(1)} %shard_map.108.before_ref, bf16[2,512,128]{2,1,0:T(8,128)(2,1)S(1)} %collective-permute-done.4.refs_0_, bf16[4,512,128]{2,1,0:T(8,128)(2,1)S(1)} %collective-permute-done.5.refs_1_, ...), custom_call_target="tpu_custom_call" | custom-call | flops 5000000000 | bytes 8650752 | tf_op jit(solution)/shard_map/pallas_call | solution.py:312
  46.2 8.7 %collective-permute-done.7.refs_0_ = bf16[4,512,128]{2,1,0:T(8,128)(2,1)S(1)} collective-permute-done((bf16[4,512,128]{2,1,0:T(8,128)(2,1)S(1)}, bf16[4,512,128]{2,1,0:T(8,128)(2,1)S(1)}, u32[]{:S(2)}, u32[]{:S(2)}) %collective-permute-start.7) | collective-permute-done | bytes 524320 | tf_op jit(solution)/shard_map/ppermute | solution.py:294
  55.4 1.4 %shard_map.111 = (bf16[512,896]{1,0:T(8,128)(2,1)S(1)}, f32[128,192]{1,0:T(8,128)S(1)}, f32[32,192]{1,0:T(8,128)S(1)}, f32[32,192]{1,0:T(8,128)S(1)}) custom-call(f32[7,8,128]{2,1,0:T(8,128)S(1)} %get-tuple-element.21.mask_ref, bf16[7,512,512]{2,1,0:T(8,128)(2,1)S(1)} %get-tuple-element.22.squares_ref, f32[7,512,128]{2,1,0:T(8,128)S(1)} %shard_map.110.before_ref, ...), custom_call_target="tpu_custom_call" | custom-call | bytes 7794688 | tf_op jit(solution)/shard_map/pallas_call | solution.py:312
  56.8 3.6 %collective-permute-start.11 = (f32[32,192]{1,0:T(8,128)S(1)}, f32[32,192]{1,0:T(8,128)S(1)}, u32[]{:S(2)}, u32[]{:S(2)}) collective-permute-start(f32[32,192]{1,0:T(8,128)S(1)} %get-tuple-element.36), channel_id=1, source_target_pairs={{0,28},{4,8},{8,4},{12,16},{16,12},{20,24},{24,20},{28,0},{1,29},{... | collective-permute-start | bytes 73736 | tf_op jit(solution)/shard_map/ppermute | solution.py:288
  60.7 2.8 %collective-permute-done.11.got_b_ref = f32[32,192]{1,0:T(8,128)S(1)} collective-permute-done((f32[32,192]{1,0:T(8,128)S(1)}, f32[32,192]{1,0:T(8,128)S(1)}, u32[]{:S(2)}, u32[]{:S(2)}) %collective-permute-start.11) | collective-permute-done | bytes 24608 | tf_op jit(solution)/shard_map/ppermute | solution.py:288
  63.7 1.6 %collective-permute-start.13 = (f32[128,32]{1,0:T(8,128)S(1)}, f32[128,32]{1,0:T(8,128)S(1)}, u32[]{:S(2)}, u32[]{:S(2)}) collective-permute-start(f32[128,32]{1,0:T(8,128)S(1)} %get-tuple-element.39), channel_id=1, source_target_pairs={{0,3},{1,2},{2,1},{3,0},{4,7},{5,6},{6,5},{7,4},{8,11},{9,10},{10,... | collective-permute-start | bytes 49160 | tf_op jit(solution)/shard_map/ppermute | solution.py:288
  65.4 1.1 %shard_map.112 = bf16[512,896]{1,0:T(8,128)(2,1)} custom-call(bf16[512,896]{1,0:T(8,128)(2,1)S(1)} %get-tuple-element.33.own_ref), custom_call_target="tpu_custom_call" | custom-call | bytes 1835008 | tf_op jit(solution)/shard_map/pallas_call | solution.py:312
  66.5 1.2 %collective-permute-done.13.got_b_ref = f32[128,32]{1,0:T(8,128)S(1)} collective-permute-done((f32[128,32]{1,0:T(8,128)S(1)}, f32[128,32]{1,0:T(8,128)S(1)}, u32[]{:S(2)}, u32[]{:S(2)}) %collective-permute-start.13) | collective-permute-done | bytes 16416 | tf_op jit(solution)/shard_map/ppermute | solution.py:288
  67.6 0.7 %shard_map.114 = f32[128,128]{1,0:T(8,128)} custom-call(f32[128,128]{1,0:T(8,128)S(1)} %get-tuple-element.37.center_ref, f32[128,32]{1,0:T(8,128)S(1)} %collective-permute-done.12.got_a_ref, f32[128,32]{1,0:T(8,128)S(1)} %collective-permute-done.13.got_b_ref), custom_call_target="tpu_custom_call" | custom-call | bytes 163840 | tf_op jit(solution)/shard_map/pallas_call | solution.py:312
  (29 shorter events, 3.4 us)
Async XLA Ops:
  3.2 17.3 %collective-permute-start = (bf16[4,512,128]{2,1,0:T(8,128)(2,1)}, bf16[4,512,128]{2,1,0:T(8,128)(2,1)S(1)}, u32[]{:S(2)}, u32[]{:S(2)}) collective-permute-start(bf16[4,512,128]{2,1,0:T(8,128)(2,1)} %get-tuple-element.24.x1a_ref), channel_id=1, source_target_pairs={{0,4},{4,0},{8,12},{12,8},{16,20},{20,16},{24,28},{28,24},{1,5},{5... | collective-permute-start | bytes 1572872 | tf_op jit(solution)/shard_map/ppermute | solution.py:282
  6.2 15.5 %collective-permute-start.1 = (bf16[4,512,128]{2,1,0:T(8,128)(2,1)}, bf16[4,512,128]{2,1,0:T(8,128)(2,1)S(1)}, u32[]{:S(2)}, u32[]{:S(2)}) collective-permute-start(bf16[4,512,128]{2,1,0:T(8,128)(2,1)} %get-tuple-element.26), channel_id=1, source_target_pairs={{0,8},{4,28},{8,16},{12,4},{16,24},{20,12},{24,0},{28,20},{1,9},{5... | collective-permute-start | bytes 1572872 | tf_op jit(solution)/shard_map/ppermute | solution.py:294
  7.8 19.8 %collective-permute-start.3 = (bf16[3,512,128]{2,1,0:T(8,128)(2,1)}, bf16[3,512,128]{2,1,0:T(8,128)(2,1)S(1)}, u32[]{:S(2)}, u32[]{:S(2)}) collective-permute-start(bf16[3,512,128]{2,1,0:T(8,128)(2,1)} %get-tuple-element.25.x1b_ref), channel_id=1, source_target_pairs={{0,4},{4,0},{8,12},{12,8},{16,20},{20,16},{24,28},{28,24},{1,5},{5... | collective-permute-start | bytes 1179656 | tf_op jit(solution)/shard_map/ppermute | solution.py:282
  12.3 0.7 %copy-start = (s32[8,56]{1,0:T(8,128)S(1)}, s32[8,56]{1,0:T(8,128)}, u32[]{:S(2)}) copy-start(s32[8,56]{1,0:T(8,128)} %pattern_hbm.1) | copy-start | bytes 5380
  12.9 2.0 %copy-start.1 = (bf16[512,3584]{1,0:T(8,128)(2,1)S(1)}, bf16[512,3584]{1,0:T(8,128)(2,1)}, u32[]{:S(2)}) copy-start(bf16[512,3584]{1,0:T(8,128)(2,1)} %p2_ref.1) | copy-start | bytes 11010052
  15.0 0.7 copy-start.4
  15.6 0.7 copy-start.5
  16.3 0.7 copy-start.6
  17.0 0.7 copy-start.7
  17.6 2.2 %copy-start.2 = (bf16[4,512,128]{2,1,0:T(8,128)(2,1)S(1)}, bf16[4,512,128]{2,1,0:T(8,128)(2,1)}, u32[]{:S(2)}) copy-start(bf16[4,512,128]{2,1,0:T(8,128)(2,1)} %get-tuple-element.24.x1a_ref) | copy-start | bytes 1572868
  17.6 2.2 %copy-start.3 = (bf16[3,512,128]{2,1,0:T(8,128)(2,1)S(1)}, bf16[3,512,128]{2,1,0:T(8,128)(2,1)}, u32[]{:S(2)}) copy-start(bf16[3,512,128]{2,1,0:T(8,128)(2,1)} %get-tuple-element.25.x1b_ref) | copy-start | bytes 1179652
  19.8 10.0 %copy-start.8 = (bf16[1,512,128]{2,1,0:T(8,128)(2,1)S(1)}, bf16[1,512,128]{2,1,0:T(8,128)(2,1)}, u32[]{:S(2)}) copy-start(bf16[1,512,128]{2,1,0:T(8,128)(2,1)} %get-tuple-element.29) | copy-start | bytes 393220
  20.6 16.7 %collective-permute-start.2 = (bf16[4,512,128]{2,1,0:T(8,128)(2,1)S(1)}, bf16[4,512,128]{2,1,0:T(8,128)(2,1)S(1)}, u32[]{:S(2)}, u32[]{:S(2)}) collective-permute-start(bf16[4,512,128]{2,1,0:T(8,128)(2,1)S(1)} %collective-permute-done.refs_0_), channel_id=1, source_target_pairs={{0,8},{4,28},{8,16},{12,4},{16,24},{20,12},{24,0},{28,20},{1,9},{5... | collective-permute-start | bytes 1572872 | tf_op jit(solution)/shard_map/ppermute | solution.py:294
  21.7 16.3 %collective-permute-start.5 = (bf16[4,512,128]{2,1,0:T(8,128)(2,1)S(1)}, bf16[4,512,128]{2,1,0:T(8,128)(2,1)S(1)}, u32[]{:S(2)}, u32[]{:S(2)}) collective-permute-start(bf16[4,512,128]{2,1,0:T(8,128)(2,1)S(1)} %collective-permute-done.1.refs_1_), channel_id=1, source_target_pairs={{0,4},{4,0},{8,12},{12,8},{16,20},{20,16},{24,28},{28,24},{1,5},{5... | collective-permute-start | bytes 1572872 | tf_op jit(solution)/shard_map/ppermute | solution.py:282
  27.7 14.6 %collective-permute-start.4 = (bf16[2,512,128]{2,1,0:T(8,128)(2,1)S(1)}, bf16[2,512,128]{2,1,0:T(8,128)(2,1)S(1)}, u32[]{:S(2)}, u32[]{:S(2)}) collective-permute-start(bf16[2,512,128]{2,1,0:T(8,128)(2,1)S(1)} %slice.8), channel_id=1, source_target_pairs={{0,8},{4,28},{8,16},{12,4},{16,24},{20,12},{24,0},{28,20},{1,9},{5... | collective-permute-start | bytes 786440 | tf_op jit(solution)/shard_map/ppermute | solution.py:294
  29.9 15.3 %collective-permute-start.6 = (bf16[1,512,128]{2,1,0:T(8,128)(2,1)S(1)}, bf16[1,512,128]{2,1,0:T(8,128)(2,1)S(1)}, u32[]{:S(2)}, u32[]{:S(2)}) collective-permute-start(bf16[1,512,128]{2,1,0:T(8,128)(2,1)S(1)} %copy-done.8), channel_id=1, source_target_pairs={{0,8},{4,28},{8,16},{12,4},{16,24},{20,12},{24,0},{28,20},{1,9},{5... | collective-permute-start | bytes 393224 | tf_op jit(solution)/shard_map/ppermute | solution.py:294
  38.0 17.3 %collective-permute-start.8 = (bf16[4,512,128]{2,1,0:T(8,128)(2,1)S(1)}, bf16[4,512,128]{2,1,0:T(8,128)(2,1)S(1)}, u32[]{:S(2)}, u32[]{:S(2)}) collective-permute-start(bf16[4,512,128]{2,1,0:T(8,128)(2,1)S(1)} %collective-permute-done.2.refs_0_), channel_id=1, source_target_pairs={{0,4},{4,0},{8,12},{12,8},{16,20},{20,16},{24,28},{28,24},{1,5},{5... | collective-permute-start | bytes 1572872 | tf_op jit(solution)/shard_map/ppermute | solution.py:282
  39.8 15.1 %collective-permute-start.7 = (bf16[4,512,128]{2,1,0:T(8,128)(2,1)S(1)}, bf16[4,512,128]{2,1,0:T(8,128)(2,1)S(1)}, u32[]{:S(2)}, u32[]{:S(2)}) collective-permute-start(bf16[4,512,128]{2,1,0:T(8,128)(2,1)S(1)} %collective-permute-done.2.refs_0_), channel_id=1, source_target_pairs={{0,8},{4,28},{8,16},{12,4},{16,24},{20,12},{24,0},{28,20},{1,9},{5... | collective-permute-start | bytes 1572872 | tf_op jit(solution)/shard_map/ppermute | solution.py:294
  42.3 13.1 %collective-permute-start.9 = (bf16[1,512,128]{2,1,0:T(8,128)(2,1)S(1)}, bf16[1,512,128]{2,1,0:T(8,128)(2,1)S(1)}, u32[]{:S(2)}, u32[]{:S(2)}) collective-permute-start(bf16[1,512,128]{2,1,0:T(8,128)(2,1)S(1)} %slice.9), channel_id=1, source_target_pairs={{0,4},{4,0},{8,12},{12,8},{16,20},{20,16},{24,28},{28,24},{1,5},{5... | collective-permute-start | bytes 393224 | tf_op jit(solution)/shard_map/ppermute | solution.py:282
  56.8 4.0 %collective-permute-start.10 = (f32[32,192]{1,0:T(8,128)S(1)}, f32[32,192]{1,0:T(8,128)S(1)}, u32[]{:S(2)}, u32[]{:S(2)}) collective-permute-start(f32[32,192]{1,0:T(8,128)S(1)} %get-tuple-element.35), channel_id=1, source_target_pairs={{0,4},{4,0},{8,12},{12,8},{16,20},{20,16},{24,28},{28,24},{1,5},{5... | collective-permute-start | bytes 73736 | tf_op jit(solution)/shard_map/ppermute | solution.py:282
  56.8 6.7 %collective-permute-start.11 = (f32[32,192]{1,0:T(8,128)S(1)}, f32[32,192]{1,0:T(8,128)S(1)}, u32[]{:S(2)}, u32[]{:S(2)}) collective-permute-start(f32[32,192]{1,0:T(8,128)S(1)} %get-tuple-element.36), channel_id=1, source_target_pairs={{0,28},{4,8},{8,4},{12,16},{16,12},{20,24},{24,20},{28,0},{1,29},{... | collective-permute-start | bytes 73736 | tf_op jit(solution)/shard_map/ppermute | solution.py:288
  63.7 2.8 %collective-permute-start.12 = (f32[128,32]{1,0:T(8,128)S(1)}, f32[128,32]{1,0:T(8,128)S(1)}, u32[]{:S(2)}, u32[]{:S(2)}) collective-permute-start(f32[128,32]{1,0:T(8,128)S(1)} %get-tuple-element.38), channel_id=1, source_target_pairs={{0,1},{1,0},{2,3},{3,2},{4,5},{5,4},{6,7},{7,6},{8,9},{9,8},{10,11... | collective-permute-start | bytes 49160 | tf_op jit(solution)/shard_map/ppermute | solution.py:282
  63.7 3.9 %collective-permute-start.13 = (f32[128,32]{1,0:T(8,128)S(1)}, f32[128,32]{1,0:T(8,128)S(1)}, u32[]{:S(2)}, u32[]{:S(2)}) collective-permute-start(f32[128,32]{1,0:T(8,128)S(1)} %get-tuple-element.39), channel_id=1, source_target_pairs={{0,3},{1,2},{2,1},{3,0},{4,7},{5,6},{6,5},{7,4},{8,11},{9,10},{10,... | collective-permute-start | bytes 49160 | tf_op jit(solution)/shard_map/ppermute | solution.py:288

commit v4 on v2

v4 whole, which is shorter than its diff:
```python
import functools

import jax
import jax.numpy as jnp
from jax import lax
from jax.experimental import pallas as pl
from jax.experimental.pallas import tpu as pltpu
from jax.sharding import PartitionSpec as P

HD = 3
SX = 128
SY = 128
M = 32
EX = SX + 2 * M
EY = SY + 2 * M
CHUNKS = 2 * HD + 1
NEAR = HD + 1
AHEAD = HD + 2
VMEM = pl.BlockSpec(memory_space=pltpu.VMEM)
SMEM = pl.BlockSpec(memory_space=pltpu.SMEM)
HBM = pl.BlockSpec(memory_space=pltpu.HBM)
F32 = jnp.float32
BF16 = jnp.bfloat16


class Dims:
    def __init__(self, pattern, x_basis, n_col):
        self.br, self.win = pattern.shape
        self.bs = x_basis.shape[0] // self.br
        self.n_col = n_col
        self.wc = self.win // n_col
        self.stride = self.br // n_col
        self.uw = self.stride * self.bs
        self.rows = self.br * self.bs


def block_mask(pattern_ref, block_row, slots, bs, dtype):
    lane = lax.broadcasted_iota(jnp.int32, (1, bs * len(slots)), 1)
    row = jnp.zeros((1, bs * len(slots)), jnp.int32)
    for place, slot in enumerate(slots):
        inside = (lane >= place * bs) & (lane < (place + 1) * bs)
        row = jnp.where(inside, pattern_ref[block_row, slot], row)
    return row.astype(F32).astype(dtype)


def own_slots(dims, chunk, column):
    return [dims.n_col * (chunk * dims.stride + s) + column for s in range(dims.stride)]


def mask_kernel(
    dims,
    pattern_hbm,
    density_hbm,
    x1a_ref,
    x1b_ref,
    *refs,
):
    z1_refs, refs = refs[:-8], refs[-8:]
    pattern_ref, tile_ref, kept_ref, pattern_sem, tile_sems, x1a_sem, x1b_sem, z1_sem = refs
    odd = lax.axis_index("row") % 2
    column = lax.axis_index("col")
    bs, uw = dims.bs, dims.uw
    wide = tile_ref.shape[2]
    fetch_pattern = pltpu.make_async_copy(pattern_hbm, pattern_ref, pattern_sem)
    fetch_pattern.start()
    fetches = []
    for part in range(tile_ref.shape[0]):
        cols = pl.ds(part * wide, wide)
        fetch = pltpu.make_async_copy(density_hbm.at[:, cols], tile_ref.at[part], tile_sems.at[part])
        fetch.start()
        fetches.append(fetch)
    fetch_pattern.wait()
    near, first = x1a_ref.shape[0], z1_refs[0].shape[0]

    def copies_of(chunk, lane_odd):
        own = chunk if lane_odd else CHUNKS - 1 - chunk
        sent = CHUNKS - 1 - own
        tile = kept_ref.at[chunk]
        found = [
            pltpu.make_async_copy(tile, x1a_ref.at[sent], x1a_sem.at[sent])
            if sent < near
            else pltpu.make_async_copy(tile, x1b_ref.at[sent - near], x1b_sem.at[sent - near])
        ]
        if own < 5:
            dest = z1_refs[0].at[own] if own < first else z1_refs[1].at[own - first]
            found.append(pltpu.make_async_copy(tile, dest, z1_sem.at[own]))
        return found

    arrived = 0
    for chunk in range(CHUNKS):
        part, start = divmod(chunk * uw, wide)
        if part == arrived:
            fetches[part].wait()
            arrived += 1
        for i in range(dims.br):
            rows = slice(i * bs, (i + 1) * bs)
            mask = block_mask(pattern_ref, i, own_slots(dims, chunk, column), bs, BF16)
            kept_ref[chunk, rows, :] = tile_ref[part, rows, start : start + uw] * mask
        for lane_odd in (0, 1):

            @pl.when(odd == lane_odd)
            def _():
                for copy in copies_of(chunk, lane_odd):
                    copy.start()

    for lane_odd in (0, 1):

        @pl.when(odd == lane_odd)
        def _():
            for chunk in range(CHUNKS):
                for copy in copies_of(chunk, lane_odd):
                    copy.wait()


def own_block_cols(dims, p2_ref, slot, column):
    pair = pl.multiple_of((dims.n_col * slot // 2 + column // 2) * 2 * dims.bs, 2 * dims.bs)
    wide = p2_ref[:, pl.ds(pair, 2 * dims.bs)].astype(F32)
    return jnp.where(column % 2 == 1, wide[:, dims.bs :], wide[:, : dims.bs])


def spread_kernel(dims, *refs):
    inputs, refs = refs[:7], refs[7:]
    xt_ref, y_ref, mask_ref, wide_ref = refs[:4]
    held, sems = refs[4:11], refs[11]
    copies = [
        pltpu.make_async_copy(source, dest, sems.at[at])
        for at, (source, dest) in enumerate(zip(inputs, held))
    ]
    for copy in copies:
        copy.start()
    for copy in copies:
        copy.wait()
    pattern_ref, x_offset_ref, x_extent_ref, y_offset_ref, y_extent_ref, x_basis_ref, y_basis_ref = held
    odd = lax.axis_index("row") % 2
    column = lax.axis_index("col")
    bs, br = dims.bs, dims.br
    width = br * bs
    for i in range(br):
        for block in range(CHUNKS):
            slots = [block * br + t for t in range(br)]
            mask = block_mask(pattern_ref, i, slots, bs, F32)
            wide_ref[i : i + 1, block * width : (block + 1) * width] = mask
    tx = y_basis_ref.shape[0]
    step = lax.broadcasted_iota(jnp.int32, (tx, EY), 0)
    cell = lax.broadcasted_iota(jnp.int32, (tx, EY), 1)
    for chunk in range(CHUNKS):
        place = jnp.where(odd == 1, chunk, CHUNKS - 1 - chunk)
        for i in range(br):
            slots = own_slots(dims, chunk, column)
            mask_ref[place, i : i + 1, :] = 2.0 * block_mask(pattern_ref, i, slots, bs, F32)
        for s in range(dims.stride):
            m = chunk * dims.stride + s
            hit = (cell == y_offset_ref[0, m] + step) & (step < y_extent_ref[0, m])
            spread = lax.dot_general(
                y_basis_ref[:, m * bs : (m + 1) * bs],
                hit.astype(F32).astype(BF16),
                (((0,), (0,)), ((), ())),
                preferred_element_type=F32,
            )
            y_ref[place, s * bs : (s + 1) * bs, :] = spread.astype(BF16)
    step = lax.broadcasted_iota(jnp.int32, (EX, tx), 1)
    cell = lax.broadcasted_iota(jnp.int32, (EX, tx), 0)
    for i in range(br):
        hit = (cell == x_offset_ref[i] + step) & (step < x_extent_ref[i])
        spread = jnp.dot(
            hit.astype(F32).astype(BF16),
            x_basis_ref[:, i * bs : (i + 1) * bs],
            preferred_element_type=F32,
        )
        xt_ref[:, i * bs : (i + 1) * bs] = spread.astype(BF16)


def square_kernel(dims, p2_ref, wide_ref, *refs):
    squares_ref, summed_ref = refs[3:5]
    for source, dest in zip(refs[:3], refs[5:]):
        dest[...] = source[...]
    odd = lax.axis_index("row") % 2
    column = lax.axis_index("col")
    bs, br = dims.bs, dims.br
    width = br * bs
    for block in range(CHUNKS):
        place = jnp.where(odd == 1, block, CHUNKS - 1 - block)
        cols = slice(block * width, (block + 1) * width)
        for i in range(br):
            rows = slice(i * bs, (i + 1) * bs)
            squares_ref[place, rows, :] = p2_ref[rows, cols] * wide_ref[i : i + 1, cols].astype(BF16)
    for chunk in range(CHUNKS):
        place = jnp.where(odd == 1, chunk, CHUNKS - 1 - chunk)
        parts = [
            own_block_cols(dims, p2_ref, chunk * dims.stride + s, column)
            for s in range(dims.stride)
        ]
        own = parts[0] if len(parts) == 1 else jnp.concatenate(parts, axis=1)
        summed_ref[place] = 1.5 * own


def paired(terms):
    return [terms[at : at + 2] for at in range(0, len(terms), 2)]


def add_products(square, terms, summed_ref):
    for group in paired(terms):
        tiles = [tile[...] for _, tile in group]
        wide = tiles[0] if len(tiles) == 1 else jnp.concatenate(tiles, axis=1)
        product = jnp.dot(square, wide, preferred_element_type=F32)
        uw = tiles[0].shape[1]
        for at, (place, _) in enumerate(group):
            summed_ref[place] -= product[:, at * uw : (at + 1) * uw]


def first_kernel(squares_ref, before_ref, x1a_ref, x1b_ref, summed_ref):
    summed_ref[...] = before_ref[...]
    own = lambda j: x1a_ref.at[j] if j < NEAR else x1b_ref.at[j - NEAR]
    add_products(
        squares_ref[HD], [(k, own(CHUNKS - 1 - k)) for k in range(CHUNKS)], summed_ref
    )


def stage_kernel(terms, squares_ref, before_ref, *refs):
    summed_ref = refs[-1]
    summed_ref[...] = before_ref[...]
    for distance, pairs in terms:
        add_products(
            squares_ref[HD + distance],
            [(place, refs[which].at[at]) for place, which, at in pairs],
            summed_ref,
        )


def last_kernel(dims, mask_ref, squares_ref, before_ref, x2p_ref, x2q_ref, z3_ref, z1b_ref, *refs):
    xt_ref, y_ref, new_ref, middle_ref, rim_a_ref, rim_b_ref = refs
    odd = lax.axis_index("row") % 2
    bs, uw = dims.bs, dims.uw

    def product(distance, *tiles):
        wide = tiles[0] if len(tiles) == 1 else jnp.concatenate(tiles, axis=1)
        return jnp.dot(squares_ref[HD + distance], wide, preferred_element_type=F32)

    def finish(k, total):
        for i in range(dims.br):
            rows = slice(i * bs, (i + 1) * bs)
            kept = total[rows] * mask_ref[k, i : i + 1, :]
            new_ref[rows, k * uw : (k + 1) * uw] = kept.astype(BF16)

    x2 = [x2p_ref[j] for j in range(NEAR)] + [x2q_ref[0]]
    low = product(-2, x2[4], x2[3])
    mid = product(-2, x2[1], x2[0]) + product(3, z3_ref[0], z3_ref[1])
    high = product(3, z3_ref[2], z3_ref[3])
    finish(0, before_ref[0] - low[:, :uw])
    finish(1, before_ref[1] - low[:, uw:])
    finish(2, before_ref[2] - product(-2, x2[2]))
    finish(3, before_ref[3] - mid[:, :uw])
    finish(4, before_ref[4] - mid[:, uw:])
    finish(5, before_ref[5] - high[:, :uw])
    finish(6, before_ref[6] - high[:, uw:] - product(2, z1b_ref[0]))
    half = jnp.dot(
        new_ref[...], y_ref[...].reshape(CHUNKS * uw, EY), preferred_element_type=F32
    )
    extended = jnp.dot(xt_ref[...], half.astype(BF16), preferred_element_type=F32)
    middle_ref[...] = extended[M : M + SX]
    lower, upper = extended[:M], extended[SX + M :]
    rim_a_ref[...] = jnp.where(odd == 1, lower, upper)
    rim_b_ref[...] = jnp.where(odd == 1, upper, lower)


def order_kernel(dims, own_ref, new_ref):
    odd = lax.axis_index("row") % 2
    uw = dims.uw

    @pl.when(odd == 1)
    def _():
        new_ref[...] = own_ref[...]

    @pl.when(odd == 0)
    def _():
        for k in range(CHUNKS):
            at = CHUNKS - 1 - k
            new_ref[:, at * uw : (at + 1) * uw] = own_ref[:, k * uw : (k + 1) * uw]


def row_rims_kernel(middle_ref, got_a_ref, got_b_ref, center_ref, rim_a_ref, rim_b_ref):
    odd = lax.axis_index("row") % 2
    col_odd = lax.axis_index("col") % 2
    got_a, got_b = got_a_ref[...], got_b_ref[...]
    low = jnp.where(odd == 1, got_a, got_b)
    high = jnp.where(odd == 1, got_b, got_a)
    interior = jnp.concatenate(
        [middle_ref[:M] + low, middle_ref[M : SX - M], middle_ref[SX - M :] + high], axis=0
    )
    center_ref[...] = interior[:, M : M + SY]
    lower, upper = interior[:, :M], interior[:, SY + M :]
    rim_a_ref[...] = jnp.where(col_odd == 1, lower, upper)
    rim_b_ref[...] = jnp.where(col_odd == 1, upper, lower)


def col_rims_kernel(center_ref, got_a_ref, got_b_ref, grid_ref):
    col_odd = lax.axis_index("col") % 2
    got_a, got_b = got_a_ref[...], got_b_ref[...]
    low = jnp.where(col_odd == 1, got_a, got_b)
    high = jnp.where(col_odd == 1, got_b, got_a)
    none = jnp.zeros((SX, SY - 2 * M), F32)
    grid_ref[...] = center_ref[...] + jnp.concatenate([low, none, high], axis=1)


def swap_partner(value, axis):
    count = lax.axis_size(axis)
    return lax.ppermute(value, axis, [(s, s ^ 1) for s in range(count)])


def swap_other(value, axis):
    count = lax.axis_size(axis)
    pairs = [(s, (s - 1) % count if s % 2 == 0 else (s + 1) % count) for s in range(count)]
    return lax.ppermute(value, axis, pairs)


def shift_level(value):
    count = lax.axis_size("row")
    pairs = [(s, (s + 2) % count if s % 2 == 0 else (s - 2) % count) for s in range(count)]
    return lax.ppermute(value, "row", pairs)


def after(value, *others):
    return lax.optimization_barrier((value,) + others)[0]


def call(kernel, outs, ins, scratch=(), beside=0, stay=(), outs_stay=False, limit=24):
    shapes = [jax.ShapeDtypeStruct(shape, dtype) for shape, dtype in outs]
    specs = [
        HBM
        if at in stay
        else SMEM
        if jnp.issubdtype(value.dtype, jnp.integer)
        else VMEM
        for at, value in enumerate(ins)
    ]
    moved = sum(value.size * value.dtype.itemsize for value in list(ins) + shapes)
    return pl.pallas_call(
        kernel,
        out_shape=shapes,
        in_specs=specs,
        out_specs=[HBM if outs_stay else VMEM] * len(shapes),
        scratch_shapes=list(scratch),
        compiler_params=pltpu.CompilerParams(vmem_limit_bytes=limit * 2**20),
        cost_estimate=pl.CostEstimate(
            flops=beside * 10**9, bytes_accessed=moved, transcendentals=0
        ),
    )(*ins)


def shards(p2_panel, density, pattern, x_basis, x_offset, x_extent, y_basis, y_offset, y_extent):
    dims = Dims(pattern, x_basis, lax.axis_size("col"))
    rows, uw = dims.rows, dims.uw
    chunks = lambda count: ((count, rows, uw), BF16)
    total = ((CHUNKS, rows, uw), F32)

    parts = CHUNKS if uw % 128 == 0 else 1
    own_p, own_q, own_z, own_zb = call(
        functools.partial(mask_kernel, dims),
        [chunks(NEAR), chunks(CHUNKS - NEAR), chunks(NEAR), chunks(AHEAD - NEAR)],
        [pattern, density],
        scratch=[
            pltpu.SMEM(pattern.shape, jnp.int32),
            pltpu.VMEM((parts, rows, CHUNKS * uw // parts), BF16),
            pltpu.VMEM((CHUNKS, rows, uw), BF16),
            pltpu.SemaphoreType.DMA(()),
            pltpu.SemaphoreType.DMA((parts,)),
            pltpu.SemaphoreType.DMA((NEAR,)),
            pltpu.SemaphoreType.DMA((CHUNKS - NEAR,)),
            pltpu.SemaphoreType.DMA((AHEAD,)),
        ],
        stay=(0, 1),
        outs_stay=True,
        limit=60,
    )
    x1p = swap_partner(own_p, "row")
    z1 = shift_level(own_z)
    x1q = swap_partner(own_q, "row")

    small = [pattern, x_offset, x_extent, y_offset, y_extent, x_basis.T, y_basis[0].T]
    xt, y_spread, mask, wide = call(
        functools.partial(spread_kernel, dims),
        [
            ((EX, rows), BF16),
            ((CHUNKS, uw, EY), BF16),
            ((CHUNKS, dims.br, uw), F32),
            ((dims.br, dims.win * dims.bs), F32),
        ],
        small,
        scratch=[
            (pltpu.SMEM if jnp.issubdtype(value.dtype, jnp.integer) else pltpu.VMEM)(
                value.shape, value.dtype
            )
            for value in small
        ]
        + [pltpu.SemaphoreType.DMA((len(small),))],
        stay=range(len(small)),
        limit=60,
        beside=6,
    )
    kept = [xt, y_spread, mask]
    squares, summed, xt, y_spread, mask = call(
        functools.partial(square_kernel, dims),
        [((CHUNKS, rows, rows), BF16), total] + [(value.shape, value.dtype) for value in kept],
        [p2_panel, wide] + kept,
        beside=1,
    )
    ready = summed

    def stage(summed, terms, beside=0):
        tiles = []
        for _, pairs in terms:
            for _, tile, _ in pairs:
                if not any(tile is known for known in tiles):
                    tiles.append(tile)
        spot = lambda tile: next(at for at, known in enumerate(tiles) if known is tile)
        listed = [(d, [(place, spot(tile), at) for place, tile, at in pairs]) for d, pairs in terms]
        return call(
            functools.partial(stage_kernel, listed),
            [total],
            [squares, summed] + tiles,
            beside=beside,
        )[0]

    (summed,) = call(first_kernel, [total], [squares, summed, own_p, own_q])
    z2p = shift_level(after(x1p, ready))
    x3 = swap_partner(z1, "row")
    z2q = shift_level(x1q[: 2 * HD - NEAR])
    z1b = shift_level(after(own_zb, z1))
    partner = [(j - 1, x1p, j) for j in range(1, NEAR)]
    partner += [(j - 1, x1q, j - NEAR) for j in range(NEAR, CHUNKS)]
    summed = stage(
        summed, [(-1, partner), (2, [(j + 2, z1, j) for j in range(NEAR)])], beside=3
    )
    x2p = swap_partner(after(z2p, summed), "row")
    z3 = shift_level(z2p)
    summed = stage(summed, [(1, [(j + 1, z2p, j) for j in range(NEAR)])])
    x2q = swap_partner(after(z2q[: AHEAD - NEAR], z2p), "row")
    summed = stage(
        summed,
        [
            (1, [(j + 1, z2q, j - NEAR) for j in range(NEAR, 2 * HD)]),
            (-3, [(3 - j, x3, j) for j in range(NEAR)]),
        ],
        beside=4,
    )
    new_own, middle, rim_a, rim_b = call(
        functools.partial(last_kernel, dims),
        [
            ((rows, dims.wc * dims.bs), BF16),
            ((SX, EY), F32),
            ((M, EY), F32),
            ((M, EY), F32),
        ],
        [mask, squares, summed, x2p, x2q, z3, z1b, xt, y_spread],
    )
    (new_density,) = call(
        functools.partial(order_kernel, dims), [(new_own.shape, BF16)], [new_own]
    )
    got_a = swap_partner(rim_a, "row")
    got_b = swap_other(rim_b, "row")
    center, rim_a, rim_b = call(
        row_rims_kernel,
        [((SX, SY), F32), ((SX, M), F32), ((SX, M), F32)],
        [middle, got_a, got_b],
    )
    got_a = swap_partner(rim_a, "col")
    got_b = swap_other(rim_b, "col")
    (grid_density,) = call(col_rims_kernel, [((SX, SY), F32)], [center, got_a, got_b])
    return new_density, grid_density


def solution(mesh):
    placed = (
        P("row", None),
        P("row", "col"),
        P("row", None),
        P("row", None),
        P("row"),
        P("row"),
        P("row", "col", None),
        P("row", "col"),
        P("row", "col"),
    )
    return jax.shard_map(
        shards,
        mesh=mesh,
        in_specs=placed,
        out_specs=(P("row", "col"), P("row", "col")),
        check_vma=False,
    )
```

time: 72 us -> 67.1 us (0.932)
  waiting for transfers between devices: 31.7 us -> 23.4 us
  starting transfers between devices: 20.4 us -> 25.7 us
  local copies, waits for them, and re-layouts: 7.29 us -> 3.63 us
  Pallas kernels: 11.5 us -> 13.3 us
    ppermute x4 -> x5, waiting for transfers between devices: 20.5 us -> 15.9 us  [shift_level(): return lax.ppermute(value, 'row', pairs)]
    unnamed x18 -> x16, local copies, waits for them, and re-layouts: 7.21 us -> 3.6 us
    ppermute x4 -> x5, starting transfers between devices: 4.5 us -> 7.93 us  [shift_level(): return lax.ppermute(value, 'row', pairs)]
    ppermute x6 -> x7, waiting for transfers between devices: 5.7 us -> 3.56 us  [swap_partner(): return lax.ppermute(value, axis, [(s, s ^ 1) for s in range(count)])]
    pallas_call x10 -> x11, Pallas kernels: 11.5 us -> 13.3 us  [call(): pl.pallas_call(kernel, out_shape=shapes, in_specs=specs, out_specs=[HBM i...]
    ppermute x2, starting transfers between devices: 3.65 us -> 5.43 us  [swap_other(): return lax.ppermute(value, axis, pairs)]
    ppermute x2, waiting for transfers between devices: 5.51 us -> 3.99 us  [swap_other(): return lax.ppermute(value, axis, pairs)]
    ppermute x6 -> x7, starting transfers between devices: 12.2 us -> 12.3 us  [swap_partner(): return lax.ppermute(value, axis, [(s, s ^ 1) for s in range(count)])]
  transfers between devices with their start and end apart: 12 -> 14, of which waited for: 8 -> 8; matrix products, arithmetic and copies ran while one was open for 3% -> 0% of each run, Pallas kernels for 9% -> 13%
where the time goes in v4:
time: 67.1 us; the launch traced here: 66.8 us
  starting transfers between devices  25.7 us (38%)
  waiting for transfers between devices  23.4 us (35%)
  Pallas kernels  13.3 us (20%)
  local copies, waits for them, and re-layouts  3.63 us (5%)
  between operations  0.76 us (1%)
    ppermute x5, waiting for transfers between devices, shift_level(): return lax.ppermute(value, 'row', pairs)  15.9 us
    pallas_call x11, Pallas kernels, call(): pl.pallas_call(kernel, out_shape=shapes, in_specs=specs, out_specs=[HBM i...  13.3 us
    ppermute x7, starting transfers between devices, swap_partner(): return lax.ppermute(value, axis, [(s, s ^ 1) for s in range(count)])  12.3 us
    ppermute x5, starting transfers between devices, shift_level(): return lax.ppermute(value, 'row', pairs)  7.93 us
    ppermute x2, starting transfers between devices, swap_other(): return lax.ppermute(value, axis, pairs)  5.43 us
    ppermute x2, waiting for transfers between devices, swap_other(): return lax.ppermute(value, axis, pairs)  3.99 us
    unnamed x16, local copies, waits for them, and re-layouts  3.6 us
    ppermute x7, waiting for transfers between devices, swap_partner(): return lax.ppermute(value, axis, [(s, s ^ 1) for s in range(count)])  3.56 us
  transfers between devices with their start and end apart: 14, of which 8 were waited for; matrix products, arithmetic and copies ran while one was open for 0% of the time, Pallas kernels for 13%

profile of v4, /device:TPU:0, one launch (start us, length us, event | category | flops | bytes accessed | tf_op | source)
XLA Modules:
  0.0 66.8 jit_solution(15417163671757719450)
XLA Ops:
  0.6 2.3 %shard_map.106 = (bf16[4,512,128]{2,1,0:T(8,128)(2,1)}, bf16[3,512,128]{2,1,0:T(8,128)(2,1)}, bf16[4,512,128]{2,1,0:T(8,128)(2,1)}, bf16[1,512,128]{2,1,0:T(8,128)(2,1)}) custom-call(s32[8,56]{1,0:T(8,128)} %pattern_hbm.1, bf16[512,896]{1,0:T(8,128)(2,1)} %density_hbm.1), custom_call_target="tpu_custom_call" | custom-call | bytes 2492160 | tf_op jit(solution)/shard_map/pallas_call | solution.py:337
  2.9 3.0 %collective-permute-start = (bf16[4,512,128]{2,1,0:T(8,128)(2,1)}, bf16[4,512,128]{2,1,0:T(8,128)(2,1)}, u32[]{:S(2)}, u32[]{:S(2)}) collective-permute-start(bf16[4,512,128]{2,1,0:T(8,128)(2,1)} %get-tuple-element.33.x1a_ref), channel_id=1, source_target_pairs={{0,4},{4,0},{8,12},{12,8},{16,20},{20,16},{24,28},{28,24},{1,5},{5... | collective-permute-start | bytes 1572872 | tf_op jit(solution)/shard_map/ppermute | solution.py:307
  5.9 1.6 %collective-permute-start.2 = (bf16[4,512,128]{2,1,0:T(8,128)(2,1)}, bf16[4,512,128]{2,1,0:T(8,128)(2,1)}, u32[]{:S(2)}, u32[]{:S(2)}) collective-permute-start(bf16[4,512,128]{2,1,0:T(8,128)(2,1)} %get-tuple-element.35), channel_id=1, source_target_pairs={{0,8},{4,28},{8,16},{12,4},{16,24},{20,12},{24,0},{28,20},{1,9},{5... | collective-permute-start | bytes 1572872 | tf_op jit(solution)/shard_map/ppermute | solution.py:319
  7.5 2.6 %collective-permute-start.1 = (bf16[3,512,128]{2,1,0:T(8,128)(2,1)}, bf16[3,512,128]{2,1,0:T(8,128)(2,1)S(1)}, u32[]{:S(2)}, u32[]{:S(2)}) collective-permute-start(bf16[3,512,128]{2,1,0:T(8,128)(2,1)} %get-tuple-element.34.x1b_ref), channel_id=1, source_target_pairs={{0,4},{4,0},{8,12},{12,8},{16,20},{20,16},{24,28},{28,24},{1,5},{5... | collective-permute-start | bytes 1179656 | tf_op jit(solution)/shard_map/ppermute | solution.py:307
  10.1 2.4 %shard_map.104 = (bf16[192,512]{1,0:T(8,128)(2,1)}, bf16[7,128,192]{2,1,0:T(8,128)(2,1)}, f32[7,8,128]{2,1,0:T(8,128)}, f32[8,3584]{1,0:T(8,128)}) custom-call(s32[8,56]{1,0:T(8,128)} %pattern_hbm.1, s32[8]{0:T(128)} %refs_1_.1, s32[8]{0:T(128)} %refs_2_.1, s32[1,14]{1,0:T(1,128)} %refs_3_.1, s32[1,14]{1,0:T(1,128)} %refs_4_.1, bf16[32,512]{1,0:T(8,128)(2,1)} %bitcast.5, ...), custom_call_target="tpu_custom_call" | custom-call | flops 6000000000 | bytes 776112 | tf_op jit(solution)/shard_map/pallas_call | solution.py:337
  12.5 1.0 %copy-done.2 = bf16[7,128,192]{2,1,0:T(8,128)(2,1)S(1)} copy-done((bf16[7,128,192]{2,1,0:T(8,128)(2,1)S(1)}, bf16[7,128,192]{2,1,0:T(8,128)(2,1)}, u32[]{:S(2)}) %copy-start.2) | copy-done | bytes 344088
  13.5 0.9 %copy-done.4 = bf16[192,512]{1,0:T(8,128)(2,1)S(1)} copy-done((bf16[192,512]{1,0:T(8,128)(2,1)S(1)}, bf16[192,512]{1,0:T(8,128)(2,1)}, u32[]{:S(2)}) %copy-start.4) | copy-done | bytes 196632
  14.5 0.9 %copy-done.5 = f32[8,3584]{1,0:T(8,128)S(1)} copy-done((f32[8,3584]{1,0:T(8,128)S(1)}, f32[8,3584]{1,0:T(8,128)}, u32[]{:S(2)}) %copy-start.5) | copy-done | bytes 114712
  15.4 0.7 %copy-done.6 = f32[7,8,128]{2,1,0:T(8,128)S(1)} copy-done((f32[7,8,128]{2,1,0:T(8,128)S(1)}, f32[7,8,128]{2,1,0:T(8,128)}, u32[]{:S(2)}) %copy-start.6) | copy-done | bytes 28696
  16.1 1.2 %shard_map.105 = (bf16[7,512,512]{2,1,0:T(8,128)(2,1)S(1)}, f32[7,512,128]{2,1,0:T(8,128)S(1)}, bf16[192,512]{1,0:T(8,128)(2,1)S(1)}, bf16[7,128,192]{2,1,0:T(8,128)(2,1)S(1)}, f32[7,8,128]{2,1,0:T(8,128)S(1)}) custom-call(bf16[512,3584]{1,0:T(8,128)(2,1)S(1)} %copy-done, f32[8,3584]{1,0:T(8,128)S(1)} %copy-done.5, bf16[192,512]{1,0:T(8,128)(2,1)S(1)} %copy-done.4, ...), custom_call_target="tpu_custom_call" | custom-call | flops 1000000000 | bytes 10428416 | tf_op jit(solution)/shard_map/pallas_call | solution.py:337
  17.3 1.6 %collective-permute-done.refs_0_ = bf16[4,512,128]{2,1,0:T(8,128)(2,1)} collective-permute-done((bf16[4,512,128]{2,1,0:T(8,128)(2,1)}, bf16[4,512,128]{2,1,0:T(8,128)(2,1)}, u32[]{:S(2)}, u32[]{:S(2)}) %collective-permute-start) | collective-permute-done | bytes 524320 | tf_op jit(solution)/shard_map/ppermute | solution.py:307
  18.9 2.2 %collective-permute-start.3 = (bf16[4,512,128]{2,1,0:T(8,128)(2,1)}, bf16[4,512,128]{2,1,0:T(8,128)(2,1)S(1)}, u32[]{:S(2)}, u32[]{:S(2)}) collective-permute-start(bf16[4,512,128]{2,1,0:T(8,128)(2,1)} %collective-permute-done.refs_0_), channel_id=1, source_target_pairs={{0,8},{4,28},{8,16},{12,4},{16,24},{20,12},{24,0},{28,20},{1,9},{5... | collective-permute-start | bytes 1572872 | tf_op jit(solution)/shard_map/ppermute | solution.py:319
  21.4 3.2 %collective-permute-start.5 = (bf16[4,512,128]{2,1,0:T(8,128)(2,1)}, bf16[4,512,128]{2,1,0:T(8,128)(2,1)S(1)}, u32[]{:S(2)}, u32[]{:S(2)}) collective-permute-start(bf16[4,512,128]{2,1,0:T(8,128)(2,1)} %collective-permute-done.2.refs_2_), channel_id=1, source_target_pairs={{0,4},{4,0},{8,12},{12,8},{16,20},{20,16},{24,28},{28,24},{1,5},{5... | collective-permute-start | bytes 1572872 | tf_op jit(solution)/shard_map/ppermute | solution.py:307
  24.6 0.7 %shard_map.107.before_ref = f32[7,512,128]{2,1,0:T(8,128)S(1)} custom-call(bf16[7,512,512]{2,1,0:T(8,128)(2,1)S(1)} %get-tuple-element.31.squares_ref, f32[7,512,128]{2,1,0:T(8,128)S(1)} %get-tuple-element.32.before_ref, bf16[4,512,128]{2,1,0:T(8,128)(2,1)S(1)} %copy-done.1, bf16[3,512,128]{2,1,0:T(8,128)(2,1)S(1)} %copy-done.3), custom_call_target="tpu_custom_call" | custom-call | bytes 8257536 | tf_op jit(solution)/shard_map/pallas_call | solution.py:337
  25.3 1.9 %collective-permute-done.1.refs_1_ = bf16[3,512,128]{2,1,0:T(8,128)(2,1)S(1)} collective-permute-done((bf16[3,512,128]{2,1,0:T(8,128)(2,1)}, bf16[3,512,128]{2,1,0:T(8,128)(2,1)S(1)}, u32[]{:S(2)}, u32[]{:S(2)}) %collective-permute-start.1) | collective-permute-done | bytes 393248 | tf_op jit(solution)/shard_map/ppermute | solution.py:307
  27.3 2.2 %collective-permute-start.4 = (bf16[2,512,128]{2,1,0:T(8,128)(2,1)S(1)}, bf16[2,512,128]{2,1,0:T(8,128)(2,1)S(1)}, u32[]{:S(2)}, u32[]{:S(2)}) collective-permute-start(bf16[2,512,128]{2,1,0:T(8,128)(2,1)S(1)} %slice.8), channel_id=1, source_target_pairs={{0,8},{4,28},{8,16},{12,4},{16,24},{20,12},{24,0},{28,20},{1,9},{5... | collective-permute-start | bytes 786440 | tf_op jit(solution)/shard_map/ppermute | solution.py:319
  29.5 2.1 %shard_map.108.before_ref = f32[7,512,128]{2,1,0:T(8,128)S(1)} custom-call(bf16[7,512,512]{2,1,0:T(8,128)(2,1)S(1)} %get-tuple-element.31.squares_ref, f32[7,512,128]{2,1,0:T(8,128)S(1)} %shard_map.107.before_ref, bf16[4,512,128]{2,1,0:T(8,128)(2,1)} %collective-permute-done.refs_0_, bf16[3,512,128]{2,1,0:T(8,128)(2,1)S(1)} %collective-permute-done.1.refs_1_, ...), custom_call_target="tpu_custom_call" | custom-call | flops 3000000000 | bytes 8781824 | tf_op jit(solution)/shard_map/pallas_call | solution.py:337
  31.6 4.4 %collective-permute-done.3.refs_0_ = bf16[4,512,128]{2,1,0:T(8,128)(2,1)S(1)} collective-permute-done((bf16[4,512,128]{2,1,0:T(8,128)(2,1)}, bf16[4,512,128]{2,1,0:T(8,128)(2,1)S(1)}, u32[]{:S(2)}, u32[]{:S(2)}) %collective-permute-start.3) | collective-permute-done | bytes 524320 | tf_op jit(solution)/shard_map/ppermute | solution.py:319
  36.1 1.0 %collective-permute-start.6 = (bf16[4,512,128]{2,1,0:T(8,128)(2,1)S(1)}, bf16[4,512,128]{2,1,0:T(8,128)(2,1)S(1)}, u32[]{:S(2)}, u32[]{:S(2)}) collective-permute-start(bf16[4,512,128]{2,1,0:T(8,128)(2,1)S(1)} %collective-permute-done.3.refs_0_), channel_id=1, source_target_pairs={{0,4},{4,0},{8,12},{12,8},{16,20},{20,16},{24,28},{28,24},{1,5},{5... | collective-permute-start | bytes 1572872 | tf_op jit(solution)/shard_map/ppermute | solution.py:307
  37.4 1.6 %collective-permute-start.9 = (bf16[1,512,128]{2,1,0:T(8,128)(2,1)S(1)}, bf16[1,512,128]{2,1,0:T(8,128)(2,1)S(1)}, u32[]{:S(2)}, u32[]{:S(2)}) collective-permute-start(bf16[1,512,128]{2,1,0:T(8,128)(2,1)S(1)} %copy-done.7), channel_id=1, source_target_pairs={{0,8},{4,28},{8,16},{12,4},{16,24},{20,12},{24,0},{28,20},{1,9},{5... | collective-permute-start | bytes 393224 | tf_op jit(solution)/shard_map/ppermute | solution.py:319
  39.0 1.9 %collective-permute-done.4.refs_0_ = bf16[2,512,128]{2,1,0:T(8,128)(2,1)S(1)} collective-permute-done((bf16[2,512,128]{2,1,0:T(8,128)(2,1)S(1)}, bf16[2,512,128]{2,1,0:T(8,128)(2,1)S(1)}, u32[]{:S(2)}, u32[]{:S(2)}) %collective-permute-start.4) | collective-permute-done | bytes 262176 | tf_op jit(solution)/shard_map/ppermute | solution.py:319
  40.9 1.8 %collective-permute-start.7 = (bf16[1,512,128]{2,1,0:T(8,128)(2,1)S(1)}, bf16[1,512,128]{2,1,0:T(8,128)(2,1)S(1)}, u32[]{:S(2)}, u32[]{:S(2)}) collective-permute-start(bf16[1,512,128]{2,1,0:T(8,128)(2,1)S(1)} %slice.9), channel_id=1, source_target_pairs={{0,4},{4,0},{8,12},{12,8},{16,20},{20,16},{24,28},{28,24},{1,5},{5... | collective-permute-start | bytes 393224 | tf_op jit(solution)/shard_map/ppermute | solution.py:307
  43.1 0.6 shard_map.110.before_ref
  43.7 9.2 %collective-permute-done.9.z1b_ref = bf16[1,512,128]{2,1,0:T(8,128)(2,1)S(1)} collective-permute-done((bf16[1,512,128]{2,1,0:T(8,128)(2,1)S(1)}, bf16[1,512,128]{2,1,0:T(8,128)(2,1)S(1)}, u32[]{:S(2)}, u32[]{:S(2)}) %collective-permute-start.9) | collective-permute-done | bytes 131104 | tf_op jit(solution)/shard_map/ppermute | solution.py:319
  52.9 1.7 %shard_map.111 = (bf16[512,896]{1,0:T(8,128)(2,1)S(1)}, f32[128,192]{1,0:T(8,128)S(1)}, f32[32,192]{1,0:T(8,128)S(1)}, f32[32,192]{1,0:T(8,128)S(1)}) custom-call(f32[7,8,128]{2,1,0:T(8,128)S(1)} %get-tuple-element.30.mask_ref, bf16[7,512,512]{2,1,0:T(8,128)(2,1)S(1)} %get-tuple-element.31.squares_ref, f32[7,512,128]{2,1,0:T(8,128)S(1)} %shard_map.110.before_ref, ...), custom_call_target="tpu_custom_call" | custom-call | bytes 8450048 | tf_op jit(solution)/shard_map/pallas_call | solution.py:337
  54.6 0.8 %collective-permute-start.10 = (f32[32,192]{1,0:T(8,128)S(1)}, f32[32,192]{1,0:T(8,128)S(1)}, u32[]{:S(2)}, u32[]{:S(2)}) collective-permute-start(f32[32,192]{1,0:T(8,128)S(1)} %get-tuple-element.45), channel_id=1, source_target_pairs={{0,4},{4,0},{8,12},{12,8},{16,20},{20,16},{24,28},{28,24},{1,5},{5... | collective-permute-start | bytes 73736 | tf_op jit(solution)/shard_map/ppermute | solution.py:307
  55.4 3.8 %collective-permute-start.11 = (f32[32,192]{1,0:T(8,128)S(1)}, f32[32,192]{1,0:T(8,128)S(1)}, u32[]{:S(2)}, u32[]{:S(2)}) collective-permute-start(f32[32,192]{1,0:T(8,128)S(1)} %get-tuple-element.46), channel_id=1, source_target_pairs={{0,28},{4,8},{8,4},{12,16},{16,12},{20,24},{24,20},{28,0},{1,29},{... | collective-permute-start | bytes 73736 | tf_op jit(solution)/shard_map/ppermute | solution.py:313
  59.2 2.8 %collective-permute-done.11.got_b_ref = f32[32,192]{1,0:T(8,128)S(1)} collective-permute-done((f32[32,192]{1,0:T(8,128)S(1)}, f32[32,192]{1,0:T(8,128)S(1)}, u32[]{:S(2)}, u32[]{:S(2)}) %collective-permute-start.11) | collective-permute-done | bytes 24608 | tf_op jit(solution)/shard_map/ppermute | solution.py:313
  62.2 1.6 %collective-permute-start.13 = (f32[128,32]{1,0:T(8,128)S(1)}, f32[128,32]{1,0:T(8,128)S(1)}, u32[]{:S(2)}, u32[]{:S(2)}) collective-permute-start(f32[128,32]{1,0:T(8,128)S(1)} %get-tuple-element.49), channel_id=1, source_target_pairs={{0,3},{1,2},{2,1},{3,0},{4,7},{5,6},{6,5},{7,4},{8,11},{9,10},{10,... | collective-permute-start | bytes 49160 | tf_op jit(solution)/shard_map/ppermute | solution.py:313
  63.8 1.1 %shard_map.112 = bf16[512,896]{1,0:T(8,128)(2,1)} custom-call(bf16[512,896]{1,0:T(8,128)(2,1)S(1)} %get-tuple-element.43.own_ref), custom_call_target="tpu_custom_call" | custom-call | bytes 1835008 | tf_op jit(solution)/shard_map/pallas_call | solution.py:337
  64.9 1.2 %collective-permute-done.13.got_b_ref = f32[128,32]{1,0:T(8,128)S(1)} collective-permute-done((f32[128,32]{1,0:T(8,128)S(1)}, f32[128,32]{1,0:T(8,128)S(1)}, u32[]{:S(2)}, u32[]{:S(2)}) %collective-permute-start.13) | collective-permute-done | bytes 16416 | tf_op jit(solution)/shard_map/ppermute | solution.py:313
  66.1 0.7 %shard_map.114 = f32[128,128]{1,0:T(8,128)} custom-call(f32[128,128]{1,0:T(8,128)S(1)} %get-tuple-element.47.center_ref, f32[128,32]{1,0:T(8,128)S(1)} %collective-permute-done.12.got_a_ref, f32[128,32]{1,0:T(8,128)S(1)} %collective-permute-done.13.got_b_ref), custom_call_target="tpu_custom_call" | custom-call | bytes 163840 | tf_op jit(solution)/shard_map/pallas_call | solution.py:337
  (25 shorter events, 1.4 us)
Async XLA Ops:
  2.9 16.0 %collective-permute-start = (bf16[4,512,128]{2,1,0:T(8,128)(2,1)}, bf16[4,512,128]{2,1,0:T(8,128)(2,1)}, u32[]{:S(2)}, u32[]{:S(2)}) collective-permute-start(bf16[4,512,128]{2,1,0:T(8,128)(2,1)} %get-tuple-element.33.x1a_ref), channel_id=1, source_target_pairs={{0,4},{4,0},{8,12},{12,8},{16,20},{20,16},{24,28},{28,24},{1,5},{5... | collective-permute-start | bytes 1572872 | tf_op jit(solution)/shard_map/ppermute | solution.py:307
  5.9 15.6 %collective-permute-start.2 = (bf16[4,512,128]{2,1,0:T(8,128)(2,1)}, bf16[4,512,128]{2,1,0:T(8,128)(2,1)}, u32[]{:S(2)}, u32[]{:S(2)}) collective-permute-start(bf16[4,512,128]{2,1,0:T(8,128)(2,1)} %get-tuple-element.35), channel_id=1, source_target_pairs={{0,8},{4,28},{8,16},{12,4},{16,24},{20,12},{24,0},{28,20},{1,9},{5... | collective-permute-start | bytes 1572872 | tf_op jit(solution)/shard_map/ppermute | solution.py:319
  7.5 19.8 %collective-permute-start.1 = (bf16[3,512,128]{2,1,0:T(8,128)(2,1)}, bf16[3,512,128]{2,1,0:T(8,128)(2,1)S(1)}, u32[]{:S(2)}, u32[]{:S(2)}) collective-permute-start(bf16[3,512,128]{2,1,0:T(8,128)(2,1)} %get-tuple-element.34.x1b_ref), channel_id=1, source_target_pairs={{0,4},{4,0},{8,12},{12,8},{16,20},{20,16},{24,28},{28,24},{1,5},{5... | collective-permute-start | bytes 1179656 | tf_op jit(solution)/shard_map/ppermute | solution.py:307
  10.1 2.4 %copy-start = (bf16[512,3584]{1,0:T(8,128)(2,1)S(1)}, bf16[512,3584]{1,0:T(8,128)(2,1)}, u32[]{:S(2)}) copy-start(bf16[512,3584]{1,0:T(8,128)(2,1)} %p2_ref.1) | copy-start | bytes 11010052
  12.5 1.0 %copy-start.2 = (bf16[7,128,192]{2,1,0:T(8,128)(2,1)S(1)}, bf16[7,128,192]{2,1,0:T(8,128)(2,1)}, u32[]{:S(2)}) copy-start(bf16[7,128,192]{2,1,0:T(8,128)(2,1)} %get-tuple-element.28.refs_1_) | copy-start | bytes 1032196
  13.5 0.9 %copy-start.4 = (bf16[192,512]{1,0:T(8,128)(2,1)S(1)}, bf16[192,512]{1,0:T(8,128)(2,1)}, u32[]{:S(2)}) copy-start(bf16[192,512]{1,0:T(8,128)(2,1)} %get-tuple-element.27.refs_0_) | copy-start | bytes 589828
  14.5 0.9 %copy-start.5 = (f32[8,3584]{1,0:T(8,128)S(1)}, f32[8,3584]{1,0:T(8,128)}, u32[]{:S(2)}) copy-start(f32[8,3584]{1,0:T(8,128)} %get-tuple-element.26.wide_ref) | copy-start | bytes 344068
  15.4 0.7 %copy-start.6 = (f32[7,8,128]{2,1,0:T(8,128)S(1)}, f32[7,8,128]{2,1,0:T(8,128)}, u32[]{:S(2)}) copy-start(f32[7,8,128]{2,1,0:T(8,128)} %get-tuple-element.29.refs_2_) | copy-start | bytes 86020
  16.1 8.5 %copy-start.1 = (bf16[4,512,128]{2,1,0:T(8,128)(2,1)S(1)}, bf16[4,512,128]{2,1,0:T(8,128)(2,1)}, u32[]{:S(2)}) copy-start(bf16[4,512,128]{2,1,0:T(8,128)(2,1)} %get-tuple-element.33.x1a_ref) | copy-start | bytes 1572868
  16.1 8.5 %copy-start.3 = (bf16[3,512,128]{2,1,0:T(8,128)(2,1)S(1)}, bf16[3,512,128]{2,1,0:T(8,128)(2,1)}, u32[]{:S(2)}) copy-start(bf16[3,512,128]{2,1,0:T(8,128)(2,1)} %get-tuple-element.34.x1b_ref) | copy-start | bytes 1179652
  18.9 17.1 %collective-permute-start.3 = (bf16[4,512,128]{2,1,0:T(8,128)(2,1)}, bf16[4,512,128]{2,1,0:T(8,128)(2,1)S(1)}, u32[]{:S(2)}, u32[]{:S(2)}) collective-permute-start(bf16[4,512,128]{2,1,0:T(8,128)(2,1)} %collective-permute-done.refs_0_), channel_id=1, source_target_pairs={{0,8},{4,28},{8,16},{12,4},{16,24},{20,12},{24,0},{28,20},{1,9},{5... | collective-permute-start | bytes 1572872 | tf_op jit(solution)/shard_map/ppermute | solution.py:319
  21.4 21.7 %collective-permute-start.5 = (bf16[4,512,128]{2,1,0:T(8,128)(2,1)}, bf16[4,512,128]{2,1,0:T(8,128)(2,1)S(1)}, u32[]{:S(2)}, u32[]{:S(2)}) collective-permute-start(bf16[4,512,128]{2,1,0:T(8,128)(2,1)} %collective-permute-done.2.refs_2_), channel_id=1, source_target_pairs={{0,4},{4,0},{8,12},{12,8},{16,20},{20,16},{24,28},{28,24},{1,5},{5... | collective-permute-start | bytes 1572872 | tf_op jit(solution)/shard_map/ppermute | solution.py:307
  27.3 10.1 %copy-start.7 = (bf16[1,512,128]{2,1,0:T(8,128)(2,1)S(1)}, bf16[1,512,128]{2,1,0:T(8,128)(2,1)}, u32[]{:S(2)}) copy-start(bf16[1,512,128]{2,1,0:T(8,128)(2,1)} %get-tuple-element.40) | copy-start | bytes 393220
  27.3 13.6 %collective-permute-start.4 = (bf16[2,512,128]{2,1,0:T(8,128)(2,1)S(1)}, bf16[2,512,128]{2,1,0:T(8,128)(2,1)S(1)}, u32[]{:S(2)}, u32[]{:S(2)}) collective-permute-start(bf16[2,512,128]{2,1,0:T(8,128)(2,1)S(1)} %slice.8), channel_id=1, source_target_pairs={{0,8},{4,28},{8,16},{12,4},{16,24},{20,12},{24,0},{28,20},{1,9},{5... | collective-permute-start | bytes 786440 | tf_op jit(solution)/shard_map/ppermute | solution.py:319
  36.1 16.9 %collective-permute-start.6 = (bf16[4,512,128]{2,1,0:T(8,128)(2,1)S(1)}, bf16[4,512,128]{2,1,0:T(8,128)(2,1)S(1)}, u32[]{:S(2)}, u32[]{:S(2)}) collective-permute-start(bf16[4,512,128]{2,1,0:T(8,128)(2,1)S(1)} %collective-permute-done.3.refs_0_), channel_id=1, source_target_pairs={{0,4},{4,0},{8,12},{12,8},{16,20},{20,16},{24,28},{28,24},{1,5},{5... | collective-permute-start | bytes 1572872 | tf_op jit(solution)/shard_map/ppermute | solution.py:307
  37.1 15.9 %collective-permute-start.8 = (bf16[4,512,128]{2,1,0:T(8,128)(2,1)S(1)}, bf16[4,512,128]{2,1,0:T(8,128)(2,1)S(1)}, u32[]{:S(2)}, u32[]{:S(2)}) collective-permute-start(bf16[4,512,128]{2,1,0:T(8,128)(2,1)S(1)} %collective-permute-done.3.refs_0_), channel_id=1, source_target_pairs={{0,8},{4,28},{8,16},{12,4},{16,24},{20,12},{24,0},{28,20},{1,9},{5... | collective-permute-start | bytes 1572872 | tf_op jit(solution)/shard_map/ppermute | solution.py:319
  37.4 15.5 %collective-permute-start.9 = (bf16[1,512,128]{2,1,0:T(8,128)(2,1)S(1)}, bf16[1,512,128]{2,1,0:T(8,128)(2,1)S(1)}, u32[]{:S(2)}, u32[]{:S(2)}) collective-permute-start(bf16[1,512,128]{2,1,0:T(8,128)(2,1)S(1)} %copy-done.7), channel_id=1, source_target_pairs={{0,8},{4,28},{8,16},{12,4},{16,24},{20,12},{24,0},{28,20},{1,9},{5... | collective-permute-start | bytes 393224 | tf_op jit(solution)/shard_map/ppermute | solution.py:319
  40.9 12.0 %collective-permute-start.7 = (bf16[1,512,128]{2,1,0:T(8,128)(2,1)S(1)}, bf16[1,512,128]{2,1,0:T(8,128)(2,1)S(1)}, u32[]{:S(2)}, u32[]{:S(2)}) collective-permute-start(bf16[1,512,128]{2,1,0:T(8,128)(2,1)S(1)} %slice.9), channel_id=1, source_target_pairs={{0,4},{4,0},{8,12},{12,8},{16,20},{20,16},{24,28},{28,24},{1,5},{5... | collective-permute-start | bytes 393224 | tf_op jit(solution)/shard_map/ppermute | solution.py:307
  54.6 4.6 %collective-permute-start.10 = (f32[32,192]{1,0:T(8,128)S(1)}, f32[32,192]{1,0:T(8,128)S(1)}, u32[]{:S(2)}, u32[]{:S(2)}) collective-permute-start(f32[32,192]{1,0:T(8,128)S(1)} %get-tuple-element.45), channel_id=1, source_target_pairs={{0,4},{4,0},{8,12},{12,8},{16,20},{20,16},{24,28},{28,24},{1,5},{5... | collective-permute-start | bytes 73736 | tf_op jit(solution)/shard_map/ppermute | solution.py:307
  55.4 6.6 %collective-permute-start.11 = (f32[32,192]{1,0:T(8,128)S(1)}, f32[32,192]{1,0:T(8,128)S(1)}, u32[]{:S(2)}, u32[]{:S(2)}) collective-permute-start(f32[32,192]{1,0:T(8,128)S(1)} %get-tuple-element.46), channel_id=1, source_target_pairs={{0,28},{4,8},{8,4},{12,16},{16,12},{20,24},{24,20},{28,0},{1,29},{... | collective-permute-start | bytes 73736 | tf_op jit(solution)/shard_map/ppermute | solution.py:313
  62.1 2.8 %collective-permute-start.12 = (f32[128,32]{1,0:T(8,128)S(1)}, f32[128,32]{1,0:T(8,128)S(1)}, u32[]{:S(2)}, u32[]{:S(2)}) collective-permute-start(f32[128,32]{1,0:T(8,128)S(1)} %get-tuple-element.48), channel_id=1, source_target_pairs={{0,1},{1,0},{2,3},{3,2},{4,5},{5,4},{6,7},{7,6},{8,9},{9,8},{10,11... | collective-permute-start | bytes 49160 | tf_op jit(solution)/shard_map/ppermute | solution.py:307
  62.2 3.9 %collective-permute-start.13 = (f32[128,32]{1,0:T(8,128)S(1)}, f32[128,32]{1,0:T(8,128)S(1)}, u32[]{:S(2)}, u32[]{:S(2)}) collective-permute-start(f32[128,32]{1,0:T(8,128)S(1)} %get-tuple-element.49), channel_id=1, source_target_pairs={{0,3},{1,2},{2,1},{3,0},{4,7},{5,6},{6,5},{7,4},{8,11},{9,10},{10,... | collective-permute-start | bytes 49160 | tf_op jit(solution)/shard_map/ppermute | solution.py:313

commit v5 on v4

--- a/solution.py
+++ b/solution.py
@@ -227,35 +227,56 @@
         )
 
 
-def last_kernel(dims, mask_ref, squares_ref, before_ref, x2p_ref, x2q_ref, z3_ref, z1b_ref, *refs):
-    xt_ref, y_ref, new_ref, middle_ref, rim_a_ref, rim_b_ref = refs
+def finish(mask_ref, k, total, new_ref, at):
+    br, uw = mask_ref.shape[1:]
+    bs = total.shape[0] // br
+    for i in range(br):
+        rows = slice(i * bs, (i + 1) * bs)
+        kept = total[rows] * mask_ref[k, i : i + 1, :]
+        new_ref[rows, at * uw : (at + 1) * uw] = kept.astype(BF16)
+
+
+def inner_kernel(
+    mask_ref, squares_ref, before_ref, x2p_ref, z3_ref, y_ref, new_ref, half_ref, edges_ref
+):
+    uw = edges_ref.shape[2]
+
+    def product(distance, *tiles):
+        wide = jnp.concatenate(tiles, axis=1)
+        return jnp.dot(squares_ref[HD + distance], wide, preferred_element_type=F32)
+
+    low = product(-2, x2p_ref[3], x2p_ref[2])
+    mid = product(-2, x2p_ref[1], x2p_ref[0]) + product(3, z3_ref[0], z3_ref[1])
+    high = product(3, z3_ref[2], z3_ref[3])
+    parts = [low[:, :uw], low[:, uw:], mid[:, :uw], mid[:, uw:], high[:, :uw]]
+    for at, part in enumerate(parts):
+        finish(mask_ref, at + 1, before_ref[at + 1] - part, new_ref, at)
+    edges_ref[0] = before_ref[0]
+    edges_ref[1] = before_ref[CHUNKS - 1] - high[:, uw:]
+    inner = y_ref[1 : CHUNKS - 1].reshape((CHUNKS - 2) * uw, EY)
+    half_ref[...] = jnp.dot(new_ref[...], inner, preferred_element_type=F32)
+
+
+def last_kernel(
+    mask_ref,
+    squares_ref,
+    edges_ref,
+    x2q_ref,
+    z1b_ref,
+    xt_ref,
+    y_ref,
+    half_ref,
+    new_ref,
+    middle_ref,
+    rim_a_ref,
+    rim_b_ref,
+):
     odd = lax.axis_index("row") % 2
-    bs, uw = dims.bs, dims.uw
-
-    def product(distance, *tiles):
-        wide = tiles[0] if len(tiles) == 1 else jnp.concatenate(tiles, axis=1)
-        return jnp.dot(squares_ref[HD + distance], wide, preferred_element_type=F32)
-
-    def finish(k, total):
-        for i in range(dims.br):
-            rows = slice(i * bs, (i + 1) * bs)
-            kept = total[rows] * mask_ref[k, i : i + 1, :]
-            new_ref[rows, k * uw : (k + 1) * uw] = kept.astype(BF16)
-
-    x2 = [x2p_ref[j] for j in range(NEAR)] + [x2q_ref[0]]
-    low = product(-2, x2[4], x2[3])
-    mid = product(-2, x2[1], x2[0]) + product(3, z3_ref[0], z3_ref[1])
-    high = product(3, z3_ref[2], z3_ref[3])
-    finish(0, before_ref[0] - low[:, :uw])
-    finish(1, before_ref[1] - low[:, uw:])
-    finish(2, before_ref[2] - product(-2, x2[2]))
-    finish(3, before_ref[3] - mid[:, :uw])
-    finish(4, before_ref[4] - mid[:, uw:])
-    finish(5, before_ref[5] - high[:, :uw])
-    finish(6, before_ref[6] - high[:, uw:] - product(2, z1b_ref[0]))
-    half = jnp.dot(
-        new_ref[...], y_ref[...].reshape(CHUNKS * uw, EY), preferred_element_type=F32
-    )
+    product = lambda d, tile: jnp.dot(squares_ref[HD + d], tile, preferred_element_type=F32)
+    finish(mask_ref, 0, edges_ref[0] - product(-2, x2q_ref[0]), new_ref, 0)
+    finish(mask_ref, CHUNKS - 1, edges_ref[1] - product(2, z1b_ref[0]), new_ref, 1)
+    outer = jnp.concatenate([y_ref[0], y_ref[CHUNKS - 1]], axis=0)
+    half = half_ref[...] + jnp.dot(new_ref[...], outer, preferred_element_type=F32)
     extended = jnp.dot(xt_ref[...], half.astype(BF16), preferred_element_type=F32)
     middle_ref[...] = extended[M : M + SX]
     lower, upper = extended[:M], extended[SX + M :]
@@ -263,19 +284,23 @@
     rim_b_ref[...] = jnp.where(odd == 1, upper, lower)
 
 
-def order_kernel(dims, own_ref, new_ref):
+def order_kernel(inner_ref, edges_ref, new_ref):
     odd = lax.axis_index("row") % 2
-    uw = dims.uw
+    uw = edges_ref.shape[1] // 2
 
     @pl.when(odd == 1)
     def _():
-        new_ref[...] = own_ref[...]
+        new_ref[:, :uw] = edges_ref[:, :uw]
+        new_ref[:, uw : (CHUNKS - 1) * uw] = inner_ref[...]
+        new_ref[:, (CHUNKS - 1) * uw :] = edges_ref[:, uw:]
 
     @pl.when(odd == 0)
     def _():
-        for k in range(CHUNKS):
-            at = CHUNKS - 1 - k
-            new_ref[:, at * uw : (at + 1) * uw] = own_ref[:, k * uw : (k + 1) * uw]
+        new_ref[:, :uw] = edges_ref[:, uw:]
+        for at in range(CHUNKS - 2):
+            place = CHUNKS - 2 - at
+            new_ref[:, place * uw : (place + 1) * uw] = inner_ref[:, at * uw : (at + 1) * uw]
+        new_ref[:, (CHUNKS - 1) * uw :] = edges_ref[:, :uw]
 
 
 def row_rims_kernel(middle_ref, got_a_ref, got_b_ref, center_ref, rim_a_ref, rim_b_ref):
@@ -443,25 +468,26 @@
         ],
         beside=4,
     )
-    new_own, middle, rim_a, rim_b = call(
-        functools.partial(last_kernel, dims),
-        [
-            ((rows, dims.wc * dims.bs), BF16),
-            ((SX, EY), F32),
-            ((M, EY), F32),
-            ((M, EY), F32),
-        ],
-        [mask, squares, summed, x2p, x2q, z3, z1b, xt, y_spread],
+    new_inner, half, edges = call(
+        inner_kernel,
+        [((rows, (CHUNKS - 2) * uw), BF16), ((rows, EY), F32), ((2, rows, uw), F32)],
+        [mask, squares, summed, x2p, z3, y_spread],
+        beside=0,
+    )
+    new_edges, middle, rim_a, rim_b = call(
+        last_kernel,
+        [((rows, 2 * uw), BF16), ((SX, EY), F32), ((M, EY), F32), ((M, EY), F32)],
+        [mask, squares, edges, x2q, z1b, xt, y_spread, half],
     )
     (new_density,) = call(
-        functools.partial(order_kernel, dims), [(new_own.shape, BF16)], [new_own]
+        order_kernel, [((rows, dims.wc * dims.bs), BF16)], [new_inner, new_edges]
     )
     got_a = swap_partner(rim_a, "row")
     got_b = swap_other(rim_b, "row")
     center, rim_a, rim_b = call(
         row_rims_kernel,
         [((SX, SY), F32), ((SX, M), F32), ((SX, M), F32)],
-        [middle, got_a, got_b],
+        [after(middle, new_density), got_a, got_b],
     )
     got_a = swap_partner(rim_a, "col")
     got_b = swap_other(rim_b, "col")

time: 67.1 us -> 66.2 us (0.987)
  waiting for transfers between devices: 23.4 us -> 22.2 us
    ppermute x5, waiting for transfers between devices: 15.9 us -> 7.99 us  [shift_level(): return lax.ppermute(value, 'row', pairs)]
    ppermute x7, waiting for transfers between devices: 3.56 us -> 10.2 us  [swap_partner(): return lax.ppermute(value, axis, [(s, s ^ 1) for s in range(count)])]
    pallas_call x11 -> x12, Pallas kernels: 13.3 us -> 13.7 us  [call(): pl.pallas_call(kernel, out_shape=shapes, in_specs=specs, out_specs=[HBM i...]
  transfers between devices with their start and end apart: 14 -> 14, of which waited for: 8 -> 10; matrix products, arithmetic and copies ran while one was open for 0% -> 0% of each run, Pallas kernels for 13% -> 15%
where the time goes in v5:
time: 66.2 us; the launch traced here: 65.9 us
  starting transfers between devices  25.7 us (39%)
  waiting for transfers between devices  22.2 us (34%)
  Pallas kernels  13.7 us (21%)
  local copies, waits for them, and re-layouts  3.63 us (5%)
  between operations  0.76 us (1%)
    pallas_call x12, Pallas kernels, call(): pl.pallas_call(kernel, out_shape=shapes, in_specs=specs, out_specs=[HBM i...  13.7 us
    ppermute x7, starting transfers between devices, swap_partner(): return lax.ppermute(value, axis, [(s, s ^ 1) for s in range(count)])  12.3 us
    ppermute x7, waiting for transfers between devices, swap_partner(): return lax.ppermute(value, axis, [(s, s ^ 1) for s in range(count)])  10.2 us
    ppermute x5, waiting for transfers between devices, shift_level(): return lax.ppermute(value, 'row', pairs)  7.99 us
    ppermute x5, starting transfers between devices, shift_level(): return lax.ppermute(value, 'row', pairs)  7.92 us
    ppermute x2, starting transfers between devices, swap_other(): return lax.ppermute(value, axis, pairs)  5.43 us
    ppermute x2, waiting for transfers between devices, swap_other(): return lax.ppermute(value, axis, pairs)  3.98 us
    unnamed x16, local copies, waits for them, and re-layouts  3.6 us
  transfers between devices with their start and end apart: 14, of which 10 were waited for; matrix products, arithmetic and copies ran while one was open for 0% of the time, Pallas kernels for 15%

profile of v5, /device:TPU:0, one launch (start us, length us, event | category | flops | bytes accessed | tf_op | source)
XLA Modules:
  0.0 65.9 jit_solution(10029724950510534035)
XLA Ops:
  0.6 2.3 %shard_map.106 = (bf16[4,512,128]{2,1,0:T(8,128)(2,1)}, bf16[3,512,128]{2,1,0:T(8,128)(2,1)}, bf16[4,512,128]{2,1,0:T(8,128)(2,1)}, bf16[1,512,128]{2,1,0:T(8,128)(2,1)}) custom-call(s32[8,56]{1,0:T(8,128)} %pattern_hbm.1, bf16[512,896]{1,0:T(8,128)(2,1)} %density_hbm.1), custom_call_target="tpu_custom_call" | custom-call | bytes 2492160 | tf_op jit(solution)/shard_map/pallas_call | solution.py:362
  2.9 3.0 %collective-permute-start = (bf16[4,512,128]{2,1,0:T(8,128)(2,1)}, bf16[4,512,128]{2,1,0:T(8,128)(2,1)}, u32[]{:S(2)}, u32[]{:S(2)}) collective-permute-start(bf16[4,512,128]{2,1,0:T(8,128)(2,1)} %get-tuple-element.37.x1a_ref), channel_id=1, source_target_pairs={{0,4},{4,0},{8,12},{12,8},{16,20},{20,16},{24,28},{28,24},{1,5},{5... | collective-permute-start | bytes 1572872 | tf_op jit(solution)/shard_map/ppermute | solution.py:332
  5.9 1.6 %collective-permute-start.2 = (bf16[4,512,128]{2,1,0:T(8,128)(2,1)}, bf16[4,512,128]{2,1,0:T(8,128)(2,1)}, u32[]{:S(2)}, u32[]{:S(2)}) collective-permute-start(bf16[4,512,128]{2,1,0:T(8,128)(2,1)} %get-tuple-element.39), channel_id=1, source_target_pairs={{0,8},{4,28},{8,16},{12,4},{16,24},{20,12},{24,0},{28,20},{1,9},{5... | collective-permute-start | bytes 1572872 | tf_op jit(solution)/shard_map/ppermute | solution.py:344
  7.5 2.6 %collective-permute-start.1 = (bf16[3,512,128]{2,1,0:T(8,128)(2,1)}, bf16[3,512,128]{2,1,0:T(8,128)(2,1)S(1)}, u32[]{:S(2)}, u32[]{:S(2)}) collective-permute-start(bf16[3,512,128]{2,1,0:T(8,128)(2,1)} %get-tuple-element.38.x1b_ref), channel_id=1, source_target_pairs={{0,4},{4,0},{8,12},{12,8},{16,20},{20,16},{24,28},{28,24},{1,5},{5... | collective-permute-start | bytes 1179656 | tf_op jit(solution)/shard_map/ppermute | solution.py:332
  10.1 2.4 %shard_map.104 = (bf16[192,512]{1,0:T(8,128)(2,1)}, bf16[7,128,192]{2,1,0:T(8,128)(2,1)}, f32[7,8,128]{2,1,0:T(8,128)}, f32[8,3584]{1,0:T(8,128)}) custom-call(s32[8,56]{1,0:T(8,128)} %pattern_hbm.1, s32[8]{0:T(128)} %refs_1_.1, s32[8]{0:T(128)} %refs_2_.1, s32[1,14]{1,0:T(1,128)} %refs_3_.1, s32[1,14]{1,0:T(1,128)} %refs_4_.1, bf16[32,512]{1,0:T(8,128)(2,1)} %bitcast.5, ...), custom_call_target="tpu_custom_call" | custom-call | flops 6000000000 | bytes 776112 | tf_op jit(solution)/shard_map/pallas_call | solution.py:362
  12.5 1.0 %copy-done.2 = bf16[7,128,192]{2,1,0:T(8,128)(2,1)S(1)} copy-done((bf16[7,128,192]{2,1,0:T(8,128)(2,1)S(1)}, bf16[7,128,192]{2,1,0:T(8,128)(2,1)}, u32[]{:S(2)}) %copy-start.2) | copy-done | bytes 344088
  13.5 0.9 %copy-done.4 = bf16[192,512]{1,0:T(8,128)(2,1)S(1)} copy-done((bf16[192,512]{1,0:T(8,128)(2,1)S(1)}, bf16[192,512]{1,0:T(8,128)(2,1)}, u32[]{:S(2)}) %copy-start.4) | copy-done | bytes 196632
  14.5 0.9 %copy-done.5 = f32[8,3584]{1,0:T(8,128)S(1)} copy-done((f32[8,3584]{1,0:T(8,128)S(1)}, f32[8,3584]{1,0:T(8,128)}, u32[]{:S(2)}) %copy-start.5) | copy-done | bytes 114712
  15.4 0.7 %copy-done.6 = f32[7,8,128]{2,1,0:T(8,128)S(1)} copy-done((f32[7,8,128]{2,1,0:T(8,128)S(1)}, f32[7,8,128]{2,1,0:T(8,128)}, u32[]{:S(2)}) %copy-start.6) | copy-done | bytes 28696
  16.1 1.2 %shard_map.105 = (bf16[7,512,512]{2,1,0:T(8,128)(2,1)S(1)}, f32[7,512,128]{2,1,0:T(8,128)S(1)}, bf16[192,512]{1,0:T(8,128)(2,1)S(1)}, bf16[7,128,192]{2,1,0:T(8,128)(2,1)S(1)}, f32[7,8,128]{2,1,0:T(8,128)S(1)}) custom-call(bf16[512,3584]{1,0:T(8,128)(2,1)S(1)} %copy-done, f32[8,3584]{1,0:T(8,128)S(1)} %copy-done.5, bf16[192,512]{1,0:T(8,128)(2,1)S(1)} %copy-done.4, ...), custom_call_target="tpu_custom_call" | custom-call | flops 1000000000 | bytes 10428416 | tf_op jit(solution)/shard_map/pallas_call | solution.py:362
  17.3 1.6 %collective-permute-done.refs_0_ = bf16[4,512,128]{2,1,0:T(8,128)(2,1)} collective-permute-done((bf16[4,512,128]{2,1,0:T(8,128)(2,1)}, bf16[4,512,128]{2,1,0:T(8,128)(2,1)}, u32[]{:S(2)}, u32[]{:S(2)}) %collective-permute-start) | collective-permute-done | bytes 524320 | tf_op jit(solution)/shard_map/ppermute | solution.py:332
  18.9 2.2 %collective-permute-start.3 = (bf16[4,512,128]{2,1,0:T(8,128)(2,1)}, bf16[4,512,128]{2,1,0:T(8,128)(2,1)S(1)}, u32[]{:S(2)}, u32[]{:S(2)}) collective-permute-start(bf16[4,512,128]{2,1,0:T(8,128)(2,1)} %collective-permute-done.refs_0_), channel_id=1, source_target_pairs={{0,8},{4,28},{8,16},{12,4},{16,24},{20,12},{24,0},{28,20},{1,9},{5... | collective-permute-start | bytes 1572872 | tf_op jit(solution)/shard_map/ppermute | solution.py:344
  21.4 3.2 %collective-permute-start.5 = (bf16[4,512,128]{2,1,0:T(8,128)(2,1)}, bf16[4,512,128]{2,1,0:T(8,128)(2,1)S(1)}, u32[]{:S(2)}, u32[]{:S(2)}) collective-permute-start(bf16[4,512,128]{2,1,0:T(8,128)(2,1)} %collective-permute-done.2.refs_2_), channel_id=1, source_target_pairs={{0,4},{4,0},{8,12},{12,8},{16,20},{20,16},{24,28},{28,24},{1,5},{5... | collective-permute-start | bytes 1572872 | tf_op jit(solution)/shard_map/ppermute | solution.py:332
  24.6 0.7 %shard_map.107.before_ref = f32[7,512,128]{2,1,0:T(8,128)S(1)} custom-call(bf16[7,512,512]{2,1,0:T(8,128)(2,1)S(1)} %get-tuple-element.35.squares_ref, f32[7,512,128]{2,1,0:T(8,128)S(1)} %get-tuple-element.36.before_ref, bf16[4,512,128]{2,1,0:T(8,128)(2,1)S(1)} %copy-done.1, bf16[3,512,128]{2,1,0:T(8,128)(2,1)S(1)} %copy-done.3), custom_call_target="tpu_custom_call" | custom-call | bytes 8257536 | tf_op jit(solution)/shard_map/pallas_call | solution.py:362
  25.3 1.9 %collective-permute-done.1.refs_1_ = bf16[3,512,128]{2,1,0:T(8,128)(2,1)S(1)} collective-permute-done((bf16[3,512,128]{2,1,0:T(8,128)(2,1)}, bf16[3,512,128]{2,1,0:T(8,128)(2,1)S(1)}, u32[]{:S(2)}, u32[]{:S(2)}) %collective-permute-start.1) | collective-permute-done | bytes 393248 | tf_op jit(solution)/shard_map/ppermute | solution.py:332
  27.3 2.2 %collective-permute-start.4 = (bf16[2,512,128]{2,1,0:T(8,128)(2,1)S(1)}, bf16[2,512,128]{2,1,0:T(8,128)(2,1)S(1)}, u32[]{:S(2)}, u32[]{:S(2)}) collective-permute-start(bf16[2,512,128]{2,1,0:T(8,128)(2,1)S(1)} %slice.8), channel_id=1, source_target_pairs={{0,8},{4,28},{8,16},{12,4},{16,24},{20,12},{24,0},{28,20},{1,9},{5... | collective-permute-start | bytes 786440 | tf_op jit(solution)/shard_map/ppermute | solution.py:344
  29.5 2.1 %shard_map.108.before_ref = f32[7,512,128]{2,1,0:T(8,128)S(1)} custom-call(bf16[7,512,512]{2,1,0:T(8,128)(2,1)S(1)} %get-tuple-element.35.squares_ref, f32[7,512,128]{2,1,0:T(8,128)S(1)} %shard_map.107.before_ref, bf16[4,512,128]{2,1,0:T(8,128)(2,1)} %collective-permute-done.refs_0_, bf16[3,512,128]{2,1,0:T(8,128)(2,1)S(1)} %collective-permute-done.1.refs_1_, ...), custom_call_target="tpu_custom_call" | custom-call | flops 3000000000 | bytes 8781824 | tf_op jit(solution)/shard_map/pallas_call | solution.py:362
  31.6 4.4 %collective-permute-done.3.refs_0_ = bf16[4,512,128]{2,1,0:T(8,128)(2,1)S(1)} collective-permute-done((bf16[4,512,128]{2,1,0:T(8,128)(2,1)}, bf16[4,512,128]{2,1,0:T(8,128)(2,1)S(1)}, u32[]{:S(2)}, u32[]{:S(2)}) %collective-permute-start.3) | collective-permute-done | bytes 524320 | tf_op jit(solution)/shard_map/ppermute | solution.py:344
  36.1 1.0 %collective-permute-start.6 = (bf16[4,512,128]{2,1,0:T(8,128)(2,1)S(1)}, bf16[4,512,128]{2,1,0:T(8,128)(2,1)S(1)}, u32[]{:S(2)}, u32[]{:S(2)}) collective-permute-start(bf16[4,512,128]{2,1,0:T(8,128)(2,1)S(1)} %collective-permute-done.3.refs_0_), channel_id=1, source_target_pairs={{0,4},{4,0},{8,12},{12,8},{16,20},{20,16},{24,28},{28,24},{1,5},{5... | collective-permute-start | bytes 1572872 | tf_op jit(solution)/shard_map/ppermute | solution.py:332
  37.4 1.6 %collective-permute-start.9 = (bf16[1,512,128]{2,1,0:T(8,128)(2,1)S(1)}, bf16[1,512,128]{2,1,0:T(8,128)(2,1)S(1)}, u32[]{:S(2)}, u32[]{:S(2)}) collective-permute-start(bf16[1,512,128]{2,1,0:T(8,128)(2,1)S(1)} %copy-done.7), channel_id=1, source_target_pairs={{0,8},{4,28},{8,16},{12,4},{16,24},{20,12},{24,0},{28,20},{1,9},{5... | collective-permute-start | bytes 393224 | tf_op jit(solution)/shard_map/ppermute | solution.py:344
  39.0 1.9 %collective-permute-done.4.refs_0_ = bf16[2,512,128]{2,1,0:T(8,128)(2,1)S(1)} collective-permute-done((bf16[2,512,128]{2,1,0:T(8,128)(2,1)S(1)}, bf16[2,512,128]{2,1,0:T(8,128)(2,1)S(1)}, u32[]{:S(2)}, u32[]{:S(2)}) %collective-permute-start.4) | collective-permute-done | bytes 262176 | tf_op jit(solution)/shard_map/ppermute | solution.py:344
  40.9 1.8 %collective-permute-start.8 = (bf16[1,512,128]{2,1,0:T(8,128)(2,1)S(1)}, bf16[1,512,128]{2,1,0:T(8,128)(2,1)S(1)}, u32[]{:S(2)}, u32[]{:S(2)}) collective-permute-start(bf16[1,512,128]{2,1,0:T(8,128)(2,1)S(1)} %slice.9), channel_id=1, source_target_pairs={{0,4},{4,0},{8,12},{12,8},{16,20},{20,16},{24,28},{28,24},{1,5},{5... | collective-permute-start | bytes 393224 | tf_op jit(solution)/shard_map/ppermute | solution.py:332
  43.7 6.6 %collective-permute-done.6.x2p_ref = bf16[4,512,128]{2,1,0:T(8,128)(2,1)S(1)} collective-permute-done((bf16[4,512,128]{2,1,0:T(8,128)(2,1)S(1)}, bf16[4,512,128]{2,1,0:T(8,128)(2,1)S(1)}, u32[]{:S(2)}, u32[]{:S(2)}) %collective-permute-start.6) | collective-permute-done | bytes 524320 | tf_op jit(solution)/shard_map/ppermute | solution.py:332
  50.3 1.2 %collective-permute-done.7.z3_ref = bf16[4,512,128]{2,1,0:T(8,128)(2,1)S(1)} collective-permute-done((bf16[4,512,128]{2,1,0:T(8,128)(2,1)S(1)}, bf16[4,512,128]{2,1,0:T(8,128)(2,1)S(1)}, u32[]{:S(2)}, u32[]{:S(2)}) %collective-permute-start.7) | collective-permute-done | bytes 524320 | tf_op jit(solution)/shard_map/ppermute | solution.py:344
  51.5 1.2 %shard_map.111 = (bf16[512,640]{1,0:T(8,128)(2,1)S(1)}, f32[512,192]{1,0:T(8,128)S(1)}, f32[2,512,128]{2,1,0:T(8,128)S(1)}) custom-call(f32[7,8,128]{2,1,0:T(8,128)S(1)} %get-tuple-element.34.mask_ref, bf16[7,512,512]{2,1,0:T(8,128)(2,1)S(1)} %get-tuple-element.35.squares_ref, f32[7,512,128]{2,1,0:T(8,128)S(1)} %shard_map.110.before_ref, ...), custom_call_target="tpu_custom_call" | custom-call | bytes 8499200 | tf_op jit(solution)/shard_map/pallas_call | solution.py:362
  52.9 0.8 %shard_map.112 = (bf16[512,256]{1,0:T(8,128)(2,1)S(1)}, f32[128,192]{1,0:T(8,128)S(1)}, f32[32,192]{1,0:T(8,128)S(1)}, f32[32,192]{1,0:T(8,128)S(1)}) custom-call(f32[7,8,128]{2,1,0:T(8,128)S(1)} %get-tuple-element.34.mask_ref, bf16[7,512,512]{2,1,0:T(8,128)(2,1)S(1)} %get-tuple-element.35.squares_ref, f32[2,512,128]{2,1,0:T(8,128)S(1)} %get-tuple-element.44.edges_ref, ...), custom_call_target="tpu_custom_call" | custom-call | bytes 5828608 | tf_op jit(solution)/shard_map/pallas_call | solution.py:362
  53.7 0.8 %collective-permute-start.10 = (f32[32,192]{1,0:T(8,128)S(1)}, f32[32,192]{1,0:T(8,128)S(1)}, u32[]{:S(2)}, u32[]{:S(2)}) collective-permute-start(f32[32,192]{1,0:T(8,128)S(1)} %get-tuple-element.53), channel_id=1, source_target_pairs={{0,4},{4,0},{8,12},{12,8},{16,20},{20,16},{24,28},{28,24},{1,5},{5... | collective-permute-start | bytes 73736 | tf_op jit(solution)/shard_map/ppermute | solution.py:332
  54.5 3.8 %collective-permute-start.11 = (f32[32,192]{1,0:T(8,128)S(1)}, f32[32,192]{1,0:T(8,128)S(1)}, u32[]{:S(2)}, u32[]{:S(2)}) collective-permute-start(f32[32,192]{1,0:T(8,128)S(1)} %get-tuple-element.54), channel_id=1, source_target_pairs={{0,28},{4,8},{8,4},{12,16},{16,12},{20,24},{24,20},{28,0},{1,29},{... | collective-permute-start | bytes 73736 | tf_op jit(solution)/shard_map/ppermute | solution.py:338
  58.3 1.1 %shard_map.113 = bf16[512,896]{1,0:T(8,128)(2,1)} custom-call(bf16[512,640]{1,0:T(8,128)(2,1)S(1)} %get-tuple-element.43.inner_ref, bf16[512,256]{1,0:T(8,128)(2,1)S(1)} %get-tuple-element.50.edges_ref), custom_call_target="tpu_custom_call" | custom-call | bytes 1835008 | tf_op jit(solution)/shard_map/pallas_call | solution.py:362
  59.3 1.7 %collective-permute-done.11.got_b_ref = f32[32,192]{1,0:T(8,128)S(1)} collective-permute-done((f32[32,192]{1,0:T(8,128)S(1)}, f32[32,192]{1,0:T(8,128)S(1)}, u32[]{:S(2)}, u32[]{:S(2)}) %collective-permute-start.11) | collective-permute-done | bytes 24608 | tf_op jit(solution)/shard_map/ppermute | solution.py:338
  61.3 1.6 %collective-permute-start.13 = (f32[128,32]{1,0:T(8,128)S(1)}, f32[128,32]{1,0:T(8,128)S(1)}, u32[]{:S(2)}, u32[]{:S(2)}) collective-permute-start(f32[128,32]{1,0:T(8,128)S(1)} %get-tuple-element.57), channel_id=1, source_target_pairs={{0,3},{1,2},{2,1},{3,0},{4,7},{5,6},{6,5},{7,4},{8,11},{9,10},{10,... | collective-permute-start | bytes 49160 | tf_op jit(solution)/shard_map/ppermute | solution.py:338
  62.9 2.2 %collective-permute-done.13.got_b_ref = f32[128,32]{1,0:T(8,128)S(1)} collective-permute-done((f32[128,32]{1,0:T(8,128)S(1)}, f32[128,32]{1,0:T(8,128)S(1)}, u32[]{:S(2)}, u32[]{:S(2)}) %collective-permute-start.13) | collective-permute-done | bytes 16416 | tf_op jit(solution)/shard_map/ppermute | solution.py:338
  (26 shorter events, 2.8 us)
Async XLA Ops:
  2.9 16.0 %collective-permute-start = (bf16[4,512,128]{2,1,0:T(8,128)(2,1)}, bf16[4,512,128]{2,1,0:T(8,128)(2,1)}, u32[]{:S(2)}, u32[]{:S(2)}) collective-permute-start(bf16[4,512,128]{2,1,0:T(8,128)(2,1)} %get-tuple-element.37.x1a_ref), channel_id=1, source_target_pairs={{0,4},{4,0},{8,12},{12,8},{16,20},{20,16},{24,28},{28,24},{1,5},{5... | collective-permute-start | bytes 1572872 | tf_op jit(solution)/shard_map/ppermute | solution.py:332
  5.9 15.6 %collective-permute-start.2 = (bf16[4,512,128]{2,1,0:T(8,128)(2,1)}, bf16[4,512,128]{2,1,0:T(8,128)(2,1)}, u32[]{:S(2)}, u32[]{:S(2)}) collective-permute-start(bf16[4,512,128]{2,1,0:T(8,128)(2,1)} %get-tuple-element.39), channel_id=1, source_target_pairs={{0,8},{4,28},{8,16},{12,4},{16,24},{20,12},{24,0},{28,20},{1,9},{5... | collective-permute-start | bytes 1572872 | tf_op jit(solution)/shard_map/ppermute | solution.py:344
  7.5 19.8 %collective-permute-start.1 = (bf16[3,512,128]{2,1,0:T(8,128)(2,1)}, bf16[3,512,128]{2,1,0:T(8,128)(2,1)S(1)}, u32[]{:S(2)}, u32[]{:S(2)}) collective-permute-start(bf16[3,512,128]{2,1,0:T(8,128)(2,1)} %get-tuple-element.38.x1b_ref), channel_id=1, source_target_pairs={{0,4},{4,0},{8,12},{12,8},{16,20},{20,16},{24,28},{28,24},{1,5},{5... | collective-permute-start | bytes 1179656 | tf_op jit(solution)/shard_map/ppermute | solution.py:332
  10.1 2.5 %copy-start = (bf16[512,3584]{1,0:T(8,128)(2,1)S(1)}, bf16[512,3584]{1,0:T(8,128)(2,1)}, u32[]{:S(2)}) copy-start(bf16[512,3584]{1,0:T(8,128)(2,1)} %p2_ref.1) | copy-start | bytes 11010052
  12.5 1.0 %copy-start.2 = (bf16[7,128,192]{2,1,0:T(8,128)(2,1)S(1)}, bf16[7,128,192]{2,1,0:T(8,128)(2,1)}, u32[]{:S(2)}) copy-start(bf16[7,128,192]{2,1,0:T(8,128)(2,1)} %get-tuple-element.32.refs_1_) | copy-start | bytes 1032196
  13.5 0.9 %copy-start.4 = (bf16[192,512]{1,0:T(8,128)(2,1)S(1)}, bf16[192,512]{1,0:T(8,128)(2,1)}, u32[]{:S(2)}) copy-start(bf16[192,512]{1,0:T(8,128)(2,1)} %get-tuple-element.31.refs_0_) | copy-start | bytes 589828
  14.5 0.9 %copy-start.5 = (f32[8,3584]{1,0:T(8,128)S(1)}, f32[8,3584]{1,0:T(8,128)}, u32[]{:S(2)}) copy-start(f32[8,3584]{1,0:T(8,128)} %get-tuple-element.30.wide_ref) | copy-start | bytes 344068
  15.4 0.7 %copy-start.6 = (f32[7,8,128]{2,1,0:T(8,128)S(1)}, f32[7,8,128]{2,1,0:T(8,128)}, u32[]{:S(2)}) copy-start(f32[7,8,128]{2,1,0:T(8,128)} %get-tuple-element.33.refs_2_) | copy-start | bytes 86020
  16.1 8.5 %copy-start.1 = (bf16[4,512,128]{2,1,0:T(8,128)(2,1)S(1)}, bf16[4,512,128]{2,1,0:T(8,128)(2,1)}, u32[]{:S(2)}) copy-start(bf16[4,512,128]{2,1,0:T(8,128)(2,1)} %get-tuple-element.37.x1a_ref) | copy-start | bytes 1572868
  16.1 8.5 %copy-start.3 = (bf16[3,512,128]{2,1,0:T(8,128)(2,1)S(1)}, bf16[3,512,128]{2,1,0:T(8,128)(2,1)}, u32[]{:S(2)}) copy-start(bf16[3,512,128]{2,1,0:T(8,128)(2,1)} %get-tuple-element.38.x1b_ref) | copy-start | bytes 1179652
  18.9 17.1 %collective-permute-start.3 = (bf16[4,512,128]{2,1,0:T(8,128)(2,1)}, bf16[4,512,128]{2,1,0:T(8,128)(2,1)S(1)}, u32[]{:S(2)}, u32[]{:S(2)}) collective-permute-start(bf16[4,512,128]{2,1,0:T(8,128)(2,1)} %collective-permute-done.refs_0_), channel_id=1, source_target_pairs={{0,8},{4,28},{8,16},{12,4},{16,24},{20,12},{24,0},{28,20},{1,9},{5... | collective-permute-start | bytes 1572872 | tf_op jit(solution)/shard_map/ppermute | solution.py:344
  21.4 21.7 %collective-permute-start.5 = (bf16[4,512,128]{2,1,0:T(8,128)(2,1)}, bf16[4,512,128]{2,1,0:T(8,128)(2,1)S(1)}, u32[]{:S(2)}, u32[]{:S(2)}) collective-permute-start(bf16[4,512,128]{2,1,0:T(8,128)(2,1)} %collective-permute-done.2.refs_2_), channel_id=1, source_target_pairs={{0,4},{4,0},{8,12},{12,8},{16,20},{20,16},{24,28},{28,24},{1,5},{5... | collective-permute-start | bytes 1572872 | tf_op jit(solution)/shard_map/ppermute | solution.py:332
  27.3 10.1 %copy-start.7 = (bf16[1,512,128]{2,1,0:T(8,128)(2,1)S(1)}, bf16[1,512,128]{2,1,0:T(8,128)(2,1)}, u32[]{:S(2)}) copy-start(bf16[1,512,128]{2,1,0:T(8,128)(2,1)} %get-tuple-element.47) | copy-start | bytes 393220
  27.3 13.6 %collective-permute-start.4 = (bf16[2,512,128]{2,1,0:T(8,128)(2,1)S(1)}, bf16[2,512,128]{2,1,0:T(8,128)(2,1)S(1)}, u32[]{:S(2)}, u32[]{:S(2)}) collective-permute-start(bf16[2,512,128]{2,1,0:T(8,128)(2,1)S(1)} %slice.8), channel_id=1, source_target_pairs={{0,8},{4,28},{8,16},{12,4},{16,24},{20,12},{24,0},{28,20},{1,9},{5... | collective-permute-start | bytes 786440 | tf_op jit(solution)/shard_map/ppermute | solution.py:344
  36.1 14.2 %collective-permute-start.6 = (bf16[4,512,128]{2,1,0:T(8,128)(2,1)S(1)}, bf16[4,512,128]{2,1,0:T(8,128)(2,1)S(1)}, u32[]{:S(2)}, u32[]{:S(2)}) collective-permute-start(bf16[4,512,128]{2,1,0:T(8,128)(2,1)S(1)} %collective-permute-done.3.refs_0_), channel_id=1, source_target_pairs={{0,4},{4,0},{8,12},{12,8},{16,20},{20,16},{24,28},{28,24},{1,5},{5... | collective-permute-start | bytes 1572872 | tf_op jit(solution)/shard_map/ppermute | solution.py:332
  37.1 14.5 %collective-permute-start.7 = (bf16[4,512,128]{2,1,0:T(8,128)(2,1)S(1)}, bf16[4,512,128]{2,1,0:T(8,128)(2,1)S(1)}, u32[]{:S(2)}, u32[]{:S(2)}) collective-permute-start(bf16[4,512,128]{2,1,0:T(8,128)(2,1)S(1)} %collective-permute-done.3.refs_0_), channel_id=1, source_target_pairs={{0,8},{4,28},{8,16},{12,4},{16,24},{20,12},{24,0},{28,20},{1,9},{5... | collective-permute-start | bytes 1572872 | tf_op jit(solution)/shard_map/ppermute | solution.py:344
  37.4 15.5 %collective-permute-start.9 = (bf16[1,512,128]{2,1,0:T(8,128)(2,1)S(1)}, bf16[1,512,128]{2,1,0:T(8,128)(2,1)S(1)}, u32[]{:S(2)}, u32[]{:S(2)}) collective-permute-start(bf16[1,512,128]{2,1,0:T(8,128)(2,1)S(1)} %copy-done.7), channel_id=1, source_target_pairs={{0,8},{4,28},{8,16},{12,4},{16,24},{20,12},{24,0},{28,20},{1,9},{5... | collective-permute-start | bytes 393224 | tf_op jit(solution)/shard_map/ppermute | solution.py:344
  40.9 12.1 %collective-permute-start.8 = (bf16[1,512,128]{2,1,0:T(8,128)(2,1)S(1)}, bf16[1,512,128]{2,1,0:T(8,128)(2,1)S(1)}, u32[]{:S(2)}, u32[]{:S(2)}) collective-permute-start(bf16[1,512,128]{2,1,0:T(8,128)(2,1)S(1)} %slice.9), channel_id=1, source_target_pairs={{0,4},{4,0},{8,12},{12,8},{16,20},{20,16},{24,28},{28,24},{1,5},{5... | collective-permute-start | bytes 393224 | tf_op jit(solution)/shard_map/ppermute | solution.py:332
  53.7 5.7 %collective-permute-start.10 = (f32[32,192]{1,0:T(8,128)S(1)}, f32[32,192]{1,0:T(8,128)S(1)}, u32[]{:S(2)}, u32[]{:S(2)}) collective-permute-start(f32[32,192]{1,0:T(8,128)S(1)} %get-tuple-element.53), channel_id=1, source_target_pairs={{0,4},{4,0},{8,12},{12,8},{16,20},{20,16},{24,28},{28,24},{1,5},{5... | collective-permute-start | bytes 73736 | tf_op jit(solution)/shard_map/ppermute | solution.py:332
  54.5 6.6 %collective-permute-start.11 = (f32[32,192]{1,0:T(8,128)S(1)}, f32[32,192]{1,0:T(8,128)S(1)}, u32[]{:S(2)}, u32[]{:S(2)}) collective-permute-start(f32[32,192]{1,0:T(8,128)S(1)} %get-tuple-element.54), channel_id=1, source_target_pairs={{0,28},{4,8},{8,4},{12,16},{16,12},{20,24},{24,20},{28,0},{1,29},{... | collective-permute-start | bytes 73736 | tf_op jit(solution)/shard_map/ppermute | solution.py:338
  61.2 1.7 %collective-permute-start.12 = (f32[128,32]{1,0:T(8,128)S(1)}, f32[128,32]{1,0:T(8,128)S(1)}, u32[]{:S(2)}, u32[]{:S(2)}) collective-permute-start(f32[128,32]{1,0:T(8,128)S(1)} %get-tuple-element.56), channel_id=1, source_target_pairs={{0,1},{1,0},{2,3},{3,2},{4,5},{5,4},{6,7},{7,6},{8,9},{9,8},{10,11... | collective-permute-start | bytes 49160 | tf_op jit(solution)/shard_map/ppermute | solution.py:332
  61.3 3.9 %collective-permute-start.13 = (f32[128,32]{1,0:T(8,128)S(1)}, f32[128,32]{1,0:T(8,128)S(1)}, u32[]{:S(2)}, u32[]{:S(2)}) collective-permute-start(f32[128,32]{1,0:T(8,128)S(1)} %get-tuple-element.57), channel_id=1, source_target_pairs={{0,3},{1,2},{2,1},{3,0},{4,7},{5,6},{6,5},{7,4},{8,11},{9,10},{10,... | collective-permute-start | bytes 49160 | tf_op jit(solution)/shard_map/ppermute | solution.py:338

commit v6 on v5

--- a/solution.py
+++ b/solution.py
@@ -280,8 +280,8 @@
     extended = jnp.dot(xt_ref[...], half.astype(BF16), preferred_element_type=F32)
     middle_ref[...] = extended[M : M + SX]
     lower, upper = extended[:M], extended[SX + M :]
-    rim_a_ref[...] = jnp.where(odd == 1, lower, upper)
-    rim_b_ref[...] = jnp.where(odd == 1, upper, lower)
+    rim_a_ref[...] = jnp.where(odd == 1, lower, upper).astype(BF16)
+    rim_b_ref[...] = jnp.where(odd == 1, upper, lower).astype(BF16)
 
 
 def order_kernel(inner_ref, edges_ref, new_ref):
@@ -306,25 +306,26 @@
 def row_rims_kernel(middle_ref, got_a_ref, got_b_ref, center_ref, rim_a_ref, rim_b_ref):
     odd = lax.axis_index("row") % 2
     col_odd = lax.axis_index("col") % 2
-    got_a, got_b = got_a_ref[...], got_b_ref[...]
+    got_a, got_b = got_a_ref[...].astype(F32), got_b_ref[...].astype(F32)
     low = jnp.where(odd == 1, got_a, got_b)
     high = jnp.where(odd == 1, got_b, got_a)
     interior = jnp.concatenate(
         [middle_ref[:M] + low, middle_ref[M : SX - M], middle_ref[SX - M :] + high], axis=0
     )
     center_ref[...] = interior[:, M : M + SY]
-    lower, upper = interior[:, :M], interior[:, SY + M :]
-    rim_a_ref[...] = jnp.where(col_odd == 1, lower, upper)
-    rim_b_ref[...] = jnp.where(col_odd == 1, upper, lower)
+    lower = interior[:, :SY].T[:M]
+    upper = interior[:, EY - SY :].T[SY - M :]
+    rim_a_ref[...] = jnp.where(col_odd == 1, lower, upper).astype(BF16)
+    rim_b_ref[...] = jnp.where(col_odd == 1, upper, lower).astype(BF16)
 
 
 def col_rims_kernel(center_ref, got_a_ref, got_b_ref, grid_ref):
     col_odd = lax.axis_index("col") % 2
-    got_a, got_b = got_a_ref[...], got_b_ref[...]
+    got_a, got_b = got_a_ref[...].astype(F32), got_b_ref[...].astype(F32)
     low = jnp.where(col_odd == 1, got_a, got_b)
     high = jnp.where(col_odd == 1, got_b, got_a)
-    none = jnp.zeros((SX, SY - 2 * M), F32)
-    grid_ref[...] = center_ref[...] + jnp.concatenate([low, none, high], axis=1)
+    none = jnp.zeros((SY - 2 * M, SX), F32)
+    grid_ref[...] = center_ref[...] + jnp.concatenate([low, none, high], axis=0).T
 
 
 def swap_partner(value, axis):
@@ -476,7 +477,7 @@
     )
     new_edges, middle, rim_a, rim_b = call(
         last_kernel,
-        [((rows, 2 * uw), BF16), ((SX, EY), F32), ((M, EY), F32), ((M, EY), F32)],
+        [((rows, 2 * uw), BF16), ((SX, EY), F32), ((M, EY), BF16), ((M, EY), BF16)],
         [mask, squares, edges, x2q, z1b, xt, y_spread, half],
     )
     (new_density,) = call(
@@ -486,7 +487,7 @@
     got_b = swap_other(rim_b, "row")
     center, rim_a, rim_b = call(
         row_rims_kernel,
-        [((SX, SY), F32), ((SX, M), F32), ((SX, M), F32)],
+        [((SX, SY), F32), ((M, SX), BF16), ((M, SX), BF16)],
         [after(middle, new_density), got_a, got_b],
     )
     got_a = swap_partner(rim_a, "col")

time: 66.2 us -> 65.4 us (0.988)
  waiting for transfers between devices: 22.2 us -> 21.2 us
    ppermute x2, waiting for transfers between devices: 3.98 us -> 3.06 us  [swap_other(): return lax.ppermute(value, axis, pairs)]
where the time goes in v6:
time: 65.4 us; the launch traced here: 65.1 us
  starting transfers between devices  25.7 us (39%)
  waiting for transfers between devices  21.2 us (32%)
  Pallas kernels  13.7 us (21%)
  local copies, waits for them, and re-layouts  3.63 us (6%)
  between operations  0.77 us (1%)
    pallas_call x12, Pallas kernels, call(): pl.pallas_call(kernel, out_shape=shapes, in_specs=specs, out_specs=[HBM i...  13.7 us
    ppermute x7, starting transfers between devices, swap_partner(): return lax.ppermute(value, axis, [(s, s ^ 1) for s in range(count)])  12.3 us
    ppermute x7, waiting for transfers between devices, swap_partner(): return lax.ppermute(value, axis, [(s, s ^ 1) for s in range(count)])  10.2 us
    ppermute x5, waiting for transfers between devices, shift_level(): return lax.ppermute(value, 'row', pairs)  7.99 us
    ppermute x5, starting transfers between devices, shift_level(): return lax.ppermute(value, 'row', pairs)  7.92 us
    ppermute x2, starting transfers between devices, swap_other(): return lax.ppermute(value, axis, pairs)  5.43 us
    unnamed x16, local copies, waits for them, and re-layouts  3.6 us
    ppermute x2, waiting for transfers between devices, swap_other(): return lax.ppermute(value, axis, pairs)  3.06 us
  transfers between devices with their start and end apart: 14, of which 10 were waited for; matrix products, arithmetic and copies ran while one was open for 0% of the time, Pallas kernels for 15%

profile of v6, /device:TPU:0, one launch (start us, length us, event | category | flops | bytes accessed | tf_op | source)
XLA Modules:
  0.0 65.1 jit_solution(15798447320610104319)
XLA Ops:
  0.6 2.3 %shard_map.106 = (bf16[4,512,128]{2,1,0:T(8,128)(2,1)}, bf16[3,512,128]{2,1,0:T(8,128)(2,1)}, bf16[4,512,128]{2,1,0:T(8,128)(2,1)}, bf16[1,512,128]{2,1,0:T(8,128)(2,1)}) custom-call(s32[8,56]{1,0:T(8,128)} %pattern_hbm.1, bf16[512,896]{1,0:T(8,128)(2,1)} %density_hbm.1), custom_call_target="tpu_custom_call" | custom-call | bytes 2492160 | tf_op jit(solution)/shard_map/pallas_call | solution.py:363
  2.9 3.0 %collective-permute-start = (bf16[4,512,128]{2,1,0:T(8,128)(2,1)}, bf16[4,512,128]{2,1,0:T(8,128)(2,1)}, u32[]{:S(2)}, u32[]{:S(2)}) collective-permute-start(bf16[4,512,128]{2,1,0:T(8,128)(2,1)} %get-tuple-element.37.x1a_ref), channel_id=1, source_target_pairs={{0,4},{4,0},{8,12},{12,8},{16,20},{20,16},{24,28},{28,24},{1,5},{5... | collective-permute-start | bytes 1572872 | tf_op jit(solution)/shard_map/ppermute | solution.py:333
  5.9 1.6 %collective-permute-start.2 = (bf16[4,512,128]{2,1,0:T(8,128)(2,1)}, bf16[4,512,128]{2,1,0:T(8,128)(2,1)}, u32[]{:S(2)}, u32[]{:S(2)}) collective-permute-start(bf16[4,512,128]{2,1,0:T(8,128)(2,1)} %get-tuple-element.39), channel_id=1, source_target_pairs={{0,8},{4,28},{8,16},{12,4},{16,24},{20,12},{24,0},{28,20},{1,9},{5... | collective-permute-start | bytes 1572872 | tf_op jit(solution)/shard_map/ppermute | solution.py:345
  7.5 2.6 %collective-permute-start.1 = (bf16[3,512,128]{2,1,0:T(8,128)(2,1)}, bf16[3,512,128]{2,1,0:T(8,128)(2,1)S(1)}, u32[]{:S(2)}, u32[]{:S(2)}) collective-permute-start(bf16[3,512,128]{2,1,0:T(8,128)(2,1)} %get-tuple-element.38.x1b_ref), channel_id=1, source_target_pairs={{0,4},{4,0},{8,12},{12,8},{16,20},{20,16},{24,28},{28,24},{1,5},{5... | collective-permute-start | bytes 1179656 | tf_op jit(solution)/shard_map/ppermute | solution.py:333
  10.1 2.4 %shard_map.104 = (bf16[192,512]{1,0:T(8,128)(2,1)}, bf16[7,128,192]{2,1,0:T(8,128)(2,1)}, f32[7,8,128]{2,1,0:T(8,128)}, f32[8,3584]{1,0:T(8,128)}) custom-call(s32[8,56]{1,0:T(8,128)} %pattern_hbm.1, s32[8]{0:T(128)} %refs_1_.1, s32[8]{0:T(128)} %refs_2_.1, s32[1,14]{1,0:T(1,128)} %refs_3_.1, s32[1,14]{1,0:T(1,128)} %refs_4_.1, bf16[32,512]{1,0:T(8,128)(2,1)} %bitcast.5, ...), custom_call_target="tpu_custom_call" | custom-call | flops 6000000000 | bytes 776112 | tf_op jit(solution)/shard_map/pallas_call | solution.py:363
  12.5 1.0 %copy-done.2 = bf16[7,128,192]{2,1,0:T(8,128)(2,1)S(1)} copy-done((bf16[7,128,192]{2,1,0:T(8,128)(2,1)S(1)}, bf16[7,128,192]{2,1,0:T(8,128)(2,1)}, u32[]{:S(2)}) %copy-start.2) | copy-done | bytes 344088
  13.5 0.9 %copy-done.4 = bf16[192,512]{1,0:T(8,128)(2,1)S(1)} copy-done((bf16[192,512]{1,0:T(8,128)(2,1)S(1)}, bf16[192,512]{1,0:T(8,128)(2,1)}, u32[]{:S(2)}) %copy-start.4) | copy-done | bytes 196632
  14.5 0.9 %copy-done.5 = f32[8,3584]{1,0:T(8,128)S(1)} copy-done((f32[8,3584]{1,0:T(8,128)S(1)}, f32[8,3584]{1,0:T(8,128)}, u32[]{:S(2)}) %copy-start.5) | copy-done | bytes 114712
  15.4 0.7 %copy-done.6 = f32[7,8,128]{2,1,0:T(8,128)S(1)} copy-done((f32[7,8,128]{2,1,0:T(8,128)S(1)}, f32[7,8,128]{2,1,0:T(8,128)}, u32[]{:S(2)}) %copy-start.6) | copy-done | bytes 28696
  16.1 1.2 %shard_map.105 = (bf16[7,512,512]{2,1,0:T(8,128)(2,1)S(1)}, f32[7,512,128]{2,1,0:T(8,128)S(1)}, bf16[192,512]{1,0:T(8,128)(2,1)S(1)}, bf16[7,128,192]{2,1,0:T(8,128)(2,1)S(1)}, f32[7,8,128]{2,1,0:T(8,128)S(1)}) custom-call(bf16[512,3584]{1,0:T(8,128)(2,1)S(1)} %copy-done, f32[8,3584]{1,0:T(8,128)S(1)} %copy-done.5, bf16[192,512]{1,0:T(8,128)(2,1)S(1)} %copy-done.4, ...), custom_call_target="tpu_custom_call" | custom-call | flops 1000000000 | bytes 10428416 | tf_op jit(solution)/shard_map/pallas_call | solution.py:363
  17.3 1.6 %collective-permute-done.refs_0_ = bf16[4,512,128]{2,1,0:T(8,128)(2,1)} collective-permute-done((bf16[4,512,128]{2,1,0:T(8,128)(2,1)}, bf16[4,512,128]{2,1,0:T(8,128)(2,1)}, u32[]{:S(2)}, u32[]{:S(2)}) %collective-permute-start) | collective-permute-done | bytes 524320 | tf_op jit(solution)/shard_map/ppermute | solution.py:333
  18.9 2.2 %collective-permute-start.3 = (bf16[4,512,128]{2,1,0:T(8,128)(2,1)}, bf16[4,512,128]{2,1,0:T(8,128)(2,1)S(1)}, u32[]{:S(2)}, u32[]{:S(2)}) collective-permute-start(bf16[4,512,128]{2,1,0:T(8,128)(2,1)} %collective-permute-done.refs_0_), channel_id=1, source_target_pairs={{0,8},{4,28},{8,16},{12,4},{16,24},{20,12},{24,0},{28,20},{1,9},{5... | collective-permute-start | bytes 1572872 | tf_op jit(solution)/shard_map/ppermute | solution.py:345
  21.4 3.2 %collective-permute-start.5 = (bf16[4,512,128]{2,1,0:T(8,128)(2,1)}, bf16[4,512,128]{2,1,0:T(8,128)(2,1)S(1)}, u32[]{:S(2)}, u32[]{:S(2)}) collective-permute-start(bf16[4,512,128]{2,1,0:T(8,128)(2,1)} %collective-permute-done.2.refs_2_), channel_id=1, source_target_pairs={{0,4},{4,0},{8,12},{12,8},{16,20},{20,16},{24,28},{28,24},{1,5},{5... | collective-permute-start | bytes 1572872 | tf_op jit(solution)/shard_map/ppermute | solution.py:333
  25.3 1.9 %collective-permute-done.1.refs_1_ = bf16[3,512,128]{2,1,0:T(8,128)(2,1)S(1)} collective-permute-done((bf16[3,512,128]{2,1,0:T(8,128)(2,1)}, bf16[3,512,128]{2,1,0:T(8,128)(2,1)S(1)}, u32[]{:S(2)}, u32[]{:S(2)}) %collective-permute-start.1) | collective-permute-done | bytes 393248 | tf_op jit(solution)/shard_map/ppermute | solution.py:333
  27.3 2.2 %collective-permute-start.4 = (bf16[2,512,128]{2,1,0:T(8,128)(2,1)S(1)}, bf16[2,512,128]{2,1,0:T(8,128)(2,1)S(1)}, u32[]{:S(2)}, u32[]{:S(2)}) collective-permute-start(bf16[2,512,128]{2,1,0:T(8,128)(2,1)S(1)} %slice.8), channel_id=1, source_target_pairs={{0,8},{4,28},{8,16},{12,4},{16,24},{20,12},{24,0},{28,20},{1,9},{5... | collective-permute-start | bytes 786440 | tf_op jit(solution)/shard_map/ppermute | solution.py:345
  29.5 2.1 %shard_map.108.before_ref = f32[7,512,128]{2,1,0:T(8,128)S(1)} custom-call(bf16[7,512,512]{2,1,0:T(8,128)(2,1)S(1)} %get-tuple-element.35.squares_ref, f32[7,512,128]{2,1,0:T(8,128)S(1)} %shard_map.107.before_ref, bf16[4,512,128]{2,1,0:T(8,128)(2,1)} %collective-permute-done.refs_0_, bf16[3,512,128]{2,1,0:T(8,128)(2,1)S(1)} %collective-permute-done.1.refs_1_, ...), custom_call_target="tpu_custom_call" | custom-call | flops 3000000000 | bytes 8781824 | tf_op jit(solution)/shard_map/pallas_call | solution.py:363
  31.6 4.4 %collective-permute-done.3.refs_0_ = bf16[4,512,128]{2,1,0:T(8,128)(2,1)S(1)} collective-permute-done((bf16[4,512,128]{2,1,0:T(8,128)(2,1)}, bf16[4,512,128]{2,1,0:T(8,128)(2,1)S(1)}, u32[]{:S(2)}, u32[]{:S(2)}) %collective-permute-start.3) | collective-permute-done | bytes 524320 | tf_op jit(solution)/shard_map/ppermute | solution.py:345
  36.1 1.0 %collective-permute-start.6 = (bf16[4,512,128]{2,1,0:T(8,128)(2,1)S(1)}, bf16[4,512,128]{2,1,0:T(8,128)(2,1)S(1)}, u32[]{:S(2)}, u32[]{:S(2)}) collective-permute-start(bf16[4,512,128]{2,1,0:T(8,128)(2,1)S(1)} %collective-permute-done.3.refs_0_), channel_id=1, source_target_pairs={{0,4},{4,0},{8,12},{12,8},{16,20},{20,16},{24,28},{28,24},{1,5},{5... | collective-permute-start | bytes 1572872 | tf_op jit(solution)/shard_map/ppermute | solution.py:333
  37.4 1.6 %collective-permute-start.9 = (bf16[1,512,128]{2,1,0:T(8,128)(2,1)S(1)}, bf16[1,512,128]{2,1,0:T(8,128)(2,1)S(1)}, u32[]{:S(2)}, u32[]{:S(2)}) collective-permute-start(bf16[1,512,128]{2,1,0:T(8,128)(2,1)S(1)} %copy-done.7), channel_id=1, source_target_pairs={{0,8},{4,28},{8,16},{12,4},{16,24},{20,12},{24,0},{28,20},{1,9},{5... | collective-permute-start | bytes 393224 | tf_op jit(solution)/shard_map/ppermute | solution.py:345
  39.0 1.9 %collective-permute-done.4.refs_0_ = bf16[2,512,128]{2,1,0:T(8,128)(2,1)S(1)} collective-permute-done((bf16[2,512,128]{2,1,0:T(8,128)(2,1)S(1)}, bf16[2,512,128]{2,1,0:T(8,128)(2,1)S(1)}, u32[]{:S(2)}, u32[]{:S(2)}) %collective-permute-start.4) | collective-permute-done | bytes 262176 | tf_op jit(solution)/shard_map/ppermute | solution.py:345
  40.9 1.8 %collective-permute-start.8 = (bf16[1,512,128]{2,1,0:T(8,128)(2,1)S(1)}, bf16[1,512,128]{2,1,0:T(8,128)(2,1)S(1)}, u32[]{:S(2)}, u32[]{:S(2)}) collective-permute-start(bf16[1,512,128]{2,1,0:T(8,128)(2,1)S(1)} %slice.9), channel_id=1, source_target_pairs={{0,4},{4,0},{8,12},{12,8},{16,20},{20,16},{24,28},{28,24},{1,5},{5... | collective-permute-start | bytes 393224 | tf_op jit(solution)/shard_map/ppermute | solution.py:333
  43.7 6.6 %collective-permute-done.6.x2p_ref = bf16[4,512,128]{2,1,0:T(8,128)(2,1)S(1)} collective-permute-done((bf16[4,512,128]{2,1,0:T(8,128)(2,1)S(1)}, bf16[4,512,128]{2,1,0:T(8,128)(2,1)S(1)}, u32[]{:S(2)}, u32[]{:S(2)}) %collective-permute-start.6) | collective-permute-done | bytes 524320 | tf_op jit(solution)/shard_map/ppermute | solution.py:333
  50.3 1.2 %collective-permute-done.7.z3_ref = bf16[4,512,128]{2,1,0:T(8,128)(2,1)S(1)} collective-permute-done((bf16[4,512,128]{2,1,0:T(8,128)(2,1)S(1)}, bf16[4,512,128]{2,1,0:T(8,128)(2,1)S(1)}, u32[]{:S(2)}, u32[]{:S(2)}) %collective-permute-start.7) | collective-permute-done | bytes 524320 | tf_op jit(solution)/shard_map/ppermute | solution.py:345
  51.5 1.2 %shard_map.111 = (bf16[512,640]{1,0:T(8,128)(2,1)S(1)}, f32[512,192]{1,0:T(8,128)S(1)}, f32[2,512,128]{2,1,0:T(8,128)S(1)}) custom-call(f32[7,8,128]{2,1,0:T(8,128)S(1)} %get-tuple-element.34.mask_ref, bf16[7,512,512]{2,1,0:T(8,128)(2,1)S(1)} %get-tuple-element.35.squares_ref, f32[7,512,128]{2,1,0:T(8,128)S(1)} %shard_map.110.before_ref, ...), custom_call_target="tpu_custom_call" | custom-call | bytes 8499200 | tf_op jit(solution)/shard_map/pallas_call | solution.py:363
  52.9 0.8 %shard_map.112 = (bf16[512,256]{1,0:T(8,128)(2,1)S(1)}, f32[128,192]{1,0:T(8,128)S(1)}, bf16[32,192]{1,0:T(8,128)(2,1)S(1)}, bf16[32,192]{1,0:T(8,128)(2,1)S(1)}) custom-call(f32[7,8,128]{2,1,0:T(8,128)S(1)} %get-tuple-element.34.mask_ref, bf16[7,512,512]{2,1,0:T(8,128)(2,1)S(1)} %get-tuple-element.35.squares_ref, ...), custom_call_target="tpu_custom_call" | custom-call | bytes 5804032 | tf_op jit(solution)/shard_map/pallas_call | solution.py:363
  53.7 0.8 %collective-permute-start.10 = (bf16[32,192]{1,0:T(8,128)(2,1)S(1)}, bf16[32,192]{1,0:T(8,128)(2,1)S(1)}, u32[]{:S(2)}, u32[]{:S(2)}) collective-permute-start(bf16[32,192]{1,0:T(8,128)(2,1)S(1)} %get-tuple-element.53), channel_id=1, source_target_pairs={{0,4},{4,0},{8,12},{12,8},{16,20},{20,16},{24,28},{28,24},{1,5},{5... | collective-permute-start | bytes 36872 | tf_op jit(solution)/shard_map/ppermute | solution.py:333
  54.5 3.8 %collective-permute-start.11 = (bf16[32,192]{1,0:T(8,128)(2,1)S(1)}, bf16[32,192]{1,0:T(8,128)(2,1)S(1)}, u32[]{:S(2)}, u32[]{:S(2)}) collective-permute-start(bf16[32,192]{1,0:T(8,128)(2,1)S(1)} %get-tuple-element.54), channel_id=1, source_target_pairs={{0,28},{4,8},{8,4},{12,16},{16,12},{20,24},{24,20},{28,0},{1,29},{... | collective-permute-start | bytes 36872 | tf_op jit(solution)/shard_map/ppermute | solution.py:339
  58.3 1.1 %shard_map.113 = bf16[512,896]{1,0:T(8,128)(2,1)} custom-call(bf16[512,640]{1,0:T(8,128)(2,1)S(1)} %get-tuple-element.43.inner_ref, bf16[512,256]{1,0:T(8,128)(2,1)S(1)} %get-tuple-element.50.edges_ref), custom_call_target="tpu_custom_call" | custom-call | bytes 1835008 | tf_op jit(solution)/shard_map/pallas_call | solution.py:363
  59.3 1.6 %collective-permute-done.11.got_b_ref = bf16[32,192]{1,0:T(8,128)(2,1)S(1)} collective-permute-done((bf16[32,192]{1,0:T(8,128)(2,1)S(1)}, bf16[32,192]{1,0:T(8,128)(2,1)S(1)}, u32[]{:S(2)}, u32[]{:S(2)}) %collective-permute-start.11) | collective-permute-done | bytes 12320 | tf_op jit(solution)/shard_map/ppermute | solution.py:339
  61.2 1.6 %collective-permute-start.13 = (bf16[32,128]{1,0:T(8,128)(2,1)S(1)}, bf16[32,128]{1,0:T(8,128)(2,1)S(1)}, u32[]{:S(2)}, u32[]{:S(2)}) collective-permute-start(bf16[32,128]{1,0:T(8,128)(2,1)S(1)} %get-tuple-element.57), channel_id=1, source_target_pairs={{0,3},{1,2},{2,1},{3,0},{4,7},{5,6},{6,5},{7,4},{8,11},{9,10},{10,... | collective-permute-start | bytes 24584 | tf_op jit(solution)/shard_map/ppermute | solution.py:339
  62.8 1.5 %collective-permute-done.13.got_b_ref = bf16[32,128]{1,0:T(8,128)(2,1)S(1)} collective-permute-done((bf16[32,128]{1,0:T(8,128)(2,1)S(1)}, bf16[32,128]{1,0:T(8,128)(2,1)S(1)}, u32[]{:S(2)}, u32[]{:S(2)}) %collective-permute-start.13) | collective-permute-done | bytes 8224 | tf_op jit(solution)/shard_map/ppermute | solution.py:339
  64.3 0.7 %shard_map.115 = f32[128,128]{1,0:T(8,128)} custom-call(f32[128,128]{1,0:T(8,128)S(1)} %get-tuple-element.55.center_ref, bf16[32,128]{1,0:T(8,128)(2,1)S(1)} %collective-permute-done.12.got_a_ref, bf16[32,128]{1,0:T(8,128)(2,1)S(1)} %collective-permute-done.13.got_b_ref), custom_call_target="tpu_custom_call" | custom-call | bytes 147456 | tf_op jit(solution)/shard_map/pallas_call | solution.py:363
  (26 shorter events, 2.9 us)
Async XLA Ops:
  2.9 16.0 %collective-permute-start = (bf16[4,512,128]{2,1,0:T(8,128)(2,1)}, bf16[4,512,128]{2,1,0:T(8,128)(2,1)}, u32[]{:S(2)}, u32[]{:S(2)}) collective-permute-start(bf16[4,512,128]{2,1,0:T(8,128)(2,1)} %get-tuple-element.37.x1a_ref), channel_id=1, source_target_pairs={{0,4},{4,0},{8,12},{12,8},{16,20},{20,16},{24,28},{28,24},{1,5},{5... | collective-permute-start | bytes 1572872 | tf_op jit(solution)/shard_map/ppermute | solution.py:333
  5.9 15.6 %collective-permute-start.2 = (bf16[4,512,128]{2,1,0:T(8,128)(2,1)}, bf16[4,512,128]{2,1,0:T(8,128)(2,1)}, u32[]{:S(2)}, u32[]{:S(2)}) collective-permute-start(bf16[4,512,128]{2,1,0:T(8,128)(2,1)} %get-tuple-element.39), channel_id=1, source_target_pairs={{0,8},{4,28},{8,16},{12,4},{16,24},{20,12},{24,0},{28,20},{1,9},{5... | collective-permute-start | bytes 1572872 | tf_op jit(solution)/shard_map/ppermute | solution.py:345
  7.5 19.8 %collective-permute-start.1 = (bf16[3,512,128]{2,1,0:T(8,128)(2,1)}, bf16[3,512,128]{2,1,0:T(8,128)(2,1)S(1)}, u32[]{:S(2)}, u32[]{:S(2)}) collective-permute-start(bf16[3,512,128]{2,1,0:T(8,128)(2,1)} %get-tuple-element.38.x1b_ref), channel_id=1, source_target_pairs={{0,4},{4,0},{8,12},{12,8},{16,20},{20,16},{24,28},{28,24},{1,5},{5... | collective-permute-start | bytes 1179656 | tf_op jit(solution)/shard_map/ppermute | solution.py:333
  10.1 2.5 %copy-start = (bf16[512,3584]{1,0:T(8,128)(2,1)S(1)}, bf16[512,3584]{1,0:T(8,128)(2,1)}, u32[]{:S(2)}) copy-start(bf16[512,3584]{1,0:T(8,128)(2,1)} %p2_ref.1) | copy-start | bytes 11010052
  12.5 1.0 %copy-start.2 = (bf16[7,128,192]{2,1,0:T(8,128)(2,1)S(1)}, bf16[7,128,192]{2,1,0:T(8,128)(2,1)}, u32[]{:S(2)}) copy-start(bf16[7,128,192]{2,1,0:T(8,128)(2,1)} %get-tuple-element.32.refs_1_) | copy-start | bytes 1032196
  13.5 0.9 %copy-start.4 = (bf16[192,512]{1,0:T(8,128)(2,1)S(1)}, bf16[192,512]{1,0:T(8,128)(2,1)}, u32[]{:S(2)}) copy-start(bf16[192,512]{1,0:T(8,128)(2,1)} %get-tuple-element.31.refs_0_) | copy-start | bytes 589828
  14.5 0.9 %copy-start.5 = (f32[8,3584]{1,0:T(8,128)S(1)}, f32[8,3584]{1,0:T(8,128)}, u32[]{:S(2)}) copy-start(f32[8,3584]{1,0:T(8,128)} %get-tuple-element.30.wide_ref) | copy-start | bytes 344068
  15.4 0.7 %copy-start.6 = (f32[7,8,128]{2,1,0:T(8,128)S(1)}, f32[7,8,128]{2,1,0:T(8,128)}, u32[]{:S(2)}) copy-start(f32[7,8,128]{2,1,0:T(8,128)} %get-tuple-element.33.refs_2_) | copy-start | bytes 86020
  16.1 8.5 %copy-start.1 = (bf16[4,512,128]{2,1,0:T(8,128)(2,1)S(1)}, bf16[4,512,128]{2,1,0:T(8,128)(2,1)}, u32[]{:S(2)}) copy-start(bf16[4,512,128]{2,1,0:T(8,128)(2,1)} %get-tuple-element.37.x1a_ref) | copy-start | bytes 1572868
  16.1 8.5 %copy-start.3 = (bf16[3,512,128]{2,1,0:T(8,128)(2,1)S(1)}, bf16[3,512,128]{2,1,0:T(8,128)(2,1)}, u32[]{:S(2)}) copy-start(bf16[3,512,128]{2,1,0:T(8,128)(2,1)} %get-tuple-element.38.x1b_ref) | copy-start | bytes 1179652
  18.9 17.1 %collective-permute-start.3 = (bf16[4,512,128]{2,1,0:T(8,128)(2,1)}, bf16[4,512,128]{2,1,0:T(8,128)(2,1)S(1)}, u32[]{:S(2)}, u32[]{:S(2)}) collective-permute-start(bf16[4,512,128]{2,1,0:T(8,128)(2,1)} %collective-permute-done.refs_0_), channel_id=1, source_target_pairs={{0,8},{4,28},{8,16},{12,4},{16,24},{20,12},{24,0},{28,20},{1,9},{5... | collective-permute-start | bytes 1572872 | tf_op jit(solution)/shard_map/ppermute | solution.py:345
  21.4 21.7 %collective-permute-start.5 = (bf16[4,512,128]{2,1,0:T(8,128)(2,1)}, bf16[4,512,128]{2,1,0:T(8,128)(2,1)S(1)}, u32[]{:S(2)}, u32[]{:S(2)}) collective-permute-start(bf16[4,512,128]{2,1,0:T(8,128)(2,1)} %collective-permute-done.2.refs_2_), channel_id=1, source_target_pairs={{0,4},{4,0},{8,12},{12,8},{16,20},{20,16},{24,28},{28,24},{1,5},{5... | collective-permute-start | bytes 1572872 | tf_op jit(solution)/shard_map/ppermute | solution.py:333
  27.3 10.1 %copy-start.7 = (bf16[1,512,128]{2,1,0:T(8,128)(2,1)S(1)}, bf16[1,512,128]{2,1,0:T(8,128)(2,1)}, u32[]{:S(2)}) copy-start(bf16[1,512,128]{2,1,0:T(8,128)(2,1)} %get-tuple-element.47) | copy-start | bytes 393220
  27.3 13.6 %collective-permute-start.4 = (bf16[2,512,128]{2,1,0:T(8,128)(2,1)S(1)}, bf16[2,512,128]{2,1,0:T(8,128)(2,1)S(1)}, u32[]{:S(2)}, u32[]{:S(2)}) collective-permute-start(bf16[2,512,128]{2,1,0:T(8,128)(2,1)S(1)} %slice.8), channel_id=1, source_target_pairs={{0,8},{4,28},{8,16},{12,4},{16,24},{20,12},{24,0},{28,20},{1,9},{5... | collective-permute-start | bytes 786440 | tf_op jit(solution)/shard_map/ppermute | solution.py:345
  36.1 14.2 %collective-permute-start.6 = (bf16[4,512,128]{2,1,0:T(8,128)(2,1)S(1)}, bf16[4,512,128]{2,1,0:T(8,128)(2,1)S(1)}, u32[]{:S(2)}, u32[]{:S(2)}) collective-permute-start(bf16[4,512,128]{2,1,0:T(8,128)(2,1)S(1)} %collective-permute-done.3.refs_0_), channel_id=1, source_target_pairs={{0,4},{4,0},{8,12},{12,8},{16,20},{20,16},{24,28},{28,24},{1,5},{5... | collective-permute-start | bytes 1572872 | tf_op jit(solution)/shard_map/ppermute | solution.py:333
  37.1 14.5 %collective-permute-start.7 = (bf16[4,512,128]{2,1,0:T(8,128)(2,1)S(1)}, bf16[4,512,128]{2,1,0:T(8,128)(2,1)S(1)}, u32[]{:S(2)}, u32[]{:S(2)}) collective-permute-start(bf16[4,512,128]{2,1,0:T(8,128)(2,1)S(1)} %collective-permute-done.3.refs_0_), channel_id=1, source_target_pairs={{0,8},{4,28},{8,16},{12,4},{16,24},{20,12},{24,0},{28,20},{1,9},{5... | collective-permute-start | bytes 1572872 | tf_op jit(solution)/shard_map/ppermute | solution.py:345
  37.4 15.5 %collective-permute-start.9 = (bf16[1,512,128]{2,1,0:T(8,128)(2,1)S(1)}, bf16[1,512,128]{2,1,0:T(8,128)(2,1)S(1)}, u32[]{:S(2)}, u32[]{:S(2)}) collective-permute-start(bf16[1,512,128]{2,1,0:T(8,128)(2,1)S(1)} %copy-done.7), channel_id=1, source_target_pairs={{0,8},{4,28},{8,16},{12,4},{16,24},{20,12},{24,0},{28,20},{1,9},{5... | collective-permute-start | bytes 393224 | tf_op jit(solution)/shard_map/ppermute | solution.py:345
  40.9 12.1 %collective-permute-start.8 = (bf16[1,512,128]{2,1,0:T(8,128)(2,1)S(1)}, bf16[1,512,128]{2,1,0:T(8,128)(2,1)S(1)}, u32[]{:S(2)}, u32[]{:S(2)}) collective-permute-start(bf16[1,512,128]{2,1,0:T(8,128)(2,1)S(1)} %slice.9), channel_id=1, source_target_pairs={{0,4},{4,0},{8,12},{12,8},{16,20},{20,16},{24,28},{28,24},{1,5},{5... | collective-permute-start | bytes 393224 | tf_op jit(solution)/shard_map/ppermute | solution.py:333
  53.7 5.7 %collective-permute-start.10 = (bf16[32,192]{1,0:T(8,128)(2,1)S(1)}, bf16[32,192]{1,0:T(8,128)(2,1)S(1)}, u32[]{:S(2)}, u32[]{:S(2)}) collective-permute-start(bf16[32,192]{1,0:T(8,128)(2,1)S(1)} %get-tuple-element.53), channel_id=1, source_target_pairs={{0,4},{4,0},{8,12},{12,8},{16,20},{20,16},{24,28},{28,24},{1,5},{5... | collective-permute-start | bytes 36872 | tf_op jit(solution)/shard_map/ppermute | solution.py:333
  54.5 6.4 %collective-permute-start.11 = (bf16[32,192]{1,0:T(8,128)(2,1)S(1)}, bf16[32,192]{1,0:T(8,128)(2,1)S(1)}, u32[]{:S(2)}, u32[]{:S(2)}) collective-permute-start(bf16[32,192]{1,0:T(8,128)(2,1)S(1)} %get-tuple-element.54), channel_id=1, source_target_pairs={{0,28},{4,8},{8,4},{12,16},{16,12},{20,24},{24,20},{28,0},{1,29},{... | collective-permute-start | bytes 36872 | tf_op jit(solution)/shard_map/ppermute | solution.py:339
  61.1 1.7 %collective-permute-start.12 = (bf16[32,128]{1,0:T(8,128)(2,1)S(1)}, bf16[32,128]{1,0:T(8,128)(2,1)S(1)}, u32[]{:S(2)}, u32[]{:S(2)}) collective-permute-start(bf16[32,128]{1,0:T(8,128)(2,1)S(1)} %get-tuple-element.56), channel_id=1, source_target_pairs={{0,1},{1,0},{2,3},{3,2},{4,5},{5,4},{6,7},{7,6},{8,9},{9,8},{10,11... | collective-permute-start | bytes 24584 | tf_op jit(solution)/shard_map/ppermute | solution.py:333
  61.2 3.1 %collective-permute-start.13 = (bf16[32,128]{1,0:T(8,128)(2,1)S(1)}, bf16[32,128]{1,0:T(8,128)(2,1)S(1)}, u32[]{:S(2)}, u32[]{:S(2)}) collective-permute-start(bf16[32,128]{1,0:T(8,128)(2,1)S(1)} %get-tuple-element.57), channel_id=1, source_target_pairs={{0,3},{1,2},{2,1},{3,0},{4,7},{5,6},{6,5},{7,4},{8,11},{9,10},{10,... | collective-permute-start | bytes 24584 | tf_op jit(solution)/shard_map/ppermute | solution.py:339

commit v7 on v6

--- a/solution.py
+++ b/solution.py
@@ -460,7 +460,7 @@
     x2p = swap_partner(after(z2p, summed), "row")
     z3 = shift_level(z2p)
     summed = stage(summed, [(1, [(j + 1, z2p, j) for j in range(NEAR)])])
-    x2q = swap_partner(after(z2q[: AHEAD - NEAR], z2p), "row")
+    x2q = swap_partner(z2q[: AHEAD - NEAR], "row")
     summed = stage(
         summed,
         [

time: 65.4 us -> 65.4 us (level)
  no operation moved by 1% of the time
where the time goes in v7:
time: 65.4 us; the launch traced here: 65.1 us
  starting transfers between devices  25.7 us (39%)
  waiting for transfers between devices  21.2 us (32%)
  Pallas kernels  13.7 us (21%)
  local copies, waits for them, and re-layouts  3.63 us (6%)
  between operations  0.77 us (1%)
    pallas_call x12, Pallas kernels, call(): pl.pallas_call(kernel, out_shape=shapes, in_specs=specs, out_specs=[HBM i...  13.7 us
    ppermute x7, starting transfers between devices, swap_partner(): return lax.ppermute(value, axis, [(s, s ^ 1) for s in range(count)])  12.3 us
    ppermute x7, waiting for transfers between devices, swap_partner(): return lax.ppermute(value, axis, [(s, s ^ 1) for s in range(count)])  10.2 us
    ppermute x5, waiting for transfers between devices, shift_level(): return lax.ppermute(value, 'row', pairs)  7.99 us
    ppermute x5, starting transfers between devices, shift_level(): return lax.ppermute(value, 'row', pairs)  7.92 us
    ppermute x2, starting transfers between devices, swap_other(): return lax.ppermute(value, axis, pairs)  5.43 us
    unnamed x16, local copies, waits for them, and re-layouts  3.6 us
    ppermute x2, waiting for transfers between devices, swap_other(): return lax.ppermute(value, axis, pairs)  3.06 us
  transfers between devices with their start and end apart: 14, of which 10 were waited for; matrix products, arithmetic and copies ran while one was open for 0% of the time, Pallas kernels for 15%

profile of v7, /device:TPU:0, one launch (start us, length us, event | category | flops | bytes accessed | tf_op | source)
XLA Modules:
  0.0 65.1 jit_solution(15798447320610104319)
XLA Ops:
  0.6 2.3 %shard_map.106 = (bf16[4,512,128]{2,1,0:T(8,128)(2,1)}, bf16[3,512,128]{2,1,0:T(8,128)(2,1)}, bf16[4,512,128]{2,1,0:T(8,128)(2,1)}, bf16[1,512,128]{2,1,0:T(8,128)(2,1)}) custom-call(s32[8,56]{1,0:T(8,128)} %pattern_hbm.1, bf16[512,896]{1,0:T(8,128)(2,1)} %density_hbm.1), custom_call_target="tpu_custom_call" | custom-call | bytes 2492160 | tf_op jit(solution)/shard_map/pallas_call | solution.py:363
  2.9 3.0 %collective-permute-start = (bf16[4,512,128]{2,1,0:T(8,128)(2,1)}, bf16[4,512,128]{2,1,0:T(8,128)(2,1)}, u32[]{:S(2)}, u32[]{:S(2)}) collective-permute-start(bf16[4,512,128]{2,1,0:T(8,128)(2,1)} %get-tuple-element.36.x1a_ref), channel_id=1, source_target_pairs={{0,4},{4,0},{8,12},{12,8},{16,20},{20,16},{24,28},{28,24},{1,5},{5... | collective-permute-start | bytes 1572872 | tf_op jit(solution)/shard_map/ppermute | solution.py:333
  5.9 1.6 %collective-permute-start.2 = (bf16[4,512,128]{2,1,0:T(8,128)(2,1)}, bf16[4,512,128]{2,1,0:T(8,128)(2,1)}, u32[]{:S(2)}, u32[]{:S(2)}) collective-permute-start(bf16[4,512,128]{2,1,0:T(8,128)(2,1)} %get-tuple-element.38), channel_id=1, source_target_pairs={{0,8},{4,28},{8,16},{12,4},{16,24},{20,12},{24,0},{28,20},{1,9},{5... | collective-permute-start | bytes 1572872 | tf_op jit(solution)/shard_map/ppermute | solution.py:345
  7.5 2.6 %collective-permute-start.1 = (bf16[3,512,128]{2,1,0:T(8,128)(2,1)}, bf16[3,512,128]{2,1,0:T(8,128)(2,1)S(1)}, u32[]{:S(2)}, u32[]{:S(2)}) collective-permute-start(bf16[3,512,128]{2,1,0:T(8,128)(2,1)} %get-tuple-element.37.x1b_ref), channel_id=1, source_target_pairs={{0,4},{4,0},{8,12},{12,8},{16,20},{20,16},{24,28},{28,24},{1,5},{5... | collective-permute-start | bytes 1179656 | tf_op jit(solution)/shard_map/ppermute | solution.py:333
  10.1 2.4 %shard_map.104 = (bf16[192,512]{1,0:T(8,128)(2,1)}, bf16[7,128,192]{2,1,0:T(8,128)(2,1)}, f32[7,8,128]{2,1,0:T(8,128)}, f32[8,3584]{1,0:T(8,128)}) custom-call(s32[8,56]{1,0:T(8,128)} %pattern_hbm.1, s32[8]{0:T(128)} %refs_1_.1, s32[8]{0:T(128)} %refs_2_.1, s32[1,14]{1,0:T(1,128)} %refs_3_.1, s32[1,14]{1,0:T(1,128)} %refs_4_.1, bf16[32,512]{1,0:T(8,128)(2,1)} %bitcast.5, ...), custom_call_target="tpu_custom_call" | custom-call | flops 6000000000 | bytes 776112 | tf_op jit(solution)/shard_map/pallas_call | solution.py:363
  12.5 1.0 %copy-done.2 = bf16[7,128,192]{2,1,0:T(8,128)(2,1)S(1)} copy-done((bf16[7,128,192]{2,1,0:T(8,128)(2,1)S(1)}, bf16[7,128,192]{2,1,0:T(8,128)(2,1)}, u32[]{:S(2)}) %copy-start.2) | copy-done | bytes 344088
  13.5 0.9 %copy-done.4 = bf16[192,512]{1,0:T(8,128)(2,1)S(1)} copy-done((bf16[192,512]{1,0:T(8,128)(2,1)S(1)}, bf16[192,512]{1,0:T(8,128)(2,1)}, u32[]{:S(2)}) %copy-start.4) | copy-done | bytes 196632
  14.5 0.9 %copy-done.5 = f32[8,3584]{1,0:T(8,128)S(1)} copy-done((f32[8,3584]{1,0:T(8,128)S(1)}, f32[8,3584]{1,0:T(8,128)}, u32[]{:S(2)}) %copy-start.5) | copy-done | bytes 114712
  15.4 0.7 %copy-done.6 = f32[7,8,128]{2,1,0:T(8,128)S(1)} copy-done((f32[7,8,128]{2,1,0:T(8,128)S(1)}, f32[7,8,128]{2,1,0:T(8,128)}, u32[]{:S(2)}) %copy-start.6) | copy-done | bytes 28696
  16.1 1.2 %shard_map.105 = (bf16[7,512,512]{2,1,0:T(8,128)(2,1)S(1)}, f32[7,512,128]{2,1,0:T(8,128)S(1)}, bf16[192,512]{1,0:T(8,128)(2,1)S(1)}, bf16[7,128,192]{2,1,0:T(8,128)(2,1)S(1)}, f32[7,8,128]{2,1,0:T(8,128)S(1)}) custom-call(bf16[512,3584]{1,0:T(8,128)(2,1)S(1)} %copy-done, f32[8,3584]{1,0:T(8,128)S(1)} %copy-done.5, bf16[192,512]{1,0:T(8,128)(2,1)S(1)} %copy-done.4, ...), custom_call_target="tpu_custom_call" | custom-call | flops 1000000000 | bytes 10428416 | tf_op jit(solution)/shard_map/pallas_call | solution.py:363
  17.3 1.6 %collective-permute-done.refs_0_ = bf16[4,512,128]{2,1,0:T(8,128)(2,1)} collective-permute-done((bf16[4,512,128]{2,1,0:T(8,128)(2,1)}, bf16[4,512,128]{2,1,0:T(8,128)(2,1)}, u32[]{:S(2)}, u32[]{:S(2)}) %collective-permute-start) | collective-permute-done | bytes 524320 | tf_op jit(solution)/shard_map/ppermute | solution.py:333
  18.9 2.2 %collective-permute-start.3 = (bf16[4,512,128]{2,1,0:T(8,128)(2,1)}, bf16[4,512,128]{2,1,0:T(8,128)(2,1)S(1)}, u32[]{:S(2)}, u32[]{:S(2)}) collective-permute-start(bf16[4,512,128]{2,1,0:T(8,128)(2,1)} %collective-permute-done.refs_0_), channel_id=1, source_target_pairs={{0,8},{4,28},{8,16},{12,4},{16,24},{20,12},{24,0},{28,20},{1,9},{5... | collective-permute-start | bytes 1572872 | tf_op jit(solution)/shard_map/ppermute | solution.py:345
  21.4 3.2 %collective-permute-start.5 = (bf16[4,512,128]{2,1,0:T(8,128)(2,1)}, bf16[4,512,128]{2,1,0:T(8,128)(2,1)S(1)}, u32[]{:S(2)}, u32[]{:S(2)}) collective-permute-start(bf16[4,512,128]{2,1,0:T(8,128)(2,1)} %collective-permute-done.2.refs_2_), channel_id=1, source_target_pairs={{0,4},{4,0},{8,12},{12,8},{16,20},{20,16},{24,28},{28,24},{1,5},{5... | collective-permute-start | bytes 1572872 | tf_op jit(solution)/shard_map/ppermute | solution.py:333
  25.3 1.9 %collective-permute-done.1.refs_1_ = bf16[3,512,128]{2,1,0:T(8,128)(2,1)S(1)} collective-permute-done((bf16[3,512,128]{2,1,0:T(8,128)(2,1)}, bf16[3,512,128]{2,1,0:T(8,128)(2,1)S(1)}, u32[]{:S(2)}, u32[]{:S(2)}) %collective-permute-start.1) | collective-permute-done | bytes 393248 | tf_op jit(solution)/shard_map/ppermute | solution.py:333
  27.3 2.2 %collective-permute-start.4 = (bf16[2,512,128]{2,1,0:T(8,128)(2,1)S(1)}, bf16[2,512,128]{2,1,0:T(8,128)(2,1)S(1)}, u32[]{:S(2)}, u32[]{:S(2)}) collective-permute-start(bf16[2,512,128]{2,1,0:T(8,128)(2,1)S(1)} %slice.8), channel_id=1, source_target_pairs={{0,8},{4,28},{8,16},{12,4},{16,24},{20,12},{24,0},{28,20},{1,9},{5... | collective-permute-start | bytes 786440 | tf_op jit(solution)/shard_map/ppermute | solution.py:345
  29.5 2.1 %shard_map.108.before_ref = f32[7,512,128]{2,1,0:T(8,128)S(1)} custom-call(bf16[7,512,512]{2,1,0:T(8,128)(2,1)S(1)} %get-tuple-element.34.squares_ref, f32[7,512,128]{2,1,0:T(8,128)S(1)} %shard_map.107.before_ref, bf16[4,512,128]{2,1,0:T(8,128)(2,1)} %collective-permute-done.refs_0_, bf16[3,512,128]{2,1,0:T(8,128)(2,1)S(1)} %collective-permute-done.1.refs_1_, ...), custom_call_target="tpu_custom_call" | custom-call | flops 3000000000 | bytes 8781824 | tf_op jit(solution)/shard_map/pallas_call | solution.py:363
  31.6 4.4 %collective-permute-done.3.refs_0_ = bf16[4,512,128]{2,1,0:T(8,128)(2,1)S(1)} collective-permute-done((bf16[4,512,128]{2,1,0:T(8,128)(2,1)}, bf16[4,512,128]{2,1,0:T(8,128)(2,1)S(1)}, u32[]{:S(2)}, u32[]{:S(2)}) %collective-permute-start.3) | collective-permute-done | bytes 524320 | tf_op jit(solution)/shard_map/ppermute | solution.py:345
  36.1 1.0 %collective-permute-start.6 = (bf16[4,512,128]{2,1,0:T(8,128)(2,1)S(1)}, bf16[4,512,128]{2,1,0:T(8,128)(2,1)S(1)}, u32[]{:S(2)}, u32[]{:S(2)}) collective-permute-start(bf16[4,512,128]{2,1,0:T(8,128)(2,1)S(1)} %collective-permute-done.3.refs_0_), channel_id=1, source_target_pairs={{0,4},{4,0},{8,12},{12,8},{16,20},{20,16},{24,28},{28,24},{1,5},{5... | collective-permute-start | bytes 1572872 | tf_op jit(solution)/shard_map/ppermute | solution.py:333
  37.4 1.6 %collective-permute-start.9 = (bf16[1,512,128]{2,1,0:T(8,128)(2,1)S(1)}, bf16[1,512,128]{2,1,0:T(8,128)(2,1)S(1)}, u32[]{:S(2)}, u32[]{:S(2)}) collective-permute-start(bf16[1,512,128]{2,1,0:T(8,128)(2,1)S(1)} %copy-done.7), channel_id=1, source_target_pairs={{0,8},{4,28},{8,16},{12,4},{16,24},{20,12},{24,0},{28,20},{1,9},{5... | collective-permute-start | bytes 393224 | tf_op jit(solution)/shard_map/ppermute | solution.py:345
  39.0 1.9 %collective-permute-done.4.refs_0_ = bf16[2,512,128]{2,1,0:T(8,128)(2,1)S(1)} collective-permute-done((bf16[2,512,128]{2,1,0:T(8,128)(2,1)S(1)}, bf16[2,512,128]{2,1,0:T(8,128)(2,1)S(1)}, u32[]{:S(2)}, u32[]{:S(2)}) %collective-permute-start.4) | collective-permute-done | bytes 262176 | tf_op jit(solution)/shard_map/ppermute | solution.py:345
  40.9 1.8 %collective-permute-start.8 = (bf16[1,512,128]{2,1,0:T(8,128)(2,1)S(1)}, bf16[1,512,128]{2,1,0:T(8,128)(2,1)S(1)}, u32[]{:S(2)}, u32[]{:S(2)}) collective-permute-start(bf16[1,512,128]{2,1,0:T(8,128)(2,1)S(1)} %slice.9), channel_id=1, source_target_pairs={{0,4},{4,0},{8,12},{12,8},{16,20},{20,16},{24,28},{28,24},{1,5},{5... | collective-permute-start | bytes 393224 | tf_op jit(solution)/shard_map/ppermute | solution.py:333
  43.7 6.6 %collective-permute-done.6.x2p_ref = bf16[4,512,128]{2,1,0:T(8,128)(2,1)S(1)} collective-permute-done((bf16[4,512,128]{2,1,0:T(8,128)(2,1)S(1)}, bf16[4,512,128]{2,1,0:T(8,128)(2,1)S(1)}, u32[]{:S(2)}, u32[]{:S(2)}) %collective-permute-start.6) | collective-permute-done | bytes 524320 | tf_op jit(solution)/shard_map/ppermute | solution.py:333
  50.3 1.2 %collective-permute-done.7.z3_ref = bf16[4,512,128]{2,1,0:T(8,128)(2,1)S(1)} collective-permute-done((bf16[4,512,128]{2,1,0:T(8,128)(2,1)S(1)}, bf16[4,512,128]{2,1,0:T(8,128)(2,1)S(1)}, u32[]{:S(2)}, u32[]{:S(2)}) %collective-permute-start.7) | collective-permute-done | bytes 524320 | tf_op jit(solution)/shard_map/ppermute | solution.py:345
  51.5 1.2 %shard_map.111 = (bf16[512,640]{1,0:T(8,128)(2,1)S(1)}, f32[512,192]{1,0:T(8,128)S(1)}, f32[2,512,128]{2,1,0:T(8,128)S(1)}) custom-call(f32[7,8,128]{2,1,0:T(8,128)S(1)} %get-tuple-element.33.mask_ref, bf16[7,512,512]{2,1,0:T(8,128)(2,1)S(1)} %get-tuple-element.34.squares_ref, f32[7,512,128]{2,1,0:T(8,128)S(1)} %shard_map.110.before_ref, ...), custom_call_target="tpu_custom_call" | custom-call | bytes 8499200 | tf_op jit(solution)/shard_map/pallas_call | solution.py:363
  52.9 0.8 %shard_map.112 = (bf16[512,256]{1,0:T(8,128)(2,1)S(1)}, f32[128,192]{1,0:T(8,128)S(1)}, bf16[32,192]{1,0:T(8,128)(2,1)S(1)}, bf16[32,192]{1,0:T(8,128)(2,1)S(1)}) custom-call(f32[7,8,128]{2,1,0:T(8,128)S(1)} %get-tuple-element.33.mask_ref, bf16[7,512,512]{2,1,0:T(8,128)(2,1)S(1)} %get-tuple-element.34.squares_ref, ...), custom_call_target="tpu_custom_call" | custom-call | bytes 5804032 | tf_op jit(solution)/shard_map/pallas_call | solution.py:363
  53.7 0.8 %collective-permute-start.10 = (bf16[32,192]{1,0:T(8,128)(2,1)S(1)}, bf16[32,192]{1,0:T(8,128)(2,1)S(1)}, u32[]{:S(2)}, u32[]{:S(2)}) collective-permute-start(bf16[32,192]{1,0:T(8,128)(2,1)S(1)} %get-tuple-element.51), channel_id=1, source_target_pairs={{0,4},{4,0},{8,12},{12,8},{16,20},{20,16},{24,28},{28,24},{1,5},{5... | collective-permute-start | bytes 36872 | tf_op jit(solution)/shard_map/ppermute | solution.py:333
  54.5 3.8 %collective-permute-start.11 = (bf16[32,192]{1,0:T(8,128)(2,1)S(1)}, bf16[32,192]{1,0:T(8,128)(2,1)S(1)}, u32[]{:S(2)}, u32[]{:S(2)}) collective-permute-start(bf16[32,192]{1,0:T(8,128)(2,1)S(1)} %get-tuple-element.52), channel_id=1, source_target_pairs={{0,28},{4,8},{8,4},{12,16},{16,12},{20,24},{24,20},{28,0},{1,29},{... | collective-permute-start | bytes 36872 | tf_op jit(solution)/shard_map/ppermute | solution.py:339
  58.3 1.1 %shard_map.113 = bf16[512,896]{1,0:T(8,128)(2,1)} custom-call(bf16[512,640]{1,0:T(8,128)(2,1)S(1)} %get-tuple-element.42.inner_ref, bf16[512,256]{1,0:T(8,128)(2,1)S(1)} %get-tuple-element.48.edges_ref), custom_call_target="tpu_custom_call" | custom-call | bytes 1835008 | tf_op jit(solution)/shard_map/pallas_call | solution.py:363
  59.3 1.6 %collective-permute-done.11.got_b_ref = bf16[32,192]{1,0:T(8,128)(2,1)S(1)} collective-permute-done((bf16[32,192]{1,0:T(8,128)(2,1)S(1)}, bf16[32,192]{1,0:T(8,128)(2,1)S(1)}, u32[]{:S(2)}, u32[]{:S(2)}) %collective-permute-start.11) | collective-permute-done | bytes 12320 | tf_op jit(solution)/shard_map/ppermute | solution.py:339
  61.2 1.6 %collective-permute-start.13 = (bf16[32,128]{1,0:T(8,128)(2,1)S(1)}, bf16[32,128]{1,0:T(8,128)(2,1)S(1)}, u32[]{:S(2)}, u32[]{:S(2)}) collective-permute-start(bf16[32,128]{1,0:T(8,128)(2,1)S(1)} %get-tuple-element.55), channel_id=1, source_target_pairs={{0,3},{1,2},{2,1},{3,0},{4,7},{5,6},{6,5},{7,4},{8,11},{9,10},{10,... | collective-permute-start | bytes 24584 | tf_op jit(solution)/shard_map/ppermute | solution.py:339
  62.8 1.5 %collective-permute-done.13.got_b_ref = bf16[32,128]{1,0:T(8,128)(2,1)S(1)} collective-permute-done((bf16[32,128]{1,0:T(8,128)(2,1)S(1)}, bf16[32,128]{1,0:T(8,128)(2,1)S(1)}, u32[]{:S(2)}, u32[]{:S(2)}) %collective-permute-start.13) | collective-permute-done | bytes 8224 | tf_op jit(solution)/shard_map/ppermute | solution.py:339
  64.3 0.7 %shard_map.115 = f32[128,128]{1,0:T(8,128)} custom-call(f32[128,128]{1,0:T(8,128)S(1)} %get-tuple-element.53.center_ref, bf16[32,128]{1,0:T(8,128)(2,1)S(1)} %collective-permute-done.12.got_a_ref, bf16[32,128]{1,0:T(8,128)(2,1)S(1)} %collective-permute-done.13.got_b_ref), custom_call_target="tpu_custom_call" | custom-call | bytes 147456 | tf_op jit(solution)/shard_map/pallas_call | solution.py:363
  (26 shorter events, 2.9 us)
Async XLA Ops:
  2.9 16.0 %collective-permute-start = (bf16[4,512,128]{2,1,0:T(8,128)(2,1)}, bf16[4,512,128]{2,1,0:T(8,128)(2,1)}, u32[]{:S(2)}, u32[]{:S(2)}) collective-permute-start(bf16[4,512,128]{2,1,0:T(8,128)(2,1)} %get-tuple-element.36.x1a_ref), channel_id=1, source_target_pairs={{0,4},{4,0},{8,12},{12,8},{16,20},{20,16},{24,28},{28,24},{1,5},{5... | collective-permute-start | bytes 1572872 | tf_op jit(solution)/shard_map/ppermute | solution.py:333
  5.9 15.6 %collective-permute-start.2 = (bf16[4,512,128]{2,1,0:T(8,128)(2,1)}, bf16[4,512,128]{2,1,0:T(8,128)(2,1)}, u32[]{:S(2)}, u32[]{:S(2)}) collective-permute-start(bf16[4,512,128]{2,1,0:T(8,128)(2,1)} %get-tuple-element.38), channel_id=1, source_target_pairs={{0,8},{4,28},{8,16},{12,4},{16,24},{20,12},{24,0},{28,20},{1,9},{5... | collective-permute-start | bytes 1572872 | tf_op jit(solution)/shard_map/ppermute | solution.py:345
  7.5 19.8 %collective-permute-start.1 = (bf16[3,512,128]{2,1,0:T(8,128)(2,1)}, bf16[3,512,128]{2,1,0:T(8,128)(2,1)S(1)}, u32[]{:S(2)}, u32[]{:S(2)}) collective-permute-start(bf16[3,512,128]{2,1,0:T(8,128)(2,1)} %get-tuple-element.37.x1b_ref), channel_id=1, source_target_pairs={{0,4},{4,0},{8,12},{12,8},{16,20},{20,16},{24,28},{28,24},{1,5},{5... | collective-permute-start | bytes 1179656 | tf_op jit(solution)/shard_map/ppermute | solution.py:333
  10.1 2.5 %copy-start = (bf16[512,3584]{1,0:T(8,128)(2,1)S(1)}, bf16[512,3584]{1,0:T(8,128)(2,1)}, u32[]{:S(2)}) copy-start(bf16[512,3584]{1,0:T(8,128)(2,1)} %p2_ref.1) | copy-start | bytes 11010052
  12.5 1.0 %copy-start.2 = (bf16[7,128,192]{2,1,0:T(8,128)(2,1)S(1)}, bf16[7,128,192]{2,1,0:T(8,128)(2,1)}, u32[]{:S(2)}) copy-start(bf16[7,128,192]{2,1,0:T(8,128)(2,1)} %get-tuple-element.31.refs_1_) | copy-start | bytes 1032196
  13.5 0.9 %copy-start.4 = (bf16[192,512]{1,0:T(8,128)(2,1)S(1)}, bf16[192,512]{1,0:T(8,128)(2,1)}, u32[]{:S(2)}) copy-start(bf16[192,512]{1,0:T(8,128)(2,1)} %get-tuple-element.30.refs_0_) | copy-start | bytes 589828
  14.5 0.9 %copy-start.5 = (f32[8,3584]{1,0:T(8,128)S(1)}, f32[8,3584]{1,0:T(8,128)}, u32[]{:S(2)}) copy-start(f32[8,3584]{1,0:T(8,128)} %get-tuple-element.29.wide_ref) | copy-start | bytes 344068
  15.4 0.7 %copy-start.6 = (f32[7,8,128]{2,1,0:T(8,128)S(1)}, f32[7,8,128]{2,1,0:T(8,128)}, u32[]{:S(2)}) copy-start(f32[7,8,128]{2,1,0:T(8,128)} %get-tuple-element.32.refs_2_) | copy-start | bytes 86020
  16.1 8.5 %copy-start.1 = (bf16[4,512,128]{2,1,0:T(8,128)(2,1)S(1)}, bf16[4,512,128]{2,1,0:T(8,128)(2,1)}, u32[]{:S(2)}) copy-start(bf16[4,512,128]{2,1,0:T(8,128)(2,1)} %get-tuple-element.36.x1a_ref) | copy-start | bytes 1572868
  16.1 8.5 %copy-start.3 = (bf16[3,512,128]{2,1,0:T(8,128)(2,1)S(1)}, bf16[3,512,128]{2,1,0:T(8,128)(2,1)}, u32[]{:S(2)}) copy-start(bf16[3,512,128]{2,1,0:T(8,128)(2,1)} %get-tuple-element.37.x1b_ref) | copy-start | bytes 1179652
  18.9 17.1 %collective-permute-start.3 = (bf16[4,512,128]{2,1,0:T(8,128)(2,1)}, bf16[4,512,128]{2,1,0:T(8,128)(2,1)S(1)}, u32[]{:S(2)}, u32[]{:S(2)}) collective-permute-start(bf16[4,512,128]{2,1,0:T(8,128)(2,1)} %collective-permute-done.refs_0_), channel_id=1, source_target_pairs={{0,8},{4,28},{8,16},{12,4},{16,24},{20,12},{24,0},{28,20},{1,9},{5... | collective-permute-start | bytes 1572872 | tf_op jit(solution)/shard_map/ppermute | solution.py:345
  21.4 21.7 %collective-permute-start.5 = (bf16[4,512,128]{2,1,0:T(8,128)(2,1)}, bf16[4,512,128]{2,1,0:T(8,128)(2,1)S(1)}, u32[]{:S(2)}, u32[]{:S(2)}) collective-permute-start(bf16[4,512,128]{2,1,0:T(8,128)(2,1)} %collective-permute-done.2.refs_2_), channel_id=1, source_target_pairs={{0,4},{4,0},{8,12},{12,8},{16,20},{20,16},{24,28},{28,24},{1,5},{5... | collective-permute-start | bytes 1572872 | tf_op jit(solution)/shard_map/ppermute | solution.py:333
  27.3 10.1 %copy-start.7 = (bf16[1,512,128]{2,1,0:T(8,128)(2,1)S(1)}, bf16[1,512,128]{2,1,0:T(8,128)(2,1)}, u32[]{:S(2)}) copy-start(bf16[1,512,128]{2,1,0:T(8,128)(2,1)} %get-tuple-element.45) | copy-start | bytes 393220
  27.3 13.6 %collective-permute-start.4 = (bf16[2,512,128]{2,1,0:T(8,128)(2,1)S(1)}, bf16[2,512,128]{2,1,0:T(8,128)(2,1)S(1)}, u32[]{:S(2)}, u32[]{:S(2)}) collective-permute-start(bf16[2,512,128]{2,1,0:T(8,128)(2,1)S(1)} %slice.8), channel_id=1, source_target_pairs={{0,8},{4,28},{8,16},{12,4},{16,24},{20,12},{24,0},{28,20},{1,9},{5... | collective-permute-start | bytes 786440 | tf_op jit(solution)/shard_map/ppermute | solution.py:345
  36.1 14.2 %collective-permute-start.6 = (bf16[4,512,128]{2,1,0:T(8,128)(2,1)S(1)}, bf16[4,512,128]{2,1,0:T(8,128)(2,1)S(1)}, u32[]{:S(2)}, u32[]{:S(2)}) collective-permute-start(bf16[4,512,128]{2,1,0:T(8,128)(2,1)S(1)} %collective-permute-done.3.refs_0_), channel_id=1, source_target_pairs={{0,4},{4,0},{8,12},{12,8},{16,20},{20,16},{24,28},{28,24},{1,5},{5... | collective-permute-start | bytes 1572872 | tf_op jit(solution)/shard_map/ppermute | solution.py:333
  37.1 14.5 %collective-permute-start.7 = (bf16[4,512,128]{2,1,0:T(8,128)(2,1)S(1)}, bf16[4,512,128]{2,1,0:T(8,128)(2,1)S(1)}, u32[]{:S(2)}, u32[]{:S(2)}) collective-permute-start(bf16[4,512,128]{2,1,0:T(8,128)(2,1)S(1)} %collective-permute-done.3.refs_0_), channel_id=1, source_target_pairs={{0,8},{4,28},{8,16},{12,4},{16,24},{20,12},{24,0},{28,20},{1,9},{5... | collective-permute-start | bytes 1572872 | tf_op jit(solution)/shard_map/ppermute | solution.py:345
  37.4 15.5 %collective-permute-start.9 = (bf16[1,512,128]{2,1,0:T(8,128)(2,1)S(1)}, bf16[1,512,128]{2,1,0:T(8,128)(2,1)S(1)}, u32[]{:S(2)}, u32[]{:S(2)}) collective-permute-start(bf16[1,512,128]{2,1,0:T(8,128)(2,1)S(1)} %copy-done.7), channel_id=1, source_target_pairs={{0,8},{4,28},{8,16},{12,4},{16,24},{20,12},{24,0},{28,20},{1,9},{5... | collective-permute-start | bytes 393224 | tf_op jit(solution)/shard_map/ppermute | solution.py:345
  40.9 12.1 %collective-permute-start.8 = (bf16[1,512,128]{2,1,0:T(8,128)(2,1)S(1)}, bf16[1,512,128]{2,1,0:T(8,128)(2,1)S(1)}, u32[]{:S(2)}, u32[]{:S(2)}) collective-permute-start(bf16[1,512,128]{2,1,0:T(8,128)(2,1)S(1)} %slice.9), channel_id=1, source_target_pairs={{0,4},{4,0},{8,12},{12,8},{16,20},{20,16},{24,28},{28,24},{1,5},{5... | collective-permute-start | bytes 393224 | tf_op jit(solution)/shard_map/ppermute | solution.py:333
  53.7 5.7 %collective-permute-start.10 = (bf16[32,192]{1,0:T(8,128)(2,1)S(1)}, bf16[32,192]{1,0:T(8,128)(2,1)S(1)}, u32[]{:S(2)}, u32[]{:S(2)}) collective-permute-start(bf16[32,192]{1,0:T(8,128)(2,1)S(1)} %get-tuple-element.51), channel_id=1, source_target_pairs={{0,4},{4,0},{8,12},{12,8},{16,20},{20,16},{24,28},{28,24},{1,5},{5... | collective-permute-start | bytes 36872 | tf_op jit(solution)/shard_map/ppermute | solution.py:333
  54.5 6.4 %collective-permute-start.11 = (bf16[32,192]{1,0:T(8,128)(2,1)S(1)}, bf16[32,192]{1,0:T(8,128)(2,1)S(1)}, u32[]{:S(2)}, u32[]{:S(2)}) collective-permute-start(bf16[32,192]{1,0:T(8,128)(2,1)S(1)} %get-tuple-element.52), channel_id=1, source_target_pairs={{0,28},{4,8},{8,4},{12,16},{16,12},{20,24},{24,20},{28,0},{1,29},{... | collective-permute-start | bytes 36872 | tf_op jit(solution)/shard_map/ppermute | solution.py:339
  61.1 1.7 %collective-permute-start.12 = (bf16[32,128]{1,0:T(8,128)(2,1)S(1)}, bf16[32,128]{1,0:T(8,128)(2,1)S(1)}, u32[]{:S(2)}, u32[]{:S(2)}) collective-permute-start(bf16[32,128]{1,0:T(8,128)(2,1)S(1)} %get-tuple-element.54), channel_id=1, source_target_pairs={{0,1},{1,0},{2,3},{3,2},{4,5},{5,4},{6,7},{7,6},{8,9},{9,8},{10,11... | collective-permute-start | bytes 24584 | tf_op jit(solution)/shard_map/ppermute | solution.py:333
  61.2 3.1 %collective-permute-start.13 = (bf16[32,128]{1,0:T(8,128)(2,1)S(1)}, bf16[32,128]{1,0:T(8,128)(2,1)S(1)}, u32[]{:S(2)}, u32[]{:S(2)}) collective-permute-start(bf16[32,128]{1,0:T(8,128)(2,1)S(1)} %get-tuple-element.55), channel_id=1, source_target_pairs={{0,3},{1,2},{2,1},{3,0},{4,7},{5,6},{6,5},{7,4},{8,11},{9,10},{10,... | collective-permute-start | bytes 24584 | tf_op jit(solution)/shard_map/ppermute | solution.py:339

commit v8 on v7

--- a/solution.py
+++ b/solution.py
@@ -451,7 +451,7 @@
     z2p = shift_level(after(x1p, ready))
     x3 = swap_partner(z1, "row")
     z2q = shift_level(x1q[: 2 * HD - NEAR])
-    z1b = shift_level(after(own_zb, z1))
+    z1b = shift_level(after(own_zb, z2p))
     partner = [(j - 1, x1p, j) for j in range(1, NEAR)]
     partner += [(j - 1, x1q, j - NEAR) for j in range(NEAR, CHUNKS)]
     summed = stage(

time: 65.4 us -> 65.4 us (level)
  starting transfers between devices: 25.7 us -> 22.2 us
  waiting for transfers between devices: 21.2 us -> 24.7 us
    ppermute x7, starting transfers between devices: 12.3 us -> 9.51 us  [swap_partner(): return lax.ppermute(value, axis, [(s, s ^ 1) for s in range(count)])]
    ppermute x5, waiting for transfers between devices: 7.99 us -> 9.86 us  [shift_level(): return lax.ppermute(value, 'row', pairs)]
    ppermute x7, waiting for transfers between devices: 10.2 us -> 11.8 us  [swap_partner(): return lax.ppermute(value, axis, [(s, s ^ 1) for s in range(count)])]
where the time goes in v8:
time: 65.4 us; the launch traced here: 65.1 us
  waiting for transfers between devices  24.7 us (38%)
  starting transfers between devices  22.2 us (34%)
  Pallas kernels  13.7 us (21%)
  local copies, waits for them, and re-layouts  3.63 us (6%)
  between operations  0.78 us (1%)
    pallas_call x12, Pallas kernels, call(): pl.pallas_call(kernel, out_shape=shapes, in_specs=specs, out_specs=[HBM i...  13.7 us
    ppermute x7, waiting for transfers between devices, swap_partner(): return lax.ppermute(value, axis, [(s, s ^ 1) for s in range(count)])  11.8 us
    ppermute x5, waiting for transfers between devices, shift_level(): return lax.ppermute(value, 'row', pairs)  9.86 us
    ppermute x7, starting transfers between devices, swap_partner(): return lax.ppermute(value, axis, [(s, s ^ 1) for s in range(count)])  9.51 us
    ppermute x5, starting transfers between devices, shift_level(): return lax.ppermute(value, 'row', pairs)  7.3 us
    ppermute x2, starting transfers between devices, swap_other(): return lax.ppermute(value, axis, pairs)  5.43 us
    unnamed x16, local copies, waits for them, and re-layouts  3.6 us
    ppermute x2, waiting for transfers between devices, swap_other(): return lax.ppermute(value, axis, pairs)  3.06 us
  transfers between devices with their start and end apart: 14, of which 10 were waited for; matrix products, arithmetic and copies ran while one was open for 0% of the time, Pallas kernels for 15%

profile of v8, /device:TPU:0, one launch (start us, length us, event | category | flops | bytes accessed | tf_op | source)
XLA Modules:
  0.0 65.1 jit_solution(1460634043805729161)
XLA Ops:
  0.6 2.3 %shard_map.106 = (bf16[4,512,128]{2,1,0:T(8,128)(2,1)}, bf16[3,512,128]{2,1,0:T(8,128)(2,1)}, bf16[4,512,128]{2,1,0:T(8,128)(2,1)}, bf16[1,512,128]{2,1,0:T(8,128)(2,1)}) custom-call(s32[8,56]{1,0:T(8,128)} %pattern_hbm.1, bf16[512,896]{1,0:T(8,128)(2,1)} %density_hbm.1), custom_call_target="tpu_custom_call" | custom-call | bytes 2492160 | tf_op jit(solution)/shard_map/pallas_call | solution.py:363
  2.9 3.0 %collective-permute-start = (bf16[4,512,128]{2,1,0:T(8,128)(2,1)}, bf16[4,512,128]{2,1,0:T(8,128)(2,1)}, u32[]{:S(2)}, u32[]{:S(2)}) collective-permute-start(bf16[4,512,128]{2,1,0:T(8,128)(2,1)} %get-tuple-element.36.x1a_ref), channel_id=1, source_target_pairs={{0,4},{4,0},{8,12},{12,8},{16,20},{20,16},{24,28},{28,24},{1,5},{5... | collective-permute-start | bytes 1572872 | tf_op jit(solution)/shard_map/ppermute | solution.py:333
  6.0 2.1 %collective-permute-start.2 = (bf16[4,512,128]{2,1,0:T(8,128)(2,1)}, bf16[4,512,128]{2,1,0:T(8,128)(2,1)}, u32[]{:S(2)}, u32[]{:S(2)}) collective-permute-start(bf16[4,512,128]{2,1,0:T(8,128)(2,1)} %get-tuple-element.38), channel_id=1, source_target_pairs={{0,8},{4,28},{8,16},{12,4},{16,24},{20,12},{24,0},{28,20},{1,9},{5... | collective-permute-start | bytes 1572872 | tf_op jit(solution)/shard_map/ppermute | solution.py:345
  8.0 2.4 %shard_map.104 = (bf16[192,512]{1,0:T(8,128)(2,1)}, bf16[7,128,192]{2,1,0:T(8,128)(2,1)}, f32[7,8,128]{2,1,0:T(8,128)}, f32[8,3584]{1,0:T(8,128)}) custom-call(s32[8,56]{1,0:T(8,128)} %pattern_hbm.1, s32[8]{0:T(128)} %refs_1_.1, s32[8]{0:T(128)} %refs_2_.1, s32[1,14]{1,0:T(1,128)} %refs_3_.1, s32[1,14]{1,0:T(1,128)} %refs_4_.1, bf16[32,512]{1,0:T(8,128)(2,1)} %bitcast.5, ...), custom_call_target="tpu_custom_call" | custom-call | flops 6000000000 | bytes 776112 | tf_op jit(solution)/shard_map/pallas_call | solution.py:363
  10.5 1.0 %copy-done.2 = bf16[7,128,192]{2,1,0:T(8,128)(2,1)S(1)} copy-done((bf16[7,128,192]{2,1,0:T(8,128)(2,1)S(1)}, bf16[7,128,192]{2,1,0:T(8,128)(2,1)}, u32[]{:S(2)}) %copy-start.2) | copy-done | bytes 344088
  11.5 0.9 %copy-done.4 = bf16[192,512]{1,0:T(8,128)(2,1)S(1)} copy-done((bf16[192,512]{1,0:T(8,128)(2,1)S(1)}, bf16[192,512]{1,0:T(8,128)(2,1)}, u32[]{:S(2)}) %copy-start.4) | copy-done | bytes 196632
  12.4 0.9 %copy-done.5 = f32[8,3584]{1,0:T(8,128)S(1)} copy-done((f32[8,3584]{1,0:T(8,128)S(1)}, f32[8,3584]{1,0:T(8,128)}, u32[]{:S(2)}) %copy-start.5) | copy-done | bytes 114712
  13.3 0.7 %copy-done.6 = f32[7,8,128]{2,1,0:T(8,128)S(1)} copy-done((f32[7,8,128]{2,1,0:T(8,128)S(1)}, f32[7,8,128]{2,1,0:T(8,128)}, u32[]{:S(2)}) %copy-start.6) | copy-done | bytes 28696
  14.1 1.2 %shard_map.105 = (bf16[7,512,512]{2,1,0:T(8,128)(2,1)S(1)}, f32[7,512,128]{2,1,0:T(8,128)S(1)}, bf16[192,512]{1,0:T(8,128)(2,1)S(1)}, bf16[7,128,192]{2,1,0:T(8,128)(2,1)S(1)}, f32[7,8,128]{2,1,0:T(8,128)S(1)}) custom-call(bf16[512,3584]{1,0:T(8,128)(2,1)S(1)} %copy-done, f32[8,3584]{1,0:T(8,128)S(1)} %copy-done.5, bf16[192,512]{1,0:T(8,128)(2,1)S(1)} %copy-done.4, ...), custom_call_target="tpu_custom_call" | custom-call | flops 1000000000 | bytes 10428416 | tf_op jit(solution)/shard_map/pallas_call | solution.py:363
  15.3 3.7 %collective-permute-done.refs_0_ = bf16[4,512,128]{2,1,0:T(8,128)(2,1)} collective-permute-done((bf16[4,512,128]{2,1,0:T(8,128)(2,1)}, bf16[4,512,128]{2,1,0:T(8,128)(2,1)}, u32[]{:S(2)}, u32[]{:S(2)}) %collective-permute-start) | collective-permute-done | bytes 524320 | tf_op jit(solution)/shard_map/ppermute | solution.py:333
  18.9 2.2 %collective-permute-start.3 = (bf16[4,512,128]{2,1,0:T(8,128)(2,1)}, bf16[4,512,128]{2,1,0:T(8,128)(2,1)S(1)}, u32[]{:S(2)}, u32[]{:S(2)}) collective-permute-start(bf16[4,512,128]{2,1,0:T(8,128)(2,1)} %collective-permute-done.refs_0_), channel_id=1, source_target_pairs={{0,8},{4,28},{8,16},{12,4},{16,24},{20,12},{24,0},{28,20},{1,9},{5... | collective-permute-start | bytes 1572872 | tf_op jit(solution)/shard_map/ppermute | solution.py:345
  21.1 0.6 collective-permute-done.2.refs_2_
  21.7 2.9 %collective-permute-start.5 = (bf16[4,512,128]{2,1,0:T(8,128)(2,1)}, bf16[4,512,128]{2,1,0:T(8,128)(2,1)S(1)}, u32[]{:S(2)}, u32[]{:S(2)}) collective-permute-start(bf16[4,512,128]{2,1,0:T(8,128)(2,1)} %collective-permute-done.2.refs_2_), channel_id=1, source_target_pairs={{0,4},{4,0},{8,12},{12,8},{16,20},{20,16},{24,28},{28,24},{1,5},{5... | collective-permute-start | bytes 1572872 | tf_op jit(solution)/shard_map/ppermute | solution.py:333
  24.6 0.7 %shard_map.107.before_ref = f32[7,512,128]{2,1,0:T(8,128)S(1)} custom-call(bf16[7,512,512]{2,1,0:T(8,128)(2,1)S(1)} %get-tuple-element.34.squares_ref, f32[7,512,128]{2,1,0:T(8,128)S(1)} %get-tuple-element.35.before_ref, bf16[4,512,128]{2,1,0:T(8,128)(2,1)S(1)} %copy-done.1, bf16[3,512,128]{2,1,0:T(8,128)(2,1)S(1)} %copy-done.3), custom_call_target="tpu_custom_call" | custom-call | bytes 8257536 | tf_op jit(solution)/shard_map/pallas_call | solution.py:363
  25.3 1.9 %collective-permute-done.1.refs_1_ = bf16[3,512,128]{2,1,0:T(8,128)(2,1)S(1)} collective-permute-done((bf16[3,512,128]{2,1,0:T(8,128)(2,1)}, bf16[3,512,128]{2,1,0:T(8,128)(2,1)S(1)}, u32[]{:S(2)}, u32[]{:S(2)}) %collective-permute-start.1) | collective-permute-done | bytes 393248 | tf_op jit(solution)/shard_map/ppermute | solution.py:333
  27.3 2.2 %collective-permute-start.4 = (bf16[2,512,128]{2,1,0:T(8,128)(2,1)S(1)}, bf16[2,512,128]{2,1,0:T(8,128)(2,1)S(1)}, u32[]{:S(2)}, u32[]{:S(2)}) collective-permute-start(bf16[2,512,128]{2,1,0:T(8,128)(2,1)S(1)} %slice.8), channel_id=1, source_target_pairs={{0,8},{4,28},{8,16},{12,4},{16,24},{20,12},{24,0},{28,20},{1,9},{5... | collective-permute-start | bytes 786440 | tf_op jit(solution)/shard_map/ppermute | solution.py:345
  29.5 2.1 %shard_map.108.before_ref = f32[7,512,128]{2,1,0:T(8,128)S(1)} custom-call(bf16[7,512,512]{2,1,0:T(8,128)(2,1)S(1)} %get-tuple-element.34.squares_ref, f32[7,512,128]{2,1,0:T(8,128)S(1)} %shard_map.107.before_ref, bf16[4,512,128]{2,1,0:T(8,128)(2,1)} %collective-permute-done.refs_0_, bf16[3,512,128]{2,1,0:T(8,128)(2,1)S(1)} %collective-permute-done.1.refs_1_, ...), custom_call_target="tpu_custom_call" | custom-call | flops 3000000000 | bytes 8781824 | tf_op jit(solution)/shard_map/pallas_call | solution.py:363
  31.6 4.4 %collective-permute-done.3.refs_0_ = bf16[4,512,128]{2,1,0:T(8,128)(2,1)S(1)} collective-permute-done((bf16[4,512,128]{2,1,0:T(8,128)(2,1)}, bf16[4,512,128]{2,1,0:T(8,128)(2,1)S(1)}, u32[]{:S(2)}, u32[]{:S(2)}) %collective-permute-start.3) | collective-permute-done | bytes 524320 | tf_op jit(solution)/shard_map/ppermute | solution.py:345
  36.1 1.0 %collective-permute-start.6 = (bf16[4,512,128]{2,1,0:T(8,128)(2,1)S(1)}, bf16[4,512,128]{2,1,0:T(8,128)(2,1)S(1)}, u32[]{:S(2)}, u32[]{:S(2)}) collective-permute-start(bf16[4,512,128]{2,1,0:T(8,128)(2,1)S(1)} %collective-permute-done.3.refs_0_), channel_id=1, source_target_pairs={{0,4},{4,0},{8,12},{12,8},{16,20},{20,16},{24,28},{28,24},{1,5},{5... | collective-permute-start | bytes 1572872 | tf_op jit(solution)/shard_map/ppermute | solution.py:333
  37.4 3.5 %collective-permute-done.4.refs_0_ = bf16[2,512,128]{2,1,0:T(8,128)(2,1)S(1)} collective-permute-done((bf16[2,512,128]{2,1,0:T(8,128)(2,1)S(1)}, bf16[2,512,128]{2,1,0:T(8,128)(2,1)S(1)}, u32[]{:S(2)}, u32[]{:S(2)}) %collective-permute-start.4) | collective-permute-done | bytes 262176 | tf_op jit(solution)/shard_map/ppermute | solution.py:345
  40.9 1.8 %collective-permute-start.8 = (bf16[1,512,128]{2,1,0:T(8,128)(2,1)S(1)}, bf16[1,512,128]{2,1,0:T(8,128)(2,1)S(1)}, u32[]{:S(2)}, u32[]{:S(2)}) collective-permute-start(bf16[1,512,128]{2,1,0:T(8,128)(2,1)S(1)} %slice.9), channel_id=1, source_target_pairs={{0,4},{4,0},{8,12},{12,8},{16,20},{20,16},{24,28},{28,24},{1,5},{5... | collective-permute-start | bytes 393224 | tf_op jit(solution)/shard_map/ppermute | solution.py:333
  44.2 6.2 %collective-permute-done.6.x2p_ref = bf16[4,512,128]{2,1,0:T(8,128)(2,1)S(1)} collective-permute-done((bf16[4,512,128]{2,1,0:T(8,128)(2,1)S(1)}, bf16[4,512,128]{2,1,0:T(8,128)(2,1)S(1)}, u32[]{:S(2)}, u32[]{:S(2)}) %collective-permute-start.6) | collective-permute-done | bytes 524320 | tf_op jit(solution)/shard_map/ppermute | solution.py:333
  50.3 1.2 %collective-permute-done.7.z3_ref = bf16[4,512,128]{2,1,0:T(8,128)(2,1)S(1)} collective-permute-done((bf16[4,512,128]{2,1,0:T(8,128)(2,1)S(1)}, bf16[4,512,128]{2,1,0:T(8,128)(2,1)S(1)}, u32[]{:S(2)}, u32[]{:S(2)}) %collective-permute-start.7) | collective-permute-done | bytes 524320 | tf_op jit(solution)/shard_map/ppermute | solution.py:345
  51.5 1.2 %shard_map.111 = (bf16[512,640]{1,0:T(8,128)(2,1)S(1)}, f32[512,192]{1,0:T(8,128)S(1)}, f32[2,512,128]{2,1,0:T(8,128)S(1)}) custom-call(f32[7,8,128]{2,1,0:T(8,128)S(1)} %get-tuple-element.33.mask_ref, bf16[7,512,512]{2,1,0:T(8,128)(2,1)S(1)} %get-tuple-element.34.squares_ref, f32[7,512,128]{2,1,0:T(8,128)S(1)} %shard_map.110.before_ref, ...), custom_call_target="tpu_custom_call" | custom-call | bytes 8499200 | tf_op jit(solution)/shard_map/pallas_call | solution.py:363
  52.9 0.8 %shard_map.112 = (bf16[512,256]{1,0:T(8,128)(2,1)S(1)}, f32[128,192]{1,0:T(8,128)S(1)}, bf16[32,192]{1,0:T(8,128)(2,1)S(1)}, bf16[32,192]{1,0:T(8,128)(2,1)S(1)}) custom-call(f32[7,8,128]{2,1,0:T(8,128)S(1)} %get-tuple-element.33.mask_ref, bf16[7,512,512]{2,1,0:T(8,128)(2,1)S(1)} %get-tuple-element.34.squares_ref, ...), custom_call_target="tpu_custom_call" | custom-call | bytes 5804032 | tf_op jit(solution)/shard_map/pallas_call | solution.py:363
  53.7 0.8 %collective-permute-start.10 = (bf16[32,192]{1,0:T(8,128)(2,1)S(1)}, bf16[32,192]{1,0:T(8,128)(2,1)S(1)}, u32[]{:S(2)}, u32[]{:S(2)}) collective-permute-start(bf16[32,192]{1,0:T(8,128)(2,1)S(1)} %get-tuple-element.51), channel_id=1, source_target_pairs={{0,4},{4,0},{8,12},{12,8},{16,20},{20,16},{24,28},{28,24},{1,5},{5... | collective-permute-start | bytes 36872 | tf_op jit(solution)/shard_map/ppermute | solution.py:333
  54.5 3.8 %collective-permute-start.11 = (bf16[32,192]{1,0:T(8,128)(2,1)S(1)}, bf16[32,192]{1,0:T(8,128)(2,1)S(1)}, u32[]{:S(2)}, u32[]{:S(2)}) collective-permute-start(bf16[32,192]{1,0:T(8,128)(2,1)S(1)} %get-tuple-element.52), channel_id=1, source_target_pairs={{0,28},{4,8},{8,4},{12,16},{16,12},{20,24},{24,20},{28,0},{1,29},{... | collective-permute-start | bytes 36872 | tf_op jit(solution)/shard_map/ppermute | solution.py:339
  58.3 1.1 %shard_map.113 = bf16[512,896]{1,0:T(8,128)(2,1)} custom-call(bf16[512,640]{1,0:T(8,128)(2,1)S(1)} %get-tuple-element.42.inner_ref, bf16[512,256]{1,0:T(8,128)(2,1)S(1)} %get-tuple-element.48.edges_ref), custom_call_target="tpu_custom_call" | custom-call | bytes 1835008 | tf_op jit(solution)/shard_map/pallas_call | solution.py:363
  59.3 1.6 %collective-permute-done.11.got_b_ref = bf16[32,192]{1,0:T(8,128)(2,1)S(1)} collective-permute-done((bf16[32,192]{1,0:T(8,128)(2,1)S(1)}, bf16[32,192]{1,0:T(8,128)(2,1)S(1)}, u32[]{:S(2)}, u32[]{:S(2)}) %collective-permute-start.11) | collective-permute-done | bytes 12320 | tf_op jit(solution)/shard_map/ppermute | solution.py:339
  61.2 1.6 %collective-permute-start.13 = (bf16[32,128]{1,0:T(8,128)(2,1)S(1)}, bf16[32,128]{1,0:T(8,128)(2,1)S(1)}, u32[]{:S(2)}, u32[]{:S(2)}) collective-permute-start(bf16[32,128]{1,0:T(8,128)(2,1)S(1)} %get-tuple-element.55), channel_id=1, source_target_pairs={{0,3},{1,2},{2,1},{3,0},{4,7},{5,6},{6,5},{7,4},{8,11},{9,10},{10,... | collective-permute-start | bytes 24584 | tf_op jit(solution)/shard_map/ppermute | solution.py:339
  62.8 1.5 %collective-permute-done.13.got_b_ref = bf16[32,128]{1,0:T(8,128)(2,1)S(1)} collective-permute-done((bf16[32,128]{1,0:T(8,128)(2,1)S(1)}, bf16[32,128]{1,0:T(8,128)(2,1)S(1)}, u32[]{:S(2)}, u32[]{:S(2)}) %collective-permute-start.13) | collective-permute-done | bytes 8224 | tf_op jit(solution)/shard_map/ppermute | solution.py:339
  64.3 0.7 %shard_map.115 = f32[128,128]{1,0:T(8,128)} custom-call(f32[128,128]{1,0:T(8,128)S(1)} %get-tuple-element.53.center_ref, bf16[32,128]{1,0:T(8,128)(2,1)S(1)} %collective-permute-done.12.got_a_ref, bf16[32,128]{1,0:T(8,128)(2,1)S(1)} %collective-permute-done.13.got_b_ref), custom_call_target="tpu_custom_call" | custom-call | bytes 147456 | tf_op jit(solution)/shard_map/pallas_call | solution.py:363
  (26 shorter events, 2.4 us)
Async XLA Ops:
  2.9 16.0 %collective-permute-start = (bf16[4,512,128]{2,1,0:T(8,128)(2,1)}, bf16[4,512,128]{2,1,0:T(8,128)(2,1)}, u32[]{:S(2)}, u32[]{:S(2)}) collective-permute-start(bf16[4,512,128]{2,1,0:T(8,128)(2,1)} %get-tuple-element.36.x1a_ref), channel_id=1, source_target_pairs={{0,4},{4,0},{8,12},{12,8},{16,20},{20,16},{24,28},{28,24},{1,5},{5... | collective-permute-start | bytes 1572872 | tf_op jit(solution)/shard_map/ppermute | solution.py:333
  5.9 21.4 %collective-permute-start.1 = (bf16[3,512,128]{2,1,0:T(8,128)(2,1)}, bf16[3,512,128]{2,1,0:T(8,128)(2,1)S(1)}, u32[]{:S(2)}, u32[]{:S(2)}) collective-permute-start(bf16[3,512,128]{2,1,0:T(8,128)(2,1)} %get-tuple-element.37.x1b_ref), channel_id=1, source_target_pairs={{0,4},{4,0},{8,12},{12,8},{16,20},{20,16},{24,28},{28,24},{1,5},{5... | collective-permute-start | bytes 1179656 | tf_op jit(solution)/shard_map/ppermute | solution.py:333
  6.0 15.8 %collective-permute-start.2 = (bf16[4,512,128]{2,1,0:T(8,128)(2,1)}, bf16[4,512,128]{2,1,0:T(8,128)(2,1)}, u32[]{:S(2)}, u32[]{:S(2)}) collective-permute-start(bf16[4,512,128]{2,1,0:T(8,128)(2,1)} %get-tuple-element.38), channel_id=1, source_target_pairs={{0,8},{4,28},{8,16},{12,4},{16,24},{20,12},{24,0},{28,20},{1,9},{5... | collective-permute-start | bytes 1572872 | tf_op jit(solution)/shard_map/ppermute | solution.py:345
  8.0 2.4 %copy-start = (bf16[512,3584]{1,0:T(8,128)(2,1)S(1)}, bf16[512,3584]{1,0:T(8,128)(2,1)}, u32[]{:S(2)}) copy-start(bf16[512,3584]{1,0:T(8,128)(2,1)} %p2_ref.1) | copy-start | bytes 11010052
  10.5 1.0 %copy-start.2 = (bf16[7,128,192]{2,1,0:T(8,128)(2,1)S(1)}, bf16[7,128,192]{2,1,0:T(8,128)(2,1)}, u32[]{:S(2)}) copy-start(bf16[7,128,192]{2,1,0:T(8,128)(2,1)} %get-tuple-element.31.refs_1_) | copy-start | bytes 1032196
  11.5 0.9 %copy-start.4 = (bf16[192,512]{1,0:T(8,128)(2,1)S(1)}, bf16[192,512]{1,0:T(8,128)(2,1)}, u32[]{:S(2)}) copy-start(bf16[192,512]{1,0:T(8,128)(2,1)} %get-tuple-element.30.refs_0_) | copy-start | bytes 589828
  12.4 0.9 %copy-start.5 = (f32[8,3584]{1,0:T(8,128)S(1)}, f32[8,3584]{1,0:T(8,128)}, u32[]{:S(2)}) copy-start(f32[8,3584]{1,0:T(8,128)} %get-tuple-element.29.wide_ref) | copy-start | bytes 344068
  13.3 0.7 %copy-start.6 = (f32[7,8,128]{2,1,0:T(8,128)S(1)}, f32[7,8,128]{2,1,0:T(8,128)}, u32[]{:S(2)}) copy-start(f32[7,8,128]{2,1,0:T(8,128)} %get-tuple-element.32.refs_2_) | copy-start | bytes 86020
  14.1 10.5 %copy-start.1 = (bf16[4,512,128]{2,1,0:T(8,128)(2,1)S(1)}, bf16[4,512,128]{2,1,0:T(8,128)(2,1)}, u32[]{:S(2)}) copy-start(bf16[4,512,128]{2,1,0:T(8,128)(2,1)} %get-tuple-element.36.x1a_ref) | copy-start | bytes 1572868
  14.1 10.5 %copy-start.3 = (bf16[3,512,128]{2,1,0:T(8,128)(2,1)S(1)}, bf16[3,512,128]{2,1,0:T(8,128)(2,1)}, u32[]{:S(2)}) copy-start(bf16[3,512,128]{2,1,0:T(8,128)(2,1)} %get-tuple-element.37.x1b_ref) | copy-start | bytes 1179652
  18.9 17.1 %collective-permute-start.3 = (bf16[4,512,128]{2,1,0:T(8,128)(2,1)}, bf16[4,512,128]{2,1,0:T(8,128)(2,1)S(1)}, u32[]{:S(2)}, u32[]{:S(2)}) collective-permute-start(bf16[4,512,128]{2,1,0:T(8,128)(2,1)} %collective-permute-done.refs_0_), channel_id=1, source_target_pairs={{0,8},{4,28},{8,16},{12,4},{16,24},{20,12},{24,0},{28,20},{1,9},{5... | collective-permute-start | bytes 1572872 | tf_op jit(solution)/shard_map/ppermute | solution.py:345
  21.7 21.8 %collective-permute-start.5 = (bf16[4,512,128]{2,1,0:T(8,128)(2,1)}, bf16[4,512,128]{2,1,0:T(8,128)(2,1)S(1)}, u32[]{:S(2)}, u32[]{:S(2)}) collective-permute-start(bf16[4,512,128]{2,1,0:T(8,128)(2,1)} %collective-permute-done.2.refs_2_), channel_id=1, source_target_pairs={{0,4},{4,0},{8,12},{12,8},{16,20},{20,16},{24,28},{28,24},{1,5},{5... | collective-permute-start | bytes 1572872 | tf_op jit(solution)/shard_map/ppermute | solution.py:333
  27.3 15.4 %copy-start.7 = (bf16[1,512,128]{2,1,0:T(8,128)(2,1)S(1)}, bf16[1,512,128]{2,1,0:T(8,128)(2,1)}, u32[]{:S(2)}) copy-start(bf16[1,512,128]{2,1,0:T(8,128)(2,1)} %get-tuple-element.45) | copy-start | bytes 393220
  27.3 13.6 %collective-permute-start.4 = (bf16[2,512,128]{2,1,0:T(8,128)(2,1)S(1)}, bf16[2,512,128]{2,1,0:T(8,128)(2,1)S(1)}, u32[]{:S(2)}, u32[]{:S(2)}) collective-permute-start(bf16[2,512,128]{2,1,0:T(8,128)(2,1)S(1)} %slice.8), channel_id=1, source_target_pairs={{0,8},{4,28},{8,16},{12,4},{16,24},{20,12},{24,0},{28,20},{1,9},{5... | collective-permute-start | bytes 786440 | tf_op jit(solution)/shard_map/ppermute | solution.py:345
  36.1 14.2 %collective-permute-start.6 = (bf16[4,512,128]{2,1,0:T(8,128)(2,1)S(1)}, bf16[4,512,128]{2,1,0:T(8,128)(2,1)S(1)}, u32[]{:S(2)}, u32[]{:S(2)}) collective-permute-start(bf16[4,512,128]{2,1,0:T(8,128)(2,1)S(1)} %collective-permute-done.3.refs_0_), channel_id=1, source_target_pairs={{0,4},{4,0},{8,12},{12,8},{16,20},{20,16},{24,28},{28,24},{1,5},{5... | collective-permute-start | bytes 1572872 | tf_op jit(solution)/shard_map/ppermute | solution.py:333
  37.1 14.5 %collective-permute-start.7 = (bf16[4,512,128]{2,1,0:T(8,128)(2,1)S(1)}, bf16[4,512,128]{2,1,0:T(8,128)(2,1)S(1)}, u32[]{:S(2)}, u32[]{:S(2)}) collective-permute-start(bf16[4,512,128]{2,1,0:T(8,128)(2,1)S(1)} %collective-permute-done.3.refs_0_), channel_id=1, source_target_pairs={{0,8},{4,28},{8,16},{12,4},{16,24},{20,12},{24,0},{28,20},{1,9},{5... | collective-permute-start | bytes 1572872 | tf_op jit(solution)/shard_map/ppermute | solution.py:345
  40.9 11.9 %collective-permute-start.8 = (bf16[1,512,128]{2,1,0:T(8,128)(2,1)S(1)}, bf16[1,512,128]{2,1,0:T(8,128)(2,1)S(1)}, u32[]{:S(2)}, u32[]{:S(2)}) collective-permute-start(bf16[1,512,128]{2,1,0:T(8,128)(2,1)S(1)} %slice.9), channel_id=1, source_target_pairs={{0,4},{4,0},{8,12},{12,8},{16,20},{20,16},{24,28},{28,24},{1,5},{5... | collective-permute-start | bytes 393224 | tf_op jit(solution)/shard_map/ppermute | solution.py:333
  42.7 10.3 %collective-permute-start.9 = (bf16[1,512,128]{2,1,0:T(8,128)(2,1)S(1)}, bf16[1,512,128]{2,1,0:T(8,128)(2,1)S(1)}, u32[]{:S(2)}, u32[]{:S(2)}) collective-permute-start(bf16[1,512,128]{2,1,0:T(8,128)(2,1)S(1)} %copy-done.7), channel_id=1, source_target_pairs={{0,8},{4,28},{8,16},{12,4},{16,24},{20,12},{24,0},{28,20},{1,9},{5... | collective-permute-start | bytes 393224 | tf_op jit(solution)/shard_map/ppermute | solution.py:345
  53.7 5.7 %collective-permute-start.10 = (bf16[32,192]{1,0:T(8,128)(2,1)S(1)}, bf16[32,192]{1,0:T(8,128)(2,1)S(1)}, u32[]{:S(2)}, u32[]{:S(2)}) collective-permute-start(bf16[32,192]{1,0:T(8,128)(2,1)S(1)} %get-tuple-element.51), channel_id=1, source_target_pairs={{0,4},{4,0},{8,12},{12,8},{16,20},{20,16},{24,28},{28,24},{1,5},{5... | collective-permute-start | bytes 36872 | tf_op jit(solution)/shard_map/ppermute | solution.py:333
  54.5 6.4 %collective-permute-start.11 = (bf16[32,192]{1,0:T(8,128)(2,1)S(1)}, bf16[32,192]{1,0:T(8,128)(2,1)S(1)}, u32[]{:S(2)}, u32[]{:S(2)}) collective-permute-start(bf16[32,192]{1,0:T(8,128)(2,1)S(1)} %get-tuple-element.52), channel_id=1, source_target_pairs={{0,28},{4,8},{8,4},{12,16},{16,12},{20,24},{24,20},{28,0},{1,29},{... | collective-permute-start | bytes 36872 | tf_op jit(solution)/shard_map/ppermute | solution.py:339
  61.1 1.7 %collective-permute-start.12 = (bf16[32,128]{1,0:T(8,128)(2,1)S(1)}, bf16[32,128]{1,0:T(8,128)(2,1)S(1)}, u32[]{:S(2)}, u32[]{:S(2)}) collective-permute-start(bf16[32,128]{1,0:T(8,128)(2,1)S(1)} %get-tuple-element.54), channel_id=1, source_target_pairs={{0,1},{1,0},{2,3},{3,2},{4,5},{5,4},{6,7},{7,6},{8,9},{9,8},{10,11... | collective-permute-start | bytes 24584 | tf_op jit(solution)/shard_map/ppermute | solution.py:333
  61.2 3.1 %collective-permute-start.13 = (bf16[32,128]{1,0:T(8,128)(2,1)S(1)}, bf16[32,128]{1,0:T(8,128)(2,1)S(1)}, u32[]{:S(2)}, u32[]{:S(2)}) collective-permute-start(bf16[32,128]{1,0:T(8,128)(2,1)S(1)} %get-tuple-element.55), channel_id=1, source_target_pairs={{0,3},{1,2},{2,1},{3,0},{4,7},{5,6},{6,5},{7,4},{8,11},{9,10},{10,... | collective-permute-start | bytes 24584 | tf_op jit(solution)/shard_map/ppermute | solution.py:339

commit v9 on v8

--- a/solution.py
+++ b/solution.py
@@ -488,7 +488,7 @@
     center, rim_a, rim_b = call(
         row_rims_kernel,
         [((SX, SY), F32), ((M, SX), BF16), ((M, SX), BF16)],
-        [after(middle, new_density), got_a, got_b],
+        [middle, got_a, got_b],
     )
     got_a = swap_partner(rim_a, "col")
     got_b = swap_other(rim_b, "col")

time: 65.4 us -> 65.4 us (level)
  no operation moved by 1% of the time
where the time goes in v9:
time: 65.4 us; the launch traced here: 65.1 us
  waiting for transfers between devices  24.7 us (38%)
  starting transfers between devices  22.2 us (34%)
  Pallas kernels  13.7 us (21%)
  local copies, waits for them, and re-layouts  3.63 us (6%)
  between operations  0.78 us (1%)
    pallas_call x12, Pallas kernels, call(): pl.pallas_call(kernel, out_shape=shapes, in_specs=specs, out_specs=[HBM i...  13.7 us
    ppermute x7, waiting for transfers between devices, swap_partner(): return lax.ppermute(value, axis, [(s, s ^ 1) for s in range(count)])  11.8 us
    ppermute x5, waiting for transfers between devices, shift_level(): return lax.ppermute(value, 'row', pairs)  9.86 us
    ppermute x7, starting transfers between devices, swap_partner(): return lax.ppermute(value, axis, [(s, s ^ 1) for s in range(count)])  9.51 us
    ppermute x5, starting transfers between devices, shift_level(): return lax.ppermute(value, 'row', pairs)  7.3 us
    ppermute x2, starting transfers between devices, swap_other(): return lax.ppermute(value, axis, pairs)  5.43 us
    unnamed x16, local copies, waits for them, and re-layouts  3.6 us
    ppermute x2, waiting for transfers between devices, swap_other(): return lax.ppermute(value, axis, pairs)  3.06 us
  transfers between devices with their start and end apart: 14, of which 10 were waited for; matrix products, arithmetic and copies ran while one was open for 0% of the time, Pallas kernels for 15%

profile of v9, /device:TPU:0, one launch (start us, length us, event | category | flops | bytes accessed | tf_op | source)
XLA Modules:
  0.0 65.1 jit_solution(8640821098376834001)
XLA Ops:
  0.6 2.3 %shard_map.106 = (bf16[4,512,128]{2,1,0:T(8,128)(2,1)}, bf16[3,512,128]{2,1,0:T(8,128)(2,1)}, bf16[4,512,128]{2,1,0:T(8,128)(2,1)}, bf16[1,512,128]{2,1,0:T(8,128)(2,1)}) custom-call(s32[8,56]{1,0:T(8,128)} %pattern_hbm.1, bf16[512,896]{1,0:T(8,128)(2,1)} %density_hbm.1), custom_call_target="tpu_custom_call" | custom-call | bytes 2492160 | tf_op jit(solution)/shard_map/pallas_call | solution.py:363
  2.9 3.0 %collective-permute-start = (bf16[4,512,128]{2,1,0:T(8,128)(2,1)}, bf16[4,512,128]{2,1,0:T(8,128)(2,1)}, u32[]{:S(2)}, u32[]{:S(2)}) collective-permute-start(bf16[4,512,128]{2,1,0:T(8,128)(2,1)} %get-tuple-element.35.x1a_ref), channel_id=1, source_target_pairs={{0,4},{4,0},{8,12},{12,8},{16,20},{20,16},{24,28},{28,24},{1,5},{5... | collective-permute-start | bytes 1572872 | tf_op jit(solution)/shard_map/ppermute | solution.py:333
  6.0 2.1 %collective-permute-start.2 = (bf16[4,512,128]{2,1,0:T(8,128)(2,1)}, bf16[4,512,128]{2,1,0:T(8,128)(2,1)}, u32[]{:S(2)}, u32[]{:S(2)}) collective-permute-start(bf16[4,512,128]{2,1,0:T(8,128)(2,1)} %get-tuple-element.37), channel_id=1, source_target_pairs={{0,8},{4,28},{8,16},{12,4},{16,24},{20,12},{24,0},{28,20},{1,9},{5... | collective-permute-start | bytes 1572872 | tf_op jit(solution)/shard_map/ppermute | solution.py:345
  8.0 2.4 %shard_map.104 = (bf16[192,512]{1,0:T(8,128)(2,1)}, bf16[7,128,192]{2,1,0:T(8,128)(2,1)}, f32[7,8,128]{2,1,0:T(8,128)}, f32[8,3584]{1,0:T(8,128)}) custom-call(s32[8,56]{1,0:T(8,128)} %pattern_hbm.1, s32[8]{0:T(128)} %refs_1_.1, s32[8]{0:T(128)} %refs_2_.1, s32[1,14]{1,0:T(1,128)} %refs_3_.1, s32[1,14]{1,0:T(1,128)} %refs_4_.1, bf16[32,512]{1,0:T(8,128)(2,1)} %bitcast.5, ...), custom_call_target="tpu_custom_call" | custom-call | flops 6000000000 | bytes 776112 | tf_op jit(solution)/shard_map/pallas_call | solution.py:363
  10.5 1.0 %copy-done.2 = bf16[7,128,192]{2,1,0:T(8,128)(2,1)S(1)} copy-done((bf16[7,128,192]{2,1,0:T(8,128)(2,1)S(1)}, bf16[7,128,192]{2,1,0:T(8,128)(2,1)}, u32[]{:S(2)}) %copy-start.2) | copy-done | bytes 344088
  11.5 0.9 %copy-done.4 = bf16[192,512]{1,0:T(8,128)(2,1)S(1)} copy-done((bf16[192,512]{1,0:T(8,128)(2,1)S(1)}, bf16[192,512]{1,0:T(8,128)(2,1)}, u32[]{:S(2)}) %copy-start.4) | copy-done | bytes 196632
  12.4 0.9 %copy-done.5 = f32[8,3584]{1,0:T(8,128)S(1)} copy-done((f32[8,3584]{1,0:T(8,128)S(1)}, f32[8,3584]{1,0:T(8,128)}, u32[]{:S(2)}) %copy-start.5) | copy-done | bytes 114712
  13.3 0.7 %copy-done.6 = f32[7,8,128]{2,1,0:T(8,128)S(1)} copy-done((f32[7,8,128]{2,1,0:T(8,128)S(1)}, f32[7,8,128]{2,1,0:T(8,128)}, u32[]{:S(2)}) %copy-start.6) | copy-done | bytes 28696
  14.1 1.2 %shard_map.105 = (bf16[7,512,512]{2,1,0:T(8,128)(2,1)S(1)}, f32[7,512,128]{2,1,0:T(8,128)S(1)}, bf16[192,512]{1,0:T(8,128)(2,1)S(1)}, bf16[7,128,192]{2,1,0:T(8,128)(2,1)S(1)}, f32[7,8,128]{2,1,0:T(8,128)S(1)}) custom-call(bf16[512,3584]{1,0:T(8,128)(2,1)S(1)} %copy-done, f32[8,3584]{1,0:T(8,128)S(1)} %copy-done.5, bf16[192,512]{1,0:T(8,128)(2,1)S(1)} %copy-done.4, ...), custom_call_target="tpu_custom_call" | custom-call | flops 1000000000 | bytes 10428416 | tf_op jit(solution)/shard_map/pallas_call | solution.py:363
  15.3 3.7 %collective-permute-done.refs_0_ = bf16[4,512,128]{2,1,0:T(8,128)(2,1)} collective-permute-done((bf16[4,512,128]{2,1,0:T(8,128)(2,1)}, bf16[4,512,128]{2,1,0:T(8,128)(2,1)}, u32[]{:S(2)}, u32[]{:S(2)}) %collective-permute-start) | collective-permute-done | bytes 524320 | tf_op jit(solution)/shard_map/ppermute | solution.py:333
  18.9 2.2 %collective-permute-start.3 = (bf16[4,512,128]{2,1,0:T(8,128)(2,1)}, bf16[4,512,128]{2,1,0:T(8,128)(2,1)S(1)}, u32[]{:S(2)}, u32[]{:S(2)}) collective-permute-start(bf16[4,512,128]{2,1,0:T(8,128)(2,1)} %collective-permute-done.refs_0_), channel_id=1, source_target_pairs={{0,8},{4,28},{8,16},{12,4},{16,24},{20,12},{24,0},{28,20},{1,9},{5... | collective-permute-start | bytes 1572872 | tf_op jit(solution)/shard_map/ppermute | solution.py:345
  21.1 0.6 collective-permute-done.2.refs_2_
  21.7 2.9 %collective-permute-start.5 = (bf16[4,512,128]{2,1,0:T(8,128)(2,1)}, bf16[4,512,128]{2,1,0:T(8,128)(2,1)S(1)}, u32[]{:S(2)}, u32[]{:S(2)}) collective-permute-start(bf16[4,512,128]{2,1,0:T(8,128)(2,1)} %collective-permute-done.2.refs_2_), channel_id=1, source_target_pairs={{0,4},{4,0},{8,12},{12,8},{16,20},{20,16},{24,28},{28,24},{1,5},{5... | collective-permute-start | bytes 1572872 | tf_op jit(solution)/shard_map/ppermute | solution.py:333
  24.6 0.7 %shard_map.107.before_ref = f32[7,512,128]{2,1,0:T(8,128)S(1)} custom-call(bf16[7,512,512]{2,1,0:T(8,128)(2,1)S(1)} %get-tuple-element.33.squares_ref, f32[7,512,128]{2,1,0:T(8,128)S(1)} %get-tuple-element.34.before_ref, bf16[4,512,128]{2,1,0:T(8,128)(2,1)S(1)} %copy-done.1, bf16[3,512,128]{2,1,0:T(8,128)(2,1)S(1)} %copy-done.3), custom_call_target="tpu_custom_call" | custom-call | bytes 8257536 | tf_op jit(solution)/shard_map/pallas_call | solution.py:363
  25.3 1.9 %collective-permute-done.1.refs_1_ = bf16[3,512,128]{2,1,0:T(8,128)(2,1)S(1)} collective-permute-done((bf16[3,512,128]{2,1,0:T(8,128)(2,1)}, bf16[3,512,128]{2,1,0:T(8,128)(2,1)S(1)}, u32[]{:S(2)}, u32[]{:S(2)}) %collective-permute-start.1) | collective-permute-done | bytes 393248 | tf_op jit(solution)/shard_map/ppermute | solution.py:333
  27.3 2.2 %collective-permute-start.4 = (bf16[2,512,128]{2,1,0:T(8,128)(2,1)S(1)}, bf16[2,512,128]{2,1,0:T(8,128)(2,1)S(1)}, u32[]{:S(2)}, u32[]{:S(2)}) collective-permute-start(bf16[2,512,128]{2,1,0:T(8,128)(2,1)S(1)} %slice.8), channel_id=1, source_target_pairs={{0,8},{4,28},{8,16},{12,4},{16,24},{20,12},{24,0},{28,20},{1,9},{5... | collective-permute-start | bytes 786440 | tf_op jit(solution)/shard_map/ppermute | solution.py:345
  29.5 2.1 %shard_map.108.before_ref = f32[7,512,128]{2,1,0:T(8,128)S(1)} custom-call(bf16[7,512,512]{2,1,0:T(8,128)(2,1)S(1)} %get-tuple-element.33.squares_ref, f32[7,512,128]{2,1,0:T(8,128)S(1)} %shard_map.107.before_ref, bf16[4,512,128]{2,1,0:T(8,128)(2,1)} %collective-permute-done.refs_0_, bf16[3,512,128]{2,1,0:T(8,128)(2,1)S(1)} %collective-permute-done.1.refs_1_, ...), custom_call_target="tpu_custom_call" | custom-call | flops 3000000000 | bytes 8781824 | tf_op jit(solution)/shard_map/pallas_call | solution.py:363
  31.6 4.4 %collective-permute-done.3.refs_0_ = bf16[4,512,128]{2,1,0:T(8,128)(2,1)S(1)} collective-permute-done((bf16[4,512,128]{2,1,0:T(8,128)(2,1)}, bf16[4,512,128]{2,1,0:T(8,128)(2,1)S(1)}, u32[]{:S(2)}, u32[]{:S(2)}) %collective-permute-start.3) | collective-permute-done | bytes 524320 | tf_op jit(solution)/shard_map/ppermute | solution.py:345
  36.1 1.0 %collective-permute-start.6 = (bf16[4,512,128]{2,1,0:T(8,128)(2,1)S(1)}, bf16[4,512,128]{2,1,0:T(8,128)(2,1)S(1)}, u32[]{:S(2)}, u32[]{:S(2)}) collective-permute-start(bf16[4,512,128]{2,1,0:T(8,128)(2,1)S(1)} %collective-permute-done.3.refs_0_), channel_id=1, source_target_pairs={{0,4},{4,0},{8,12},{12,8},{16,20},{20,16},{24,28},{28,24},{1,5},{5... | collective-permute-start | bytes 1572872 | tf_op jit(solution)/shard_map/ppermute | solution.py:333
  37.4 3.5 %collective-permute-done.4.refs_0_ = bf16[2,512,128]{2,1,0:T(8,128)(2,1)S(1)} collective-permute-done((bf16[2,512,128]{2,1,0:T(8,128)(2,1)S(1)}, bf16[2,512,128]{2,1,0:T(8,128)(2,1)S(1)}, u32[]{:S(2)}, u32[]{:S(2)}) %collective-permute-start.4) | collective-permute-done | bytes 262176 | tf_op jit(solution)/shard_map/ppermute | solution.py:345
  40.9 1.8 %collective-permute-start.8 = (bf16[1,512,128]{2,1,0:T(8,128)(2,1)S(1)}, bf16[1,512,128]{2,1,0:T(8,128)(2,1)S(1)}, u32[]{:S(2)}, u32[]{:S(2)}) collective-permute-start(bf16[1,512,128]{2,1,0:T(8,128)(2,1)S(1)} %slice.9), channel_id=1, source_target_pairs={{0,4},{4,0},{8,12},{12,8},{16,20},{20,16},{24,28},{28,24},{1,5},{5... | collective-permute-start | bytes 393224 | tf_op jit(solution)/shard_map/ppermute | solution.py:333
  43.6 0.6 shard_map.110.before_ref
  44.2 6.2 %collective-permute-done.6.x2p_ref = bf16[4,512,128]{2,1,0:T(8,128)(2,1)S(1)} collective-permute-done((bf16[4,512,128]{2,1,0:T(8,128)(2,1)S(1)}, bf16[4,512,128]{2,1,0:T(8,128)(2,1)S(1)}, u32[]{:S(2)}, u32[]{:S(2)}) %collective-permute-start.6) | collective-permute-done | bytes 524320 | tf_op jit(solution)/shard_map/ppermute | solution.py:333
  50.3 1.2 %collective-permute-done.7.z3_ref = bf16[4,512,128]{2,1,0:T(8,128)(2,1)S(1)} collective-permute-done((bf16[4,512,128]{2,1,0:T(8,128)(2,1)S(1)}, bf16[4,512,128]{2,1,0:T(8,128)(2,1)S(1)}, u32[]{:S(2)}, u32[]{:S(2)}) %collective-permute-start.7) | collective-permute-done | bytes 524320 | tf_op jit(solution)/shard_map/ppermute | solution.py:345
  51.5 1.2 %shard_map.111 = (bf16[512,640]{1,0:T(8,128)(2,1)S(1)}, f32[512,192]{1,0:T(8,128)S(1)}, f32[2,512,128]{2,1,0:T(8,128)S(1)}) custom-call(f32[7,8,128]{2,1,0:T(8,128)S(1)} %get-tuple-element.32.mask_ref, bf16[7,512,512]{2,1,0:T(8,128)(2,1)S(1)} %get-tuple-element.33.squares_ref, f32[7,512,128]{2,1,0:T(8,128)S(1)} %shard_map.110.before_ref, ...), custom_call_target="tpu_custom_call" | custom-call | bytes 8499200 | tf_op jit(solution)/shard_map/pallas_call | solution.py:363
  52.9 0.8 %shard_map.112 = (bf16[512,256]{1,0:T(8,128)(2,1)S(1)}, f32[128,192]{1,0:T(8,128)S(1)}, bf16[32,192]{1,0:T(8,128)(2,1)S(1)}, bf16[32,192]{1,0:T(8,128)(2,1)S(1)}) custom-call(f32[7,8,128]{2,1,0:T(8,128)S(1)} %get-tuple-element.32.mask_ref, bf16[7,512,512]{2,1,0:T(8,128)(2,1)S(1)} %get-tuple-element.33.squares_ref, ...), custom_call_target="tpu_custom_call" | custom-call | bytes 5804032 | tf_op jit(solution)/shard_map/pallas_call | solution.py:363
  53.7 0.8 %collective-permute-start.10 = (bf16[32,192]{1,0:T(8,128)(2,1)S(1)}, bf16[32,192]{1,0:T(8,128)(2,1)S(1)}, u32[]{:S(2)}, u32[]{:S(2)}) collective-permute-start(bf16[32,192]{1,0:T(8,128)(2,1)S(1)} %get-tuple-element.49), channel_id=1, source_target_pairs={{0,4},{4,0},{8,12},{12,8},{16,20},{20,16},{24,28},{28,24},{1,5},{5... | collective-permute-start | bytes 36872 | tf_op jit(solution)/shard_map/ppermute | solution.py:333
  54.5 3.8 %collective-permute-start.11 = (bf16[32,192]{1,0:T(8,128)(2,1)S(1)}, bf16[32,192]{1,0:T(8,128)(2,1)S(1)}, u32[]{:S(2)}, u32[]{:S(2)}) collective-permute-start(bf16[32,192]{1,0:T(8,128)(2,1)S(1)} %get-tuple-element.50), channel_id=1, source_target_pairs={{0,28},{4,8},{8,4},{12,16},{16,12},{20,24},{24,20},{28,0},{1,29},{... | collective-permute-start | bytes 36872 | tf_op jit(solution)/shard_map/ppermute | solution.py:339
  58.3 2.6 %collective-permute-done.11.got_b_ref = bf16[32,192]{1,0:T(8,128)(2,1)S(1)} collective-permute-done((bf16[32,192]{1,0:T(8,128)(2,1)S(1)}, bf16[32,192]{1,0:T(8,128)(2,1)S(1)}, u32[]{:S(2)}, u32[]{:S(2)}) %collective-permute-start.11) | collective-permute-done | bytes 12320 | tf_op jit(solution)/shard_map/ppermute | solution.py:339
  61.2 1.6 %collective-permute-start.13 = (bf16[32,128]{1,0:T(8,128)(2,1)S(1)}, bf16[32,128]{1,0:T(8,128)(2,1)S(1)}, u32[]{:S(2)}, u32[]{:S(2)}) collective-permute-start(bf16[32,128]{1,0:T(8,128)(2,1)S(1)} %get-tuple-element.53), channel_id=1, source_target_pairs={{0,3},{1,2},{2,1},{3,0},{4,7},{5,6},{6,5},{7,4},{8,11},{9,10},{10,... | collective-permute-start | bytes 24584 | tf_op jit(solution)/shard_map/ppermute | solution.py:339
  62.8 1.1 %shard_map.113 = bf16[512,896]{1,0:T(8,128)(2,1)} custom-call(bf16[512,640]{1,0:T(8,128)(2,1)S(1)} %get-tuple-element.41.inner_ref, bf16[512,256]{1,0:T(8,128)(2,1)S(1)} %get-tuple-element.47.edges_ref), custom_call_target="tpu_custom_call" | custom-call | bytes 1835008 | tf_op jit(solution)/shard_map/pallas_call | solution.py:363
  64.3 0.7 %shard_map.115 = f32[128,128]{1,0:T(8,128)} custom-call(f32[128,128]{1,0:T(8,128)S(1)} %get-tuple-element.51.center_ref, bf16[32,128]{1,0:T(8,128)(2,1)S(1)} %collective-permute-done.12.got_a_ref, bf16[32,128]{1,0:T(8,128)(2,1)S(1)} %collective-permute-done.13.got_b_ref), custom_call_target="tpu_custom_call" | custom-call | bytes 147456 | tf_op jit(solution)/shard_map/pallas_call | solution.py:363
  (26 shorter events, 2.2 us)
Async XLA Ops:
  2.9 16.0 %collective-permute-start = (bf16[4,512,128]{2,1,0:T(8,128)(2,1)}, bf16[4,512,128]{2,1,0:T(8,128)(2,1)}, u32[]{:S(2)}, u32[]{:S(2)}) collective-permute-start(bf16[4,512,128]{2,1,0:T(8,128)(2,1)} %get-tuple-element.35.x1a_ref), channel_id=1, source_target_pairs={{0,4},{4,0},{8,12},{12,8},{16,20},{20,16},{24,28},{28,24},{1,5},{5... | collective-permute-start | bytes 1572872 | tf_op jit(solution)/shard_map/ppermute | solution.py:333
  5.9 21.4 %collective-permute-start.1 = (bf16[3,512,128]{2,1,0:T(8,128)(2,1)}, bf16[3,512,128]{2,1,0:T(8,128)(2,1)S(1)}, u32[]{:S(2)}, u32[]{:S(2)}) collective-permute-start(bf16[3,512,128]{2,1,0:T(8,128)(2,1)} %get-tuple-element.36.x1b_ref), channel_id=1, source_target_pairs={{0,4},{4,0},{8,12},{12,8},{16,20},{20,16},{24,28},{28,24},{1,5},{5... | collective-permute-start | bytes 1179656 | tf_op jit(solution)/shard_map/ppermute | solution.py:333
  6.0 15.8 %collective-permute-start.2 = (bf16[4,512,128]{2,1,0:T(8,128)(2,1)}, bf16[4,512,128]{2,1,0:T(8,128)(2,1)}, u32[]{:S(2)}, u32[]{:S(2)}) collective-permute-start(bf16[4,512,128]{2,1,0:T(8,128)(2,1)} %get-tuple-element.37), channel_id=1, source_target_pairs={{0,8},{4,28},{8,16},{12,4},{16,24},{20,12},{24,0},{28,20},{1,9},{5... | collective-permute-start | bytes 1572872 | tf_op jit(solution)/shard_map/ppermute | solution.py:345
  8.0 2.4 %copy-start = (bf16[512,3584]{1,0:T(8,128)(2,1)S(1)}, bf16[512,3584]{1,0:T(8,128)(2,1)}, u32[]{:S(2)}) copy-start(bf16[512,3584]{1,0:T(8,128)(2,1)} %p2_ref.1) | copy-start | bytes 11010052
  10.5 1.0 %copy-start.2 = (bf16[7,128,192]{2,1,0:T(8,128)(2,1)S(1)}, bf16[7,128,192]{2,1,0:T(8,128)(2,1)}, u32[]{:S(2)}) copy-start(bf16[7,128,192]{2,1,0:T(8,128)(2,1)} %get-tuple-element.30.refs_1_) | copy-start | bytes 1032196
  11.5 0.9 %copy-start.4 = (bf16[192,512]{1,0:T(8,128)(2,1)S(1)}, bf16[192,512]{1,0:T(8,128)(2,1)}, u32[]{:S(2)}) copy-start(bf16[192,512]{1,0:T(8,128)(2,1)} %get-tuple-element.29.refs_0_) | copy-start | bytes 589828
  12.4 0.9 %copy-start.5 = (f32[8,3584]{1,0:T(8,128)S(1)}, f32[8,3584]{1,0:T(8,128)}, u32[]{:S(2)}) copy-start(f32[8,3584]{1,0:T(8,128)} %get-tuple-element.28.wide_ref) | copy-start | bytes 344068
  13.3 0.7 %copy-start.6 = (f32[7,8,128]{2,1,0:T(8,128)S(1)}, f32[7,8,128]{2,1,0:T(8,128)}, u32[]{:S(2)}) copy-start(f32[7,8,128]{2,1,0:T(8,128)} %get-tuple-element.31.refs_2_) | copy-start | bytes 86020
  14.1 10.5 %copy-start.1 = (bf16[4,512,128]{2,1,0:T(8,128)(2,1)S(1)}, bf16[4,512,128]{2,1,0:T(8,128)(2,1)}, u32[]{:S(2)}) copy-start(bf16[4,512,128]{2,1,0:T(8,128)(2,1)} %get-tuple-element.35.x1a_ref) | copy-start | bytes 1572868
  14.1 10.5 %copy-start.3 = (bf16[3,512,128]{2,1,0:T(8,128)(2,1)S(1)}, bf16[3,512,128]{2,1,0:T(8,128)(2,1)}, u32[]{:S(2)}) copy-start(bf16[3,512,128]{2,1,0:T(8,128)(2,1)} %get-tuple-element.36.x1b_ref) | copy-start | bytes 1179652
  18.9 17.1 %collective-permute-start.3 = (bf16[4,512,128]{2,1,0:T(8,128)(2,1)}, bf16[4,512,128]{2,1,0:T(8,128)(2,1)S(1)}, u32[]{:S(2)}, u32[]{:S(2)}) collective-permute-start(bf16[4,512,128]{2,1,0:T(8,128)(2,1)} %collective-permute-done.refs_0_), channel_id=1, source_target_pairs={{0,8},{4,28},{8,16},{12,4},{16,24},{20,12},{24,0},{28,20},{1,9},{5... | collective-permute-start | bytes 1572872 | tf_op jit(solution)/shard_map/ppermute | solution.py:345
  21.7 21.8 %collective-permute-start.5 = (bf16[4,512,128]{2,1,0:T(8,128)(2,1)}, bf16[4,512,128]{2,1,0:T(8,128)(2,1)S(1)}, u32[]{:S(2)}, u32[]{:S(2)}) collective-permute-start(bf16[4,512,128]{2,1,0:T(8,128)(2,1)} %collective-permute-done.2.refs_2_), channel_id=1, source_target_pairs={{0,4},{4,0},{8,12},{12,8},{16,20},{20,16},{24,28},{28,24},{1,5},{5... | collective-permute-start | bytes 1572872 | tf_op jit(solution)/shard_map/ppermute | solution.py:333
  27.3 15.4 %copy-start.7 = (bf16[1,512,128]{2,1,0:T(8,128)(2,1)S(1)}, bf16[1,512,128]{2,1,0:T(8,128)(2,1)}, u32[]{:S(2)}) copy-start(bf16[1,512,128]{2,1,0:T(8,128)(2,1)} %get-tuple-element.44) | copy-start | bytes 393220
  27.3 13.6 %collective-permute-start.4 = (bf16[2,512,128]{2,1,0:T(8,128)(2,1)S(1)}, bf16[2,512,128]{2,1,0:T(8,128)(2,1)S(1)}, u32[]{:S(2)}, u32[]{:S(2)}) collective-permute-start(bf16[2,512,128]{2,1,0:T(8,128)(2,1)S(1)} %slice.8), channel_id=1, source_target_pairs={{0,8},{4,28},{8,16},{12,4},{16,24},{20,12},{24,0},{28,20},{1,9},{5... | collective-permute-start | bytes 786440 | tf_op jit(solution)/shard_map/ppermute | solution.py:345
  36.1 14.2 %collective-permute-start.6 = (bf16[4,512,128]{2,1,0:T(8,128)(2,1)S(1)}, bf16[4,512,128]{2,1,0:T(8,128)(2,1)S(1)}, u32[]{:S(2)}, u32[]{:S(2)}) collective-permute-start(bf16[4,512,128]{2,1,0:T(8,128)(2,1)S(1)} %collective-permute-done.3.refs_0_), channel_id=1, source_target_pairs={{0,4},{4,0},{8,12},{12,8},{16,20},{20,16},{24,28},{28,24},{1,5},{5... | collective-permute-start | bytes 1572872 | tf_op jit(solution)/shard_map/ppermute | solution.py:333
  37.1 14.5 %collective-permute-start.7 = (bf16[4,512,128]{2,1,0:T(8,128)(2,1)S(1)}, bf16[4,512,128]{2,1,0:T(8,128)(2,1)S(1)}, u32[]{:S(2)}, u32[]{:S(2)}) collective-permute-start(bf16[4,512,128]{2,1,0:T(8,128)(2,1)S(1)} %collective-permute-done.3.refs_0_), channel_id=1, source_target_pairs={{0,8},{4,28},{8,16},{12,4},{16,24},{20,12},{24,0},{28,20},{1,9},{5... | collective-permute-start | bytes 1572872 | tf_op jit(solution)/shard_map/ppermute | solution.py:345
  40.9 11.9 %collective-permute-start.8 = (bf16[1,512,128]{2,1,0:T(8,128)(2,1)S(1)}, bf16[1,512,128]{2,1,0:T(8,128)(2,1)S(1)}, u32[]{:S(2)}, u32[]{:S(2)}) collective-permute-start(bf16[1,512,128]{2,1,0:T(8,128)(2,1)S(1)} %slice.9), channel_id=1, source_target_pairs={{0,4},{4,0},{8,12},{12,8},{16,20},{20,16},{24,28},{28,24},{1,5},{5... | collective-permute-start | bytes 393224 | tf_op jit(solution)/shard_map/ppermute | solution.py:333
  42.7 10.3 %collective-permute-start.9 = (bf16[1,512,128]{2,1,0:T(8,128)(2,1)S(1)}, bf16[1,512,128]{2,1,0:T(8,128)(2,1)S(1)}, u32[]{:S(2)}, u32[]{:S(2)}) collective-permute-start(bf16[1,512,128]{2,1,0:T(8,128)(2,1)S(1)} %copy-done.7), channel_id=1, source_target_pairs={{0,8},{4,28},{8,16},{12,4},{16,24},{20,12},{24,0},{28,20},{1,9},{5... | collective-permute-start | bytes 393224 | tf_op jit(solution)/shard_map/ppermute | solution.py:345
  53.7 4.6 %collective-permute-start.10 = (bf16[32,192]{1,0:T(8,128)(2,1)S(1)}, bf16[32,192]{1,0:T(8,128)(2,1)S(1)}, u32[]{:S(2)}, u32[]{:S(2)}) collective-permute-start(bf16[32,192]{1,0:T(8,128)(2,1)S(1)} %get-tuple-element.49), channel_id=1, source_target_pairs={{0,4},{4,0},{8,12},{12,8},{16,20},{20,16},{24,28},{28,24},{1,5},{5... | collective-permute-start | bytes 36872 | tf_op jit(solution)/shard_map/ppermute | solution.py:333
  54.5 6.4 %collective-permute-start.11 = (bf16[32,192]{1,0:T(8,128)(2,1)S(1)}, bf16[32,192]{1,0:T(8,128)(2,1)S(1)}, u32[]{:S(2)}, u32[]{:S(2)}) collective-permute-start(bf16[32,192]{1,0:T(8,128)(2,1)S(1)} %get-tuple-element.50), channel_id=1, source_target_pairs={{0,28},{4,8},{8,4},{12,16},{16,12},{20,24},{24,20},{28,0},{1,29},{... | collective-permute-start | bytes 36872 | tf_op jit(solution)/shard_map/ppermute | solution.py:339
  61.1 2.8 %collective-permute-start.12 = (bf16[32,128]{1,0:T(8,128)(2,1)S(1)}, bf16[32,128]{1,0:T(8,128)(2,1)S(1)}, u32[]{:S(2)}, u32[]{:S(2)}) collective-permute-start(bf16[32,128]{1,0:T(8,128)(2,1)S(1)} %get-tuple-element.52), channel_id=1, source_target_pairs={{0,1},{1,0},{2,3},{3,2},{4,5},{5,4},{6,7},{7,6},{8,9},{9,8},{10,11... | collective-permute-start | bytes 24584 | tf_op jit(solution)/shard_map/ppermute | solution.py:333
  61.2 3.1 %collective-permute-start.13 = (bf16[32,128]{1,0:T(8,128)(2,1)S(1)}, bf16[32,128]{1,0:T(8,128)(2,1)S(1)}, u32[]{:S(2)}, u32[]{:S(2)}) collective-permute-start(bf16[32,128]{1,0:T(8,128)(2,1)S(1)} %get-tuple-element.53), channel_id=1, source_target_pairs={{0,3},{1,2},{2,1},{3,0},{4,7},{5,6},{6,5},{7,4},{8,11},{9,10},{10,... | collective-permute-start | bytes 24584 | tf_op jit(solution)/shard_map/ppermute | solution.py:339
